TPU v7x, 256 devices: a whole 4x4x8 slice. The times are simulated.
256 devices in a mesh: row: 16 (over y, z_lo), col: 16 (over x, z_hi, core).
Axes of the slice: x: 4, y: 4, z: 8 (z_hi: 2, z_lo: 4; z = z_hi * 4 + z_lo), core: 2. Of those that a mesh axis runs over, the one named last changes fastest.
Arguments:
- a_vals: bfloat16 [320, 80, 4096], P('row', 'col'), may hold values from -0.3125 to 0.3125
- a_cols: int32 [320, 80], P('row', 'col'), may hold values from 0 to 319, as said below
- a_count: int32 [320, 16], P('row', 'col'), may hold values from 3 to 5, as said below
- p_vals: bfloat16 [320, 64, 2048], P('row', None, 'col'), may hold values from -0.6015625 to 0.6015625
- p_mask: int32 [320, 16], P('row', 'col'), may hold values 0 or 1
Outputs:
- coarse: float32 [2048, 2048], P('row', 'col')
Inputs may be any that keep to these rules, and one draw needn't show every extreme that they name: a_cols[i, j] lies in column range j // 5, that is from (j // 5) * 20 to (j // 5) * 20 + 19; entries of slots that are not live are ignored. `a_count`: in the column range that holds the row's own index (range i // 20) the count is 4 to 5 and 5 is reached; in every other range it is 3 to 4 and 4 is reached.
All inputs are finite; a program needn't handle non-finite values. No bound on the sum of `p_mask` on one device may be relied on, other than what follows from the above.
Results may differ from a plain program's by a relative error of at most 0.0029.
Values may be sent and summed in bfloat16 or wider, within the bound.
No kernel may reach another device: no remote copies, remote signals or barrier semaphores. Data moves between devices by JAX's collectives and lax.ppermute only.
A program may use at most 128 MiB of HBM per device.

v0:
```python
import jax
import jax.numpy as jnp
from jax import lax
from jax.sharding import PartitionSpec as P

BR = 64


def apply_blocks(total, values, offsets, ranges, fine_rows, panel):
    count = values.shape[1]
    rows = ranges[None, :] * fine_rows + offsets.astype(jnp.int32)
    picked = panel[rows]
    blocks = values.reshape(values.shape[0], count, BR, BR)
    return total + jnp.einsum("itab,itbc->iac", blocks, picked, preferred_element_type=jnp.float32)


def fold_slots(total, piece, per, fine_rows, panel):
    values, offsets = piece
    count = values.shape[1]

    def one_group(step, acc):
        first = step * per
        part_values = lax.dynamic_slice_in_dim(values, first, per, 1)
        part_offsets = lax.dynamic_slice_in_dim(offsets, first, per, 1)
        ranges = (first + jnp.arange(per, dtype=jnp.int32)) // per
        return apply_blocks(acc, part_values, part_offsets, ranges, fine_rows, panel)

    return lax.fori_loop(0, count // per, one_group, total)


def per_device(a_vals, a_cols, a_count, p_vals, p_mask):
    fine_rows = a_vals.shape[0]
    per = a_cols.shape[1]
    live = jnp.arange(per, dtype=jnp.int32)[None, :] < a_count
    masked = jnp.where(live[:, :, None], a_vals, jnp.zeros_like(a_vals))
    offsets = (a_cols - lax.axis_index("col") * fine_rows).astype(jnp.bfloat16)
    p_live = p_vals * p_mask[:, :, None].astype(jnp.bfloat16)
    panel = lax.all_gather(p_live, "row", axis=0, tiled=True)
    empty = jnp.zeros((fine_rows, BR, p_vals.shape[2]), jnp.float32)
    product = fold_slots(
        empty,
        (
            lax.all_gather(masked, "col", axis=1, tiled=True),
            lax.all_gather(offsets, "col", axis=1, tiled=True),
        ),
        per,
        fine_rows,
        panel,
    )
    prolonged = product.astype(jnp.bfloat16)
    partial_sums = jnp.einsum(
        "iak,iac->kc",
        lax.all_gather(p_live, "col", axis=2, tiled=True),
        prolonged,
        preferred_element_type=jnp.float32,
    )
    return lax.psum_scatter(partial_sums, "row", scatter_dimension=0, tiled=True)


def solution(mesh):
    placed = (
        P("row", "col", None),
        P("row", "col"),
        P("row", "col"),
        P("row", None, "col"),
        P("row", "col"),
    )
    return jax.shard_map(
        per_device, mesh=mesh, in_specs=placed, out_specs=P("row", "col"), check_vma=False
    )
```

profile of v0, /device:TPU:4, one launch (start us, length us, event | category | flops | bytes accessed | tf_op | source)
XLA Modules:
  0.0 574.5 jit_solution(13323063262520043301)
XLA Ops:
  11.7 29.1 %all-gather = bf16[16,5,20]{2,1,0:T(8,128)(2,1)S(1)} all-gather(bf16[1,5,20]{2,1,0:T(8,128)(2,1)S(1)} %fusion.10), channel_id=1, replica_groups=mesh['row'=16,'col'=16] {'col'}, dimensions={0}, use_global_device_ids=true | all-gather | bytes 3400 | tf_op jit(solution)/shard_map/all_gather | solution.py:44
  40.9 94.6 %all-gather.9.cloned.1.call-done = bf16[320,64,128]{2,1,0:T(8,128)(2,1)} async-done(((bf16[20,64,128]{2,1,0:T(8,128)(2,1)}), bf16[320,64,128]{2,1,0:T(8,128)(2,1)}) %all-gather.9.cloned.1.call-update) | async-done | bytes 5242896 | tf_op jit(solution)/shard_map/all_gather | solution.py:38
  135.4 164.9 %all-gather.7.cloned.1.call-done = bf16[20,80,4096]{2,0,1:T(8,128)(2,1)} async-done(((bf16[20,5,4096]{2,0,1:T(8,128)(2,1)}), bf16[20,80,4096]{2,0,1:T(8,128)(2,1)}) %all-gather.7.cloned.1.call-update) | async-done | bytes 13107216 | tf_op jit(solution)/shard_map/all_gather | solution.py:43
  300.3 179.3 %while.16 = (s32[]{:T(128)}, f32[20,64,128]{2,1,0:T(8,128)}, bf16[20,80,4096]{2,0,1:T(8,128)(2,1)}, bf16[20,80]{0,1:T(8,128)(2,1)S(1)}, bf16[320,64,128]{2,1,0:T...) while((s32[]{:T(128)}, f32[20,64,128]{2,1,0:T(8,128)}, ...), condition=%wide.region_1.2_spmd.clone, body=%wide.region_0.1_spmd.clone.sunk | while | flops 105186864 | bytes 10329217 | solution.py:28
  300.5 3.3 gather_fusion
  306.1 2.9 reshape.79
  310.7 3.6 gather_fusion
  316.5 2.9 reshape.79
  319.5 2.5 fusion.20
  322.2 3.3 gather_fusion
  327.8 2.9 reshape.79
  330.7 2.5 fusion.20
  333.5 3.3 gather_fusion
  339.1 2.9 reshape.79
  344.8 3.3 gather_fusion
  350.3 2.9 reshape.79
  356.0 3.3 gather_fusion
  361.6 2.9 reshape.79
  364.5 2.5 fusion.20
  367.3 3.3 gather_fusion
  372.9 2.9 reshape.79
  375.8 2.5 fusion.20
  378.5 3.4 gather_fusion
  384.1 2.9 reshape.79
  387.1 2.5 fusion.20
  389.8 3.3 gather_fusion
  395.4 2.9 reshape.79
  401.1 3.3 gather_fusion
  406.6 2.9 reshape.79
  412.3 3.3 gather_fusion
  417.9 2.9 reshape.79
  420.8 2.5 fusion.20
  423.6 3.3 gather_fusion
  429.2 2.9 reshape.79
  432.1 2.5 fusion.20
  434.8 3.3 gather_fusion
  440.4 2.9 reshape.79
  443.4 2.5 fusion.20
  446.1 3.3 gather_fusion
  451.7 2.9 reshape.79
  457.3 3.3 gather_fusion
  462.9 2.9 reshape.79
  465.9 2.5 fusion.20
  468.6 3.3 gather_fusion
  474.2 2.9 reshape.79
  477.1 2.5 fusion.20
  479.6 5.2 convolution_bitcast_fusion
  484.8 83.2 %reduce-scatter.2.cloned.1.call-done = f32[128,128]{1,0:T(8,128)} async-done(((f32[2048,128]{1,0:T(8,128)}), f32[128,128]{1,0:T(8,128)}) %reduce-scatter.2.cloned.1.call-update) | async-done | bytes 65552 | tf_op jit(solution)/shard_map/reduce_scatter | solution.py:57
  (138 shorter events, 58.4 us)
Async XLA Ops:
  6.5 3.3 copy-start
  6.5 128.9 %all-gather.9.cloned.1.call-start = ((), (), s32[]{:S(2)}) async-start(), calls=%async_computation.3 | async-start | bytes 5570560 | tf_op jit(solution)/shard_map/all_gather | solution.py:38
  9.1 291.2 %all-gather.7.cloned.1.call-start = ((), (), s32[]{:S(2)}) async-start(), calls=%async_computation.2 | async-start | bytes 16711680 | tf_op jit(solution)/shard_map/all_gather | solution.py:43
  9.8 1.9 copy-start.1
  10.9 468.7 %all-gather.5.cloned.1.call-start = ((), (), s32[]{:S(2)}) async-start(), calls=%async_computation.1 | async-start | bytes 5570560 | tf_op jit(solution)/shard_map/all_gather | solution.py:53
  11.7 556.4 %reduce-scatter.2.cloned.1.call-start = ((), (), s32[]{:S(2)}) async-start(), calls=%async_computation.4 | async-start | bytes 1114112 | tf_op jit(solution)/shard_map/reduce_scatter | solution.py:57
Sparse Core Ops, SparseCore 0:
  9.2 126.1 all-gather.8
  138.1 162.1 all-gather.6
  302.8 80.9 all-gather.4
  485.0 83.0 reduce-scatter.1
where the time goes:
time: 577 us; the launch traced here: 575 us
  waiting for transfers between devices  343 us (59%)
  local copies, waits for them, and re-layouts  140 us (24%)
  matrix products  43.7 us (8%)
  blocking collectives  29.1 us (5%)
  between operations  13.2 us (2%)
    all_gather x1, waiting for transfers between devices, per_device(): lax.all_gather(masked, 'col', axis=1, tiled=True)  165 us
    all_gather x1, waiting for transfers between devices, per_device(): panel = lax.all_gather(p_live, 'row', axis=0, tiled=True)  94.6 us
    reduce_scatter x1, waiting for transfers between devices, per_device(): lax.psum_scatter(partial_sums, 'row', scatter_dimension=0, tiled=True)  83.2 us
    gather x16, local copies, waits for them, and re-layouts, apply_blocks(): picked = panel[rows]  53.8 us
    reshape x16, local copies, waits for them, and re-layouts, apply_blocks(): blocks = values.reshape(values.shape[0], count, BR, BR)  46.8 us
    dot_general x16, matrix products, apply_blocks(): jnp.einsum('itab,itbc->iac', blocks, picked, preferred_element_type=jnp.f...  38.5 us
    dynamic_slice x16, local copies, waits for them, and re-layouts, one_group(): part_values = lax.dynamic_slice_in_dim(values, first, per, 1)  35.7 us
    all_gather x1, blocking collectives, per_device(): lax.all_gather(offsets, 'col', axis=1, tiled=True)  29.1 us
  transfers between devices with their start and end apart: 4, of which 3 were waited for; matrix products, arithmetic and copies ran while one was open for 31% of the time, Pallas kernels for 0%

commit v1 on v0

v1 whole, which is shorter than its diff:
```python
import jax
import jax.numpy as jnp
from jax import lax
from jax.experimental import pallas as pl
from jax.experimental.pallas import tpu as pltpu
from jax.sharding import PartitionSpec as P

BR = 64
AXES = ("row", "col")


def flat(y, z, x, h, c):
    return ((y * 4 + z) * 4 + x) * 4 + h * 2 + c


PLACES = [
    (y, z, x, h, c)
    for y in range(4)
    for z in range(4)
    for x in range(4)
    for h in range(2)
    for c in range(2)
]


def move(array, target):
    pairs = []
    for place in PLACES:
        to = target(*place)
        if to is not None:
            pairs.append((flat(*place), flat(*to)))
    return lax.ppermute(array, AXES, pairs)


def shift_y(k):
    return lambda y, z, x, h, c: ((y + k) % 4, z, x, h, c)


def shift_x(k):
    return lambda y, z, x, h, c: (y, z, (x + k) % 4, h, c)


def shift_z(k):
    return lambda y, z, x, h, c: (y, (z + k) % 4, x, h, c)


def flip_h(y, z, x, h, c):
    return (y, z, x, 1 - h, c)


def flip_c(y, z, x, h, c):
    return (y, z, x, h, 1 - c)


def swap_zc(y, z, x, h, c):
    return (y, (z // 2) * 2 + c, x, h, z % 2)


def ring(array, shift):
    half = array.shape[0] // 2
    before = move(array, shift(1))
    after = move(array, shift(3))
    first = move(before[:half], shift(1))
    second = move(after[half:], shift(3))
    return [array, before, after, first, second]


def apply_kernel(idx, place, *refs):
    p_refs = refs[:20]
    a_refs = refs[20:30]
    a5_ref = refs[30]
    mine, other = refs[31:33]
    panel, left, sems = refs[33:]
    y, z, x, h, c = (place[i] for i in range(5))
    copies = []

    def start(src, dst):
        copy = pltpu.make_async_copy(src, dst, sems.at[len(copies)])
        copy.start()
        copies.append(copy)

    for f in range(2):
        for k, (ref, rows, at) in enumerate(
            zip(a_refs[5 * f : 5 * f + 5], (1280, 1280, 1280, 640, 640), (0, 0, 0, 0, 640))
        ):
            slot = (0, 1, 3, 2, 2)[k] * 2 + f
            start(ref, left.at[slot, pl.ds(at, rows)])
    for d in range(4):
        source = lax.rem(z + 4 - d, 4)
        j1, l0 = source // 2, lax.rem(source, 2)
        side = lax.rem(l0 + c, 2)
        for k, (ref, rows, at) in enumerate(
            zip(p_refs[5 * d : 5 * d + 5], (1280, 1280, 1280, 640, 640), (0, 0, 0, 0, 640))
        ):
            jx = lax.rem(y + 4 - (0, 1, 3, 2, 2)[k], 4)
            start(ref, panel.at[side, pl.ds(pl.multiple_of((jx * 2 + j1) * 1280 + at, 640), rows)])
    for copy in copies:
        copy.wait()

    own = lax.rem(x + 4 - y, 4) * 2 + lax.rem(h + z // 2, 2)

    def block(off):
        rows = pl.ds(pl.multiple_of(off, BR), BR)
        return jnp.concatenate([panel[0, rows, :], panel[1, rows, :]], axis=1)

    @pl.loop(0, 20)
    def _(t):
        rows = pl.ds(pl.multiple_of(t * BR, BR), BR)
        total = jnp.dot(
            a5_ref[rows, :], block(idx[(own * 20 + t) * 5 + 4]), preferred_element_type=jnp.float32
        )
        for slot in range(8):
            at = (slot * 20 + t) * 5
            right = jnp.concatenate([block(idx[at + s]) for s in range(4)], axis=0)
            total += jnp.dot(left[slot, rows, :], right, preferred_element_type=jnp.float32)
        mine[rows, :] = total[:, :128]
        other[rows, :] = total[:, 128:]


def apply_panel(idx, place, p_pieces, a_pieces, a5):
    anywhere = pl.BlockSpec(memory_space=pl.ANY)
    inside = pl.BlockSpec(memory_space=pltpu.VMEM)
    out = jax.ShapeDtypeStruct((1280, 128), jnp.float32)
    return pl.pallas_call(
        apply_kernel,
        out_shape=(out, out),
        grid_spec=pltpu.PrefetchScalarGridSpec(
            num_scalar_prefetch=2,
            grid=(),
            in_specs=[anywhere] * 30 + [inside],
            out_specs=(inside, inside),
            scratch_shapes=[
                pltpu.VMEM((2, 8 * 1280, 128), jnp.bfloat16),
                pltpu.VMEM((8, 1280, 256), jnp.bfloat16),
                pltpu.SemaphoreType.DMA((30,)),
            ],
        ),
        compiler_params=pltpu.CompilerParams(vmem_limit_bytes=40 * 2**20),
        cost_estimate=pl.CostEstimate(
            flops=2 * 1280 * 2048 * 256, bytes_accessed=12 * 2**20, transcendentals=0
        ),
        name="apply_panel",
    )(idx, place, *p_pieces, *a_pieces, a5)


def project_kernel(place, *refs):
    t_refs = refs[:10]
    prol = refs[10]
    outs = refs[11:15]
    left, sems = refs[15:]
    y, z, x, h, c = (place[i] for i in range(5))
    copies = []
    for f in range(2):
        k1 = lax.rem(h + f, 2)
        for k, (rows, at) in enumerate(((128, 0), (128, 0), (128, 0), (64, 0), (64, 64))):
            m = lax.rem(x + 8 - (0, 1, 3, 2, 2)[k] - y, 4)
            copy = pltpu.make_async_copy(
                t_refs[5 * f + k], left.at[m, k1, pl.ds(at, rows)], sems.at[len(copies)]
            )
            copy.start()
            copies.append(copy)
    for copy in copies:
        copy.wait()
    for m in range(4):
        got = jnp.dot(
            left[m].reshape(256, 1280), prol[...], preferred_element_type=jnp.float32
        )
        outs[m][...] = got


def project(place, t_pieces, prol):
    anywhere = pl.BlockSpec(memory_space=pl.ANY)
    inside = pl.BlockSpec(memory_space=pltpu.VMEM)
    out = jax.ShapeDtypeStruct((256, 256), jnp.float32)
    return pl.pallas_call(
        project_kernel,
        out_shape=(out,) * 4,
        grid_spec=pltpu.PrefetchScalarGridSpec(
            num_scalar_prefetch=1,
            grid=(),
            in_specs=[anywhere] * 10 + [inside],
            out_specs=(inside,) * 4,
            scratch_shapes=[
                pltpu.VMEM((4, 2, 128, 1280), jnp.bfloat16),
                pltpu.SemaphoreType.DMA((10,)),
            ],
        ),
        compiler_params=pltpu.CompilerParams(vmem_limit_bytes=32 * 2**20),
        cost_estimate=pl.CostEstimate(
            flops=2 * 1280 * 1024 * 256, bytes_accessed=4 * 2**20, transcendentals=0
        ),
        name="project",
    )(place, *t_pieces, prol)


def per_device(a_vals, a_cols, a_count, p_vals, p_mask):
    row, col = lax.axis_index("row"), lax.axis_index("col")
    y, z = row // 4, row % 4
    x, h, c = col // 4, (col // 2) % 2, col % 2
    place = jnp.stack([y, z, x, h, c]).astype(jnp.int32)

    p_live = p_vals * p_mask[:, :, None].astype(jnp.bfloat16)
    p_flat = p_live.reshape(1280, 128)
    p_own = move(p_flat, swap_zc)
    p_pieces = []
    for d in range(4):
        piece = p_own if d == 0 else move(p_own, shift_z(d))
        p_pieces += ring(piece, shift_y)

    live = jnp.arange(5, dtype=jnp.int32)[None, :] < a_count
    masked = jnp.where(live[:, :, None], a_vals, jnp.zeros_like(a_vals))
    slots = masked.reshape(20, 5, BR, BR)
    four = slots[:, :4].transpose(0, 2, 1, 3).reshape(1280, 256)
    five = slots[:, 4].reshape(1280, BR)
    a_pieces = ring(four, shift_x) + ring(move(four, flip_h), shift_x)

    def from_own(step):
        def target(y, z, x, h, c):
            if x != y or c != z % 2:
                return None
            return step(y, z, x, h, c)

        return target

    def across(y, z, x, h, c):
        return (y, z, x, 1 - h, c) if h == z // 2 else None

    five = five + move(five, from_own(across))
    five = five + sum(move(five, from_own(shift_x(k))) for k in (1, 2, 3))

    offsets = jnp.clip(a_cols - col * 20, 0, 19)
    both = jnp.stack([offsets, move(offsets, flip_h)])
    spread = jnp.stack([both] + [move(both, shift_x(k)) for k in (1, 2, 3)])
    k4 = jnp.arange(4, dtype=jnp.int32)[:, None]
    f2 = jnp.arange(2, dtype=jnp.int32)[None, :]
    ranges = ((x - k4) % 4) * 2 + (h + f2) % 2
    idx = ((ranges[:, :, None, None] * 20 + spread) * BR).reshape(800)

    mine, other = apply_panel(idx, place, p_pieces, a_pieces, five)
    near = mine + move(other, flip_c)
    far = other + move(mine, flip_c)
    low = jnp.where(c == 0, near, far)
    high = jnp.where(c == 0, far, near)
    prolonged = jnp.concatenate([low, high], axis=1).astype(jnp.bfloat16)

    t_own = p_flat.T
    t_pieces = ring(t_own, shift_x) + ring(move(t_own, flip_h), shift_x)
    blocks = project(place, t_pieces, prolonged)
    summed = blocks[0]
    for m in (1, 2, 3):
        summed = summed + move(blocks[m], shift_y(m))
    parts = summed.reshape(2, 128, 2, 128)
    total = None
    for s in range(4):
        k1 = (z // 2 + s // 2) % 2
        l0 = (z + s) % 2
        part = lax.dynamic_slice(parts, (k1, 0, l0, 0), (1, 128, 1, 128)).reshape(128, 128)

        def target(y, z, x, h, c, s=s):
            return (y, ((z // 2 + s // 2) % 2) * 2 + c, x, h, (z + s) % 2)

        got = move(part, target)
        total = got if total is None else total + got
    return total


def solution(mesh):
    placed = (
        P("row", "col", None),
        P("row", "col"),
        P("row", "col"),
        P("row", None, "col"),
        P("row", "col"),
    )
    return jax.shard_map(
        per_device, mesh=mesh, in_specs=placed, out_specs=P("row", "col"), check_vma=False
    )
```

time: 577 us -> 253 us (0.44)
  the two profiles are of different devices: /device:TPU:4 before, /device:TPU:1 now
where the time goes in v1:
time: 253 us; the launch traced here: 248 us
  starting transfers between devices  125 us (49%)
  waiting for transfers between devices  81.7 us (32%)
  local copies, waits for them, and re-layouts  18.2 us (7%)
  Pallas kernels  15.2 us (6%)
  other arithmetic  6.99 us (3%)
    ppermute x55, starting transfers between devices, move(): return lax.ppermute(array, AXES, pairs)  125 us
    ppermute x55, waiting for transfers between devices, move(): return lax.ppermute(array, AXES, pairs)  81.7 us
    pallas_call x1, Pallas kernels, apply_panel(): pl.pallas_call(apply_kernel, out_shape=(out, out), grid_spec=pltpu.Prefet...  12.2 us
    slice x8, local copies, waits for them, and re-layouts, ring(): first = move(before[:half], shift(1))  5.87 us
  transfers between devices with their start and end apart: 55, of which 19 were waited for; matrix products, arithmetic and copies ran while one was open for 9% of the time, Pallas kernels for 5%

profile of v1, /device:TPU:1, one launch (start us, length us, event | category | flops | bytes accessed | tf_op | source)
XLA Modules:
  0.0 247.8 jit_solution(8716275864169726323)
XLA Ops:
  0.7 7.7 %collective-permute-start.9 = (s32[20,5]{0,1:T(8,128)S(1)}, s32[20,5]{0,1:T(8,128)S(1)}, u32[]{:S(2)}, u32[]{:S(2)}) collective-permute-start(s32[20,5]{0,1:T(8,128)S(1)} %subtract_clamp_fusion), channel_id=1, source_target_pairs={{0,2},{1,3},{2,0},{3,1},{4,6},{5,7},{6,4},{7,5},{8,10},{9,11},{10,... | collective-permute-start | bytes 1208 | tf_op jit(solution)/shard_map/ppermute | solution.py:32
  10.5 1.7 reshape.136
  13.1 3.5 %collective-permute-start.13 = (bf16[1280,128]{1,0:T(8,128)(2,1)S(1)}, bf16[1280,128]{1,0:T(8,128)(2,1)S(1)}, u32[]{:S(2)}, u32[]{:S(2)}) collective-permute-start(bf16[1280,128]{1,0:T(8,128)(2,1)S(1)} %bitcast.28), channel_id=1, source_target_pairs={{0,0},{1,16},{2,2},{3,18},{4,4},{5,20},{6,6},{7,22},{8,8},{9,24},{... | collective-permute-start | bytes 983048 | tf_op jit(solution)/shard_map/ppermute | solution.py:32
  16.6 1.4 collective-permute-start.43
  19.4 2.5 collective-permute-start.11
  23.7 1.4 collective-permute-start.45
  25.1 1.7 collective-permute-done.13.refs_0_
  26.8 5.0 %collective-permute-start.18 = (bf16[1280,128]{1,0:T(8,128)(2,1)S(1)}, bf16[1280,128]{1,0:T(8,128)(2,1)}, u32[]{:S(2)}, u32[]{:S(2)}) collective-permute-start(bf16[1280,128]{1,0:T(8,128)(2,1)S(1)} %collective-permute-done.13.refs_0_), channel_id=1, source_target_pairs={{0,16},{1,17},{2,18},{3,19},{4,20},{5,21},{6,22},{7,23},{8,24},{9,... | collective-permute-start | bytes 983048 | tf_op jit(solution)/shard_map/ppermute | solution.py:32
  31.7 10.5 %collective-permute-start.23 = (bf16[1280,128]{1,0:T(8,128)(2,1)S(1)}, bf16[1280,128]{1,0:T(8,128)(2,1)}, u32[]{:S(2)}, u32[]{:S(2)}) collective-permute-start(bf16[1280,128]{1,0:T(8,128)(2,1)S(1)} %collective-permute-done.13.refs_0_), channel_id=1, source_target_pairs={{0,32},{1,33},{2,34},{3,35},{4,36},{5,37},{6,38},{7,39},{8,40},{9,... | collective-permute-start | bytes 983048 | tf_op jit(solution)/shard_map/ppermute | solution.py:32
  44.5 4.3 %collective-permute-done.18.refs_5_ = bf16[1280,128]{1,0:T(8,128)(2,1)} collective-permute-done((bf16[1280,128]{1,0:T(8,128)(2,1)S(1)}, bf16[1280,128]{1,0:T(8,128)(2,1)}, u32[]{:S(2)}, u32[]{:S(2)}) %collective-permute-start.18) | collective-permute-done | bytes 327712 | tf_op jit(solution)/shard_map/ppermute | solution.py:32
  48.9 19.4 %collective-permute-done.23.refs_10_ = bf16[1280,128]{1,0:T(8,128)(2,1)} collective-permute-done((bf16[1280,128]{1,0:T(8,128)(2,1)S(1)}, bf16[1280,128]{1,0:T(8,128)(2,1)}, u32[]{:S(2)}, u32[]{:S(2)}) %collective-permute-start.23) | collective-permute-done | bytes 327712 | tf_op jit(solution)/shard_map/ppermute | solution.py:32
  68.2 22.6 %collective-permute-start.14 = (bf16[1280,128]{1,0:T(8,128)(2,1)S(1)}, bf16[1280,128]{1,0:T(8,128)(2,1)S(1)}, u32[]{:S(2)}, u32[]{:S(2)}) collective-permute-start(bf16[1280,128]{1,0:T(8,128)(2,1)S(1)} %collective-permute-done.13.refs_0_), channel_id=1, source_target_pairs={{0,64},{1,65},{2,66},{3,67},{4,68},{5,69},{6,70},{7,71},{8,72},{9,... | collective-permute-start | bytes 983048 | tf_op jit(solution)/shard_map/ppermute | solution.py:32
  90.9 3.2 %collective-permute-start.15 = (bf16[1280,128]{1,0:T(8,128)(2,1)S(1)}, bf16[1280,128]{1,0:T(8,128)(2,1)S(1)}, u32[]{:S(2)}, u32[]{:S(2)}) collective-permute-start(bf16[1280,128]{1,0:T(8,128)(2,1)S(1)} %collective-permute-done.13.refs_0_), channel_id=1, source_target_pairs={{0,192},{1,193},{2,194},{3,195},{4,196},{5,197},{6,198},{7,199},{8... | collective-permute-start | bytes 983048 | tf_op jit(solution)/shard_map/ppermute | solution.py:32
  94.1 6.6 %collective-permute-done.14.refs_1_ = bf16[1280,128]{1,0:T(8,128)(2,1)S(1)} collective-permute-done((bf16[1280,128]{1,0:T(8,128)(2,1)S(1)}, bf16[1280,128]{1,0:T(8,128)(2,1)S(1)}, u32[]{:S(2)}, u32[]{:S(2)}) %collective-permute-start.14) | collective-permute-done | bytes 327712 | tf_op jit(solution)/shard_map/ppermute | solution.py:32
  100.7 2.9 %collective-permute-start.20 = (bf16[1280,128]{1,0:T(8,128)(2,1)}, bf16[1280,128]{1,0:T(8,128)(2,1)}, u32[]{:S(2)}, u32[]{:S(2)}) collective-permute-start(bf16[1280,128]{1,0:T(8,128)(2,1)} %collective-permute-done.18.refs_5_), channel_id=1, source_target_pairs={{0,192},{1,193},{2,194},{3,195},{4,196},{5,197},{6,198},{7,199},{8... | collective-permute-start | bytes 983048 | tf_op jit(solution)/shard_map/ppermute | solution.py:32
  103.7 2.7 %collective-permute-start.17 = (bf16[640,128]{1,0:T(8,128)(2,1)S(1)}, bf16[640,128]{1,0:T(8,128)(2,1)S(1)}, u32[]{:S(2)}, u32[]{:S(2)}) collective-permute-start(bf16[640,128]{1,0:T(8,128)(2,1)S(1)} %slice.77), channel_id=1, source_target_pairs={{0,192},{1,193},{2,194},{3,195},{4,196},{5,197},{6,198},{7,199},{8... | collective-permute-start | bytes 491528 | tf_op jit(solution)/shard_map/ppermute | solution.py:32
  106.4 7.3 %collective-permute-done.16.refs_3_ = bf16[640,128]{1,0:T(8,128)(2,1)S(1)} collective-permute-done((bf16[640,128]{1,0:T(8,128)(2,1)S(1)}, bf16[640,128]{1,0:T(8,128)(2,1)S(1)}, u32[]{:S(2)}, u32[]{:S(2)}) %collective-permute-start.16) | collective-permute-done | bytes 163872 | tf_op jit(solution)/shard_map/ppermute | solution.py:32
  113.7 1.3 collective-permute-done.17.refs_4_
  115.7 1.7 collective-permute-start.39
  117.4 3.5 %collective-permute-start.25 = (bf16[1280,128]{1,0:T(8,128)(2,1)}, bf16[1280,128]{1,0:T(8,128)(2,1)}, u32[]{:S(2)}, u32[]{:S(2)}) collective-permute-start(bf16[1280,128]{1,0:T(8,128)(2,1)} %collective-permute-done.23.refs_10_), channel_id=1, source_target_pairs={{0,192},{1,193},{2,194},{3,195},{4,196},{5,197},{6,198},{7,199},{8... | collective-permute-start | bytes 983048 | tf_op jit(solution)/shard_map/ppermute | solution.py:32
  121.0 2.7 %collective-permute-start.30 = (bf16[1280,128]{1,0:T(8,128)(2,1)}, bf16[1280,128]{1,0:T(8,128)(2,1)}, u32[]{:S(2)}, u32[]{:S(2)}) collective-permute-start(bf16[1280,128]{1,0:T(8,128)(2,1)} %copy-done.6), channel_id=1, source_target_pairs={{0,192},{1,193},{2,194},{3,195},{4,196},{5,197},{6,198},{7,199},{8... | collective-permute-start | bytes 983048 | tf_op jit(solution)/shard_map/ppermute | solution.py:32
  125.3 4.9 %collective-permute-done.29.refs_16_ = bf16[1280,128]{1,0:T(8,128)(2,1)} collective-permute-done((bf16[1280,128]{1,0:T(8,128)(2,1)}, bf16[1280,128]{1,0:T(8,128)(2,1)}, u32[]{:S(2)}, u32[]{:S(2)}) %collective-permute-start.29) | collective-permute-done | bytes 327712 | tf_op jit(solution)/shard_map/ppermute | solution.py:32
  130.2 1.9 copy.28
  132.2 1.6 slice.78
  133.8 1.6 slice.79
  135.4 1.6 slice.80
  137.0 2.7 %collective-permute-start.22 = (bf16[640,128]{1,0:T(8,128)(2,1)}, bf16[640,128]{1,0:T(8,128)(2,1)}, u32[]{:S(2)}, u32[]{:S(2)}) collective-permute-start(bf16[640,128]{1,0:T(8,128)(2,1)} %slice.79), channel_id=1, source_target_pairs={{0,192},{1,193},{2,194},{3,195},{4,196},{5,197},{6,198},{7,199},{8... | collective-permute-start | bytes 491528 | tf_op jit(solution)/shard_map/ppermute | solution.py:32
  139.7 8.6 %collective-permute-start.26 = (bf16[640,128]{1,0:T(8,128)(2,1)}, bf16[640,128]{1,0:T(8,128)(2,1)}, u32[]{:S(2)}, u32[]{:S(2)}) collective-permute-start(bf16[640,128]{1,0:T(8,128)(2,1)} %slice.80), channel_id=1, source_target_pairs={{0,64},{1,65},{2,66},{3,67},{4,68},{5,69},{6,70},{7,71},{8,72},{9,... | collective-permute-start | bytes 491528 | tf_op jit(solution)/shard_map/ppermute | solution.py:32
  153.1 2.7 %collective-permute-start.27 = (bf16[640,128]{1,0:T(8,128)(2,1)S(1)}, bf16[640,128]{1,0:T(8,128)(2,1)S(1)}, u32[]{:S(2)}, u32[]{:S(2)}) collective-permute-start(bf16[640,128]{1,0:T(8,128)(2,1)S(1)} %slice.81), channel_id=1, source_target_pairs={{0,192},{1,193},{2,194},{3,195},{4,196},{5,197},{6,198},{7,199},{8... | collective-permute-start | bytes 491528 | tf_op jit(solution)/shard_map/ppermute | solution.py:32
  155.8 2.7 %collective-permute-start.32 = (bf16[640,128]{1,0:T(8,128)(2,1)S(1)}, bf16[640,128]{1,0:T(8,128)(2,1)S(1)}, u32[]{:S(2)}, u32[]{:S(2)}) collective-permute-start(bf16[640,128]{1,0:T(8,128)(2,1)S(1)} %slice.83), channel_id=1, source_target_pairs={{0,192},{1,193},{2,194},{3,195},{4,196},{5,197},{6,198},{7,199},{8... | collective-permute-start | bytes 491528 | tf_op jit(solution)/shard_map/ppermute | solution.py:32
  158.5 1.5 collective-permute-start.40
  162.8 5.9 %collective-permute-done.40.refs_28_ = bf16[640,256]{1,0:T(8,128)(2,1)S(1)} collective-permute-done((bf16[640,256]{1,0:T(8,128)(2,1)S(1)}, bf16[640,256]{1,0:T(8,128)(2,1)S(1)}, u32[]{:S(2)}, u32[]{:S(2)}) %collective-permute-start.40) | collective-permute-done | bytes 327712 | tf_op jit(solution)/shard_map/ppermute | solution.py:32
  168.7 12.2 %apply_panel.1 = (f32[1280,128]{1,0:T(8,128)}, f32[1280,128]{1,0:T(8,128)}) custom-call(s32[800]{0:T(1024)S(1)} %mul.44.idx, s32[5]{0:T(128)S(1)} %stack.47.place, bf16[1280,128]{1,0:T(8,128)(2,1)S(1)} %copy-done.5, bf16[1280,128]{1,0:T(8,128)(2,1)S(1)} %copy-done.1, bf16[1280,128]{1,0:T(8,128)(2,1)S(1)} %copy-done.3, ...), custom_call_target="tpu_custom_call" | custom-call | flops 1342177280 | bytes 12582912 | tf_op jit(solution)/shard_map/apply_panel/pallas_call | solution.py:124
  181.5 1.5 collective-permute-start.5
  185.1 5.8 %collective-permute-done.1.refs_2_ = bf16[128,1280]{1,0:T(8,128)(2,1)S(1)} collective-permute-done((bf16[128,1280]{1,0:T(8,128)(2,1)}, bf16[128,1280]{1,0:T(8,128)(2,1)S(1)}, u32[]{:S(2)}, u32[]{:S(2)}) %collective-permute-start.1) | collective-permute-done | bytes 327712 | tf_op jit(solution)/shard_map/ppermute | solution.py:32
  192.1 1.6 collective-permute-start.3
  193.7 4.2 %collective-permute-done.6.refs_7_ = bf16[128,1280]{1,0:T(8,128)(2,1)S(1)} collective-permute-done((bf16[128,1280]{1,0:T(8,128)(2,1)}, bf16[128,1280]{1,0:T(8,128)(2,1)S(1)}, u32[]{:S(2)}, u32[]{:S(2)}) %collective-permute-start.6) | collective-permute-done | bytes 327712 | tf_op jit(solution)/shard_map/ppermute | solution.py:32
  198.0 3.0 %collective-permute-start.8 = (bf16[64,1280]{1,0:T(8,128)(2,1)S(1)}, bf16[64,1280]{1,0:T(8,128)(2,1)S(1)}, u32[]{:S(2)}, u32[]{:S(2)}) collective-permute-start(bf16[64,1280]{1,0:T(8,128)(2,1)S(1)} %slice.75), channel_id=1, source_target_pairs={{0,12},{1,13},{2,14},{3,15},{4,0},{5,1},{6,2},{7,3},{8,4},{9,5},{1... | collective-permute-start | bytes 491528 | tf_op jit(solution)/shard_map/ppermute | solution.py:32
  200.9 1.4 select_convert_fusion.1
  204.5 3.1 %project.1 = (f32[256,256]{1,0:T(8,128)S(1)}, f32[256,256]{1,0:T(8,128)S(1)}, f32[256,256]{1,0:T(8,128)S(1)}, f32[256,256]{1,0:T(8,128)S(1)}) custom-call(s32[5]{0:T(128)S(1)} %stack.47.place, bf16[128,1280]{1,0:T(8,128)(2,1)} %bitcast.7.refs_0_, bf16[128,1280]{1,0:T(8,128)(2,1)} %collective-permute-done.refs_1_, ...), custom_call_target="tpu_custom_call" | custom-call | flops 671088640 | bytes 4194304 | tf_op jit(solution)/shard_map/project/pallas_call | solution.py:175
  208.7 1.7 collective-permute-start.50
  210.4 6.7 %collective-permute-done.48 = f32[256,256]{1,0:T(8,128)S(1)} collective-permute-done((f32[256,256]{1,0:T(8,128)S(1)}, f32[256,256]{1,0:T(8,128)S(1)}, u32[]{:S(2)}, u32[]{:S(2)}) %collective-permute-start.48) | collective-permute-done | bytes 262176 | tf_op jit(solution)/shard_map/ppermute | solution.py:32
  217.1 2.3 collective-permute-done.49
  219.4 2.3 collective-permute-done.50
  222.1 16.9 %collective-permute-start.51 = (f32[128,128]{1,0:T(8,128)S(1)}, f32[128,128]{1,0:T(8,128)S(1)}, u32[]{:S(2)}, u32[]{:S(2)}) collective-permute-start(f32[128,128]{1,0:T(8,128)S(1)} %bitcast.34), channel_id=1, source_target_pairs={{0,0},{1,16},{2,2},{3,18},{4,4},{5,20},{6,6},{7,22},{8,8},{9,24},{... | collective-permute-start | bytes 196616 | tf_op jit(solution)/shard_map/ppermute | solution.py:32
  239.2 2.1 collective-permute-start.54
  241.5 3.2 %collective-permute-done.53 = f32[128,128]{1,0:T(8,128)S(1)} collective-permute-done((f32[128,128]{1,0:T(8,128)S(1)}, f32[128,128]{1,0:T(8,128)S(1)}, u32[]{:S(2)}, u32[]{:S(2)}) %collective-permute-start.53) | collective-permute-done | bytes 65568 | tf_op jit(solution)/shard_map/ppermute | solution.py:32
  244.7 2.3 collective-permute-done.54
  (144 shorter events, 27.7 us)
Async XLA Ops:
  0.7 17.4 %collective-permute-start.9 = (s32[20,5]{0,1:T(8,128)S(1)}, s32[20,5]{0,1:T(8,128)S(1)}, u32[]{:S(2)}, u32[]{:S(2)}) collective-permute-start(s32[20,5]{0,1:T(8,128)S(1)} %subtract_clamp_fusion), channel_id=1, source_target_pairs={{0,2},{1,3},{2,0},{3,1},{4,6},{5,7},{6,4},{7,5},{8,10},{9,11},{10,... | collective-permute-start | bytes 1208 | tf_op jit(solution)/shard_map/ppermute | solution.py:32
  13.1 13.7 %collective-permute-start.13 = (bf16[1280,128]{1,0:T(8,128)(2,1)S(1)}, bf16[1280,128]{1,0:T(8,128)(2,1)S(1)}, u32[]{:S(2)}, u32[]{:S(2)}) collective-permute-start(bf16[1280,128]{1,0:T(8,128)(2,1)S(1)} %bitcast.28), channel_id=1, source_target_pairs={{0,0},{1,16},{2,2},{3,18},{4,4},{5,20},{6,6},{7,22},{8,8},{9,24},{... | collective-permute-start | bytes 983048 | tf_op jit(solution)/shard_map/ppermute | solution.py:32
  16.6 25.6 %collective-permute-start.43 = (bf16[1280,64]{1,0:T(8,128)(2,1)S(1)}, bf16[1280,64]{1,0:T(8,128)(2,1)}, u32[]{:S(2)}, u32[]{:S(2)}) collective-permute-start(bf16[1280,64]{1,0:T(8,128)(2,1)S(1)} %bitcast_add_fusion), channel_id=1, source_target_pairs={{0,4},{2,6},{17,21},{19,23},{32,36},{34,38},{49,53},{51,55},{68,72... | collective-permute-start | bytes 491528 | tf_op jit(solution)/shard_map/ppermute | solution.py:32
  21.8 9.9 %collective-permute-start.12 = (s32[2,20,5]{1,2,0:T(8,128)S(1)}, s32[2,20,5]{1,2,0:T(8,128)S(1)}, u32[]{:S(2)}, u32[]{:S(2)}) collective-permute-start(s32[2,20,5]{1,2,0:T(8,128)S(1)} %get-tuple-element.24), channel_id=1, source_target_pairs={{0,12},{1,13},{2,14},{3,15},{4,0},{5,1},{6,2},{7,3},{8,4},{9,5},{1... | collective-permute-start | bytes 2408 | tf_op jit(solution)/shard_map/ppermute | solution.py:32
  23.0 21.3 %collective-permute-start.44 = (bf16[1280,64]{1,0:T(8,128)(2,1)S(1)}, bf16[1280,64]{1,0:T(8,128)(2,1)S(1)}, u32[]{:S(2)}, u32[]{:S(2)}) collective-permute-start(bf16[1280,64]{1,0:T(8,128)(2,1)S(1)} %bitcast_add_fusion), channel_id=1, source_target_pairs={{0,8},{2,10},{17,25},{19,27},{32,40},{34,42},{49,57},{51,59},{68,7... | collective-permute-start | bytes 491528 | tf_op jit(solution)/shard_map/ppermute | solution.py:32
  23.7 20.8 %collective-permute-start.45 = (bf16[1280,64]{1,0:T(8,128)(2,1)S(1)}, bf16[1280,64]{1,0:T(8,128)(2,1)}, u32[]{:S(2)}, u32[]{:S(2)}) collective-permute-start(bf16[1280,64]{1,0:T(8,128)(2,1)S(1)} %bitcast_add_fusion), channel_id=1, source_target_pairs={{0,12},{2,14},{17,29},{19,31},{32,44},{34,46},{49,61},{51,63},{68,... | collective-permute-start | bytes 491528 | tf_op jit(solution)/shard_map/ppermute | solution.py:32
  26.8 22.1 %collective-permute-start.18 = (bf16[1280,128]{1,0:T(8,128)(2,1)S(1)}, bf16[1280,128]{1,0:T(8,128)(2,1)}, u32[]{:S(2)}, u32[]{:S(2)}) collective-permute-start(bf16[1280,128]{1,0:T(8,128)(2,1)S(1)} %collective-permute-done.13.refs_0_), channel_id=1, source_target_pairs={{0,16},{1,17},{2,18},{3,19},{4,20},{5,21},{6,22},{7,23},{8,24},{9,... | collective-permute-start | bytes 983048 | tf_op jit(solution)/shard_map/ppermute | solution.py:32
  31.7 36.5 %collective-permute-start.23 = (bf16[1280,128]{1,0:T(8,128)(2,1)S(1)}, bf16[1280,128]{1,0:T(8,128)(2,1)}, u32[]{:S(2)}, u32[]{:S(2)}) collective-permute-start(bf16[1280,128]{1,0:T(8,128)(2,1)S(1)} %collective-permute-done.13.refs_0_), channel_id=1, source_target_pairs={{0,32},{1,33},{2,34},{3,35},{4,36},{5,37},{6,38},{7,39},{8,40},{9,... | collective-permute-start | bytes 983048 | tf_op jit(solution)/shard_map/ppermute | solution.py:32
  42.2 48.6 %collective-permute-start.28 = (bf16[1280,128]{1,0:T(8,128)(2,1)S(1)}, bf16[1280,128]{1,0:T(8,128)(2,1)S(1)}, u32[]{:S(2)}, u32[]{:S(2)}) collective-permute-start(bf16[1280,128]{1,0:T(8,128)(2,1)S(1)} %collective-permute-done.13.refs_0_), channel_id=1, source_target_pairs={{0,48},{1,49},{2,50},{3,51},{4,52},{5,53},{6,54},{7,55},{8,56},{9,... | collective-permute-start | bytes 983048 | tf_op jit(solution)/shard_map/ppermute | solution.py:32
  44.3 59.3 %collective-permute-start.37 = (bf16[1280,256]{1,0:T(8,128)(2,1)S(1)}, bf16[1280,256]{1,0:T(8,128)(2,1)}, u32[]{:S(2)}, u32[]{:S(2)}) collective-permute-start(bf16[1280,256]{1,0:T(8,128)(2,1)S(1)} %reshape.137.refs_20_), channel_id=1, source_target_pairs={{0,2},{1,3},{2,0},{3,1},{4,6},{5,7},{6,4},{7,5},{8,10},{9,11},{10,... | collective-permute-start | bytes 1966088 | tf_op jit(solution)/shard_map/ppermute | solution.py:32
  44.4 59.3 %collective-permute-start.33 = (bf16[1280,256]{1,0:T(8,128)(2,1)S(1)}, bf16[1280,256]{1,0:T(8,128)(2,1)S(1)}, u32[]{:S(2)}, u32[]{:S(2)}) collective-permute-start(bf16[1280,256]{1,0:T(8,128)(2,1)S(1)} %reshape.137.refs_20_), channel_id=1, source_target_pairs={{0,4},{1,5},{2,6},{3,7},{4,8},{5,9},{6,10},{7,11},{8,12},{9,13},{1... | collective-permute-start | bytes 1966088 | tf_op jit(solution)/shard_map/ppermute | solution.py:32
  48.9 57.5 %collective-permute-start.34 = (bf16[1280,256]{1,0:T(8,128)(2,1)S(1)}, bf16[1280,256]{1,0:T(8,128)(2,1)S(1)}, u32[]{:S(2)}, u32[]{:S(2)}) collective-permute-start(bf16[1280,256]{1,0:T(8,128)(2,1)S(1)} %reshape.137.refs_20_), channel_id=1, source_target_pairs={{0,12},{1,13},{2,14},{3,15},{4,0},{5,1},{6,2},{7,3},{8,4},{9,5},{1... | collective-permute-start | bytes 1966088 | tf_op jit(solution)/shard_map/ppermute | solution.py:32
  68.2 32.5 %collective-permute-start.14 = (bf16[1280,128]{1,0:T(8,128)(2,1)S(1)}, bf16[1280,128]{1,0:T(8,128)(2,1)S(1)}, u32[]{:S(2)}, u32[]{:S(2)}) collective-permute-start(bf16[1280,128]{1,0:T(8,128)(2,1)S(1)} %collective-permute-done.13.refs_0_), channel_id=1, source_target_pairs={{0,64},{1,65},{2,66},{3,67},{4,68},{5,69},{6,70},{7,71},{8,72},{9,... | collective-permute-start | bytes 983048 | tf_op jit(solution)/shard_map/ppermute | solution.py:32
  90.9 9.9 %collective-permute-start.15 = (bf16[1280,128]{1,0:T(8,128)(2,1)S(1)}, bf16[1280,128]{1,0:T(8,128)(2,1)S(1)}, u32[]{:S(2)}, u32[]{:S(2)}) collective-permute-start(bf16[1280,128]{1,0:T(8,128)(2,1)S(1)} %collective-permute-done.13.refs_0_), channel_id=1, source_target_pairs={{0,192},{1,193},{2,194},{3,195},{4,196},{5,197},{6,198},{7,199},{8... | collective-permute-start | bytes 983048 | tf_op jit(solution)/shard_map/ppermute | solution.py:32
  100.7 16.7 %collective-permute-start.19 = (bf16[1280,128]{1,0:T(8,128)(2,1)}, bf16[1280,128]{1,0:T(8,128)(2,1)}, u32[]{:S(2)}, u32[]{:S(2)}) collective-permute-start(bf16[1280,128]{1,0:T(8,128)(2,1)} %collective-permute-done.18.refs_5_), channel_id=1, source_target_pairs={{0,64},{1,65},{2,66},{3,67},{4,68},{5,69},{6,70},{7,71},{8,72},{9,... | collective-permute-start | bytes 983048 | tf_op jit(solution)/shard_map/ppermute | solution.py:32
  100.7 20.2 %collective-permute-start.20 = (bf16[1280,128]{1,0:T(8,128)(2,1)}, bf16[1280,128]{1,0:T(8,128)(2,1)}, u32[]{:S(2)}, u32[]{:S(2)}) collective-permute-start(bf16[1280,128]{1,0:T(8,128)(2,1)} %collective-permute-done.18.refs_5_), channel_id=1, source_target_pairs={{0,192},{1,193},{2,194},{3,195},{4,196},{5,197},{6,198},{7,199},{8... | collective-permute-start | bytes 983048 | tf_op jit(solution)/shard_map/ppermute | solution.py:32
  103.6 10.0 %collective-permute-start.16 = (bf16[640,128]{1,0:T(8,128)(2,1)S(1)}, bf16[640,128]{1,0:T(8,128)(2,1)S(1)}, u32[]{:S(2)}, u32[]{:S(2)}) collective-permute-start(bf16[640,128]{1,0:T(8,128)(2,1)S(1)} %slice.76), channel_id=1, source_target_pairs={{0,64},{1,65},{2,66},{3,67},{4,68},{5,69},{6,70},{7,71},{8,72},{9,... | collective-permute-start | bytes 491528 | tf_op jit(solution)/shard_map/ppermute | solution.py:32
  103.7 11.3 %collective-permute-start.17 = (bf16[640,128]{1,0:T(8,128)(2,1)S(1)}, bf16[640,128]{1,0:T(8,128)(2,1)S(1)}, u32[]{:S(2)}, u32[]{:S(2)}) collective-permute-start(bf16[640,128]{1,0:T(8,128)(2,1)S(1)} %slice.77), channel_id=1, source_target_pairs={{0,192},{1,193},{2,194},{3,195},{4,196},{5,197},{6,198},{7,199},{8... | collective-permute-start | bytes 491528 | tf_op jit(solution)/shard_map/ppermute | solution.py:32
  106.4 14.6 %collective-permute-start.24 = (bf16[1280,128]{1,0:T(8,128)(2,1)}, bf16[1280,128]{1,0:T(8,128)(2,1)}, u32[]{:S(2)}, u32[]{:S(2)}) collective-permute-start(bf16[1280,128]{1,0:T(8,128)(2,1)} %collective-permute-done.23.refs_10_), channel_id=1, source_target_pairs={{0,64},{1,65},{2,66},{3,67},{4,68},{5,69},{6,70},{7,71},{8,72},{9,... | collective-permute-start | bytes 983048 | tf_op jit(solution)/shard_map/ppermute | solution.py:32
  113.7 23.3 %collective-permute-start.38 = (bf16[1280,256]{1,0:T(8,128)(2,1)}, bf16[1280,256]{1,0:T(8,128)(2,1)S(1)}, u32[]{:S(2)}, u32[]{:S(2)}) collective-permute-start(bf16[1280,256]{1,0:T(8,128)(2,1)} %collective-permute-done.37.refs_25_), channel_id=1, source_target_pairs={{0,4},{1,5},{2,6},{3,7},{4,8},{5,9},{6,10},{7,11},{8,12},{9,13},{1... | collective-permute-start | bytes 1966088 | tf_op jit(solution)/shard_map/ppermute | solution.py:32
  115.7 24.0 %collective-permute-start.39 = (bf16[1280,256]{1,0:T(8,128)(2,1)}, bf16[1280,256]{1,0:T(8,128)(2,1)S(1)}, u32[]{:S(2)}, u32[]{:S(2)}) collective-permute-start(bf16[1280,256]{1,0:T(8,128)(2,1)} %collective-permute-done.37.refs_25_), channel_id=1, source_target_pairs={{0,12},{1,13},{2,14},{3,15},{4,0},{5,1},{6,2},{7,3},{8,4},{9,5},{1... | collective-permute-start | bytes 1966088 | tf_op jit(solution)/shard_map/ppermute | solution.py:32
  117.4 7.9 %collective-permute-start.25 = (bf16[1280,128]{1,0:T(8,128)(2,1)}, bf16[1280,128]{1,0:T(8,128)(2,1)}, u32[]{:S(2)}, u32[]{:S(2)}) collective-permute-start(bf16[1280,128]{1,0:T(8,128)(2,1)} %collective-permute-done.23.refs_10_), channel_id=1, source_target_pairs={{0,192},{1,193},{2,194},{3,195},{4,196},{5,197},{6,198},{7,199},{8... | collective-permute-start | bytes 983048 | tf_op jit(solution)/shard_map/ppermute | solution.py:32
  121.0 9.2 %collective-permute-start.29 = (bf16[1280,128]{1,0:T(8,128)(2,1)}, bf16[1280,128]{1,0:T(8,128)(2,1)}, u32[]{:S(2)}, u32[]{:S(2)}) collective-permute-start(bf16[1280,128]{1,0:T(8,128)(2,1)} %copy-done.6), channel_id=1, source_target_pairs={{0,64},{1,65},{2,66},{3,67},{4,68},{5,69},{6,70},{7,71},{8,72},{9,... | collective-permute-start | bytes 983048 | tf_op jit(solution)/shard_map/ppermute | solution.py:32
  121.0 16.0 %collective-permute-start.30 = (bf16[1280,128]{1,0:T(8,128)(2,1)}, bf16[1280,128]{1,0:T(8,128)(2,1)}, u32[]{:S(2)}, u32[]{:S(2)}) collective-permute-start(bf16[1280,128]{1,0:T(8,128)(2,1)} %copy-done.6), channel_id=1, source_target_pairs={{0,192},{1,193},{2,194},{3,195},{4,196},{5,197},{6,198},{7,199},{8... | collective-permute-start | bytes 983048 | tf_op jit(solution)/shard_map/ppermute | solution.py:32
  125.3 27.8 %collective-permute-start.35 = (bf16[640,256]{1,0:T(8,128)(2,1)}, bf16[640,256]{1,0:T(8,128)(2,1)}, u32[]{:S(2)}, u32[]{:S(2)}) collective-permute-start(bf16[640,256]{1,0:T(8,128)(2,1)} %slice.85), channel_id=1, source_target_pairs={{0,4},{1,5},{2,6},{3,7},{4,8},{5,9},{6,10},{7,11},{8,12},{9,13},{1... | collective-permute-start | bytes 983048 | tf_op jit(solution)/shard_map/ppermute | solution.py:32
  130.2 25.6 %collective-permute-start.36 = (bf16[640,256]{1,0:T(8,128)(2,1)}, bf16[640,256]{1,0:T(8,128)(2,1)}, u32[]{:S(2)}, u32[]{:S(2)}) collective-permute-start(bf16[640,256]{1,0:T(8,128)(2,1)} %slice.86), channel_id=1, source_target_pairs={{0,12},{1,13},{2,14},{3,15},{4,0},{5,1},{6,2},{7,3},{8,4},{9,5},{1... | collective-permute-start | bytes 983048 | tf_op jit(solution)/shard_map/ppermute | solution.py:32
  137.0 18.8 %collective-permute-start.21 = (bf16[640,128]{1,0:T(8,128)(2,1)}, bf16[640,128]{1,0:T(8,128)(2,1)}, u32[]{:S(2)}, u32[]{:S(2)}) collective-permute-start(bf16[640,128]{1,0:T(8,128)(2,1)} %slice.78), channel_id=1, source_target_pairs={{0,64},{1,65},{2,66},{3,67},{4,68},{5,69},{6,70},{7,71},{8,72},{9,... | collective-permute-start | bytes 491528 | tf_op jit(solution)/shard_map/ppermute | solution.py:32
  137.0 21.5 %collective-permute-start.22 = (bf16[640,128]{1,0:T(8,128)(2,1)}, bf16[640,128]{1,0:T(8,128)(2,1)}, u32[]{:S(2)}, u32[]{:S(2)}) collective-permute-start(bf16[640,128]{1,0:T(8,128)(2,1)} %slice.79), channel_id=1, source_target_pairs={{0,192},{1,193},{2,194},{3,195},{4,196},{5,197},{6,198},{7,199},{8... | collective-permute-start | bytes 491528 | tf_op jit(solution)/shard_map/ppermute | solution.py:32
  139.7 20.3 %collective-permute-start.26 = (bf16[640,128]{1,0:T(8,128)(2,1)}, bf16[640,128]{1,0:T(8,128)(2,1)}, u32[]{:S(2)}, u32[]{:S(2)}) collective-permute-start(bf16[640,128]{1,0:T(8,128)(2,1)} %slice.80), channel_id=1, source_target_pairs={{0,64},{1,65},{2,66},{3,67},{4,68},{5,69},{6,70},{7,71},{8,72},{9,... | collective-permute-start | bytes 491528 | tf_op jit(solution)/shard_map/ppermute | solution.py:32
  153.1 9.3 %collective-permute-start.27 = (bf16[640,128]{1,0:T(8,128)(2,1)S(1)}, bf16[640,128]{1,0:T(8,128)(2,1)S(1)}, u32[]{:S(2)}, u32[]{:S(2)}) collective-permute-start(bf16[640,128]{1,0:T(8,128)(2,1)S(1)} %slice.81), channel_id=1, source_target_pairs={{0,192},{1,193},{2,194},{3,195},{4,196},{5,197},{6,198},{7,199},{8... | collective-permute-start | bytes 491528 | tf_op jit(solution)/shard_map/ppermute | solution.py:32
  155.8 6.6 %collective-permute-start.31 = (bf16[640,128]{1,0:T(8,128)(2,1)S(1)}, bf16[640,128]{1,0:T(8,128)(2,1)S(1)}, u32[]{:S(2)}, u32[]{:S(2)}) collective-permute-start(bf16[640,128]{1,0:T(8,128)(2,1)S(1)} %slice.82), channel_id=1, source_target_pairs={{0,64},{1,65},{2,66},{3,67},{4,68},{5,69},{6,70},{7,71},{8,72},{9,... | collective-permute-start | bytes 491528 | tf_op jit(solution)/shard_map/ppermute | solution.py:32
  155.8 7.0 %collective-permute-start.32 = (bf16[640,128]{1,0:T(8,128)(2,1)S(1)}, bf16[640,128]{1,0:T(8,128)(2,1)S(1)}, u32[]{:S(2)}, u32[]{:S(2)}) collective-permute-start(bf16[640,128]{1,0:T(8,128)(2,1)S(1)} %slice.83), channel_id=1, source_target_pairs={{0,192},{1,193},{2,194},{3,195},{4,196},{5,197},{6,198},{7,199},{8... | collective-permute-start | bytes 491528 | tf_op jit(solution)/shard_map/ppermute | solution.py:32
  158.5 10.1 %collective-permute-start.40 = (bf16[640,256]{1,0:T(8,128)(2,1)S(1)}, bf16[640,256]{1,0:T(8,128)(2,1)S(1)}, u32[]{:S(2)}, u32[]{:S(2)}) collective-permute-start(bf16[640,256]{1,0:T(8,128)(2,1)S(1)} %slice.87), channel_id=1, source_target_pairs={{0,4},{1,5},{2,6},{3,7},{4,8},{5,9},{6,10},{7,11},{8,12},{9,13},{1... | collective-permute-start | bytes 983048 | tf_op jit(solution)/shard_map/ppermute | solution.py:32
  160.0 8.7 %collective-permute-start.41 = (bf16[640,256]{1,0:T(8,128)(2,1)S(1)}, bf16[640,256]{1,0:T(8,128)(2,1)S(1)}, u32[]{:S(2)}, u32[]{:S(2)}) collective-permute-start(bf16[640,256]{1,0:T(8,128)(2,1)S(1)} %slice.88), channel_id=1, source_target_pairs={{0,12},{1,13},{2,14},{3,15},{4,0},{5,1},{6,2},{7,3},{8,4},{9,5},{1... | collective-permute-start | bytes 983048 | tf_op jit(solution)/shard_map/ppermute | solution.py:32
  162.3 19.1 %collective-permute-start.4 = (bf16[128,1280]{1,0:T(8,128)(2,1)}, bf16[128,1280]{1,0:T(8,128)(2,1)}, u32[]{:S(2)}, u32[]{:S(2)}) collective-permute-start(bf16[128,1280]{1,0:T(8,128)(2,1)} %bitcast.7.refs_0_), channel_id=1, source_target_pairs={{0,2},{1,3},{2,0},{3,1},{4,6},{5,7},{6,4},{7,5},{8,10},{9,11},{10,... | collective-permute-start | bytes 983048 | tf_op jit(solution)/shard_map/ppermute | solution.py:32
  162.4 20.5 %collective-permute-start = (bf16[128,1280]{1,0:T(8,128)(2,1)}, bf16[128,1280]{1,0:T(8,128)(2,1)}, u32[]{:S(2)}, u32[]{:S(2)}) collective-permute-start(bf16[128,1280]{1,0:T(8,128)(2,1)} %bitcast.7.refs_0_), channel_id=1, source_target_pairs={{0,4},{1,5},{2,6},{3,7},{4,8},{5,9},{6,10},{7,11},{8,12},{9,13},{1... | collective-permute-start | bytes 983048 | tf_op jit(solution)/shard_map/ppermute | solution.py:32
  180.8 17.1 %collective-permute-start.46 = (f32[1280,128]{1,0:T(8,128)}, f32[1280,128]{1,0:T(8,128)S(1)}, u32[]{:S(2)}, u32[]{:S(2)}) collective-permute-start(f32[1280,128]{1,0:T(8,128)} %get-tuple-element.12), channel_id=1, source_target_pairs={{0,1},{1,0},{2,3},{3,2},{4,5},{5,4},{6,7},{7,6},{8,9},{9,8},{10,11... | collective-permute-start | bytes 1966088 | tf_op jit(solution)/shard_map/ppermute | solution.py:32
  180.9 20.0 %collective-permute-start.47 = (f32[1280,128]{1,0:T(8,128)}, f32[1280,128]{1,0:T(8,128)S(1)}, u32[]{:S(2)}, u32[]{:S(2)}) collective-permute-start(f32[1280,128]{1,0:T(8,128)} %get-tuple-element.11), channel_id=1, source_target_pairs={{0,1},{1,0},{2,3},{3,2},{4,5},{5,4},{6,7},{7,6},{8,9},{9,8},{10,11... | collective-permute-start | bytes 1966088 | tf_op jit(solution)/shard_map/ppermute | solution.py:32
  181.4 9.5 %collective-permute-start.1 = (bf16[128,1280]{1,0:T(8,128)(2,1)}, bf16[128,1280]{1,0:T(8,128)(2,1)S(1)}, u32[]{:S(2)}, u32[]{:S(2)}) collective-permute-start(bf16[128,1280]{1,0:T(8,128)(2,1)} %bitcast.7.refs_0_), channel_id=1, source_target_pairs={{0,12},{1,13},{2,14},{3,15},{4,0},{5,1},{6,2},{7,3},{8,4},{9,5},{1... | collective-permute-start | bytes 983048 | tf_op jit(solution)/shard_map/ppermute | solution.py:32
  181.5 10.7 %collective-permute-start.5 = (bf16[128,1280]{1,0:T(8,128)(2,1)}, bf16[128,1280]{1,0:T(8,128)(2,1)S(1)}, u32[]{:S(2)}, u32[]{:S(2)}) collective-permute-start(bf16[128,1280]{1,0:T(8,128)(2,1)} %collective-permute-done.4.refs_5_), channel_id=1, source_target_pairs={{0,4},{1,5},{2,6},{3,7},{4,8},{5,9},{6,10},{7,11},{8,12},{9,13},{1... | collective-permute-start | bytes 983048 | tf_op jit(solution)/shard_map/ppermute | solution.py:32
  182.9 15.0 %collective-permute-start.6 = (bf16[128,1280]{1,0:T(8,128)(2,1)}, bf16[128,1280]{1,0:T(8,128)(2,1)S(1)}, u32[]{:S(2)}, u32[]{:S(2)}) collective-permute-start(bf16[128,1280]{1,0:T(8,128)(2,1)} %collective-permute-done.4.refs_5_), channel_id=1, source_target_pairs={{0,12},{1,13},{2,14},{3,15},{4,0},{5,1},{6,2},{7,3},{8,4},{9,5},{1... | collective-permute-start | bytes 983048 | tf_op jit(solution)/shard_map/ppermute | solution.py:32
  190.9 11.5 %collective-permute-start.2 = (bf16[64,1280]{1,0:T(8,128)(2,1)S(1)}, bf16[64,1280]{1,0:T(8,128)(2,1)S(1)}, u32[]{:S(2)}, u32[]{:S(2)}) collective-permute-start(bf16[64,1280]{1,0:T(8,128)(2,1)S(1)} %slice.72), channel_id=1, source_target_pairs={{0,4},{1,5},{2,6},{3,7},{4,8},{5,9},{6,10},{7,11},{8,12},{9,13},{1... | collective-permute-start | bytes 491528 | tf_op jit(solution)/shard_map/ppermute | solution.py:32
  192.1 10.3 %collective-permute-start.3 = (bf16[64,1280]{1,0:T(8,128)(2,1)S(1)}, bf16[64,1280]{1,0:T(8,128)(2,1)S(1)}, u32[]{:S(2)}, u32[]{:S(2)}) collective-permute-start(bf16[64,1280]{1,0:T(8,128)(2,1)S(1)} %slice.73), channel_id=1, source_target_pairs={{0,12},{1,13},{2,14},{3,15},{4,0},{5,1},{6,2},{7,3},{8,4},{9,5},{1... | collective-permute-start | bytes 491528 | tf_op jit(solution)/shard_map/ppermute | solution.py:32
  207.6 9.5 %collective-permute-start.48 = (f32[256,256]{1,0:T(8,128)S(1)}, f32[256,256]{1,0:T(8,128)S(1)}, u32[]{:S(2)}, u32[]{:S(2)}) collective-permute-start(f32[256,256]{1,0:T(8,128)S(1)} %get-tuple-element.14), channel_id=1, source_target_pairs={{0,64},{1,65},{2,66},{3,67},{4,68},{5,69},{6,70},{7,71},{8,72},{9,... | collective-permute-start | bytes 786440 | tf_op jit(solution)/shard_map/ppermute | solution.py:32
  207.7 11.7 %collective-permute-start.49 = (f32[256,256]{1,0:T(8,128)S(1)}, f32[256,256]{1,0:T(8,128)S(1)}, u32[]{:S(2)}, u32[]{:S(2)}) collective-permute-start(f32[256,256]{1,0:T(8,128)S(1)} %get-tuple-element.15), channel_id=1, source_target_pairs={{0,128},{1,129},{2,130},{3,131},{4,132},{5,133},{6,134},{7,135},{8... | collective-permute-start | bytes 786440 | tf_op jit(solution)/shard_map/ppermute | solution.py:32
  208.7 13.0 %collective-permute-start.50 = (f32[256,256]{1,0:T(8,128)S(1)}, f32[256,256]{1,0:T(8,128)S(1)}, u32[]{:S(2)}, u32[]{:S(2)}) collective-permute-start(f32[256,256]{1,0:T(8,128)S(1)} %get-tuple-element.16), channel_id=1, source_target_pairs={{0,192},{1,193},{2,194},{3,195},{4,196},{5,197},{6,198},{7,199},{8... | collective-permute-start | bytes 786440 | tf_op jit(solution)/shard_map/ppermute | solution.py:32
  222.1 19.2 %collective-permute-start.51 = (f32[128,128]{1,0:T(8,128)S(1)}, f32[128,128]{1,0:T(8,128)S(1)}, u32[]{:S(2)}, u32[]{:S(2)}) collective-permute-start(f32[128,128]{1,0:T(8,128)S(1)} %bitcast.34), channel_id=1, source_target_pairs={{0,0},{1,16},{2,2},{3,18},{4,4},{5,20},{6,6},{7,22},{8,8},{9,24},{... | collective-permute-start | bytes 196616 | tf_op jit(solution)/shard_map/ppermute | solution.py:32
  239.2 7.7 %collective-permute-start.54 = (f32[128,128]{1,0:T(8,128)S(1)}, f32[128,128]{1,0:T(8,128)S(1)}, u32[]{:S(2)}, u32[]{:S(2)}) collective-permute-start(f32[128,128]{1,0:T(8,128)S(1)} %bitcast.31), channel_id=1, source_target_pairs={{0,33},{1,49},{2,35},{3,51},{4,37},{5,53},{6,39},{7,55},{8,41},{9,... | collective-permute-start | bytes 196616 | tf_op jit(solution)/shard_map/ppermute | solution.py:32
  (25 other events, 376.7 us)

commit v2 on v1

v2 whole, which is shorter than its diff:
```python
import jax
import jax.numpy as jnp
from jax import lax
from jax.experimental import pallas as pl
from jax.experimental.pallas import tpu as pltpu
from jax.sharding import PartitionSpec as P

BR = 64
AXES = ("row", "col")
STEPS = (0, 1, 3, 2)


def flat(y, z, x, h, c):
    return ((y * 4 + z) * 4 + x) * 4 + h * 2 + c


PLACES = [
    (y, z, x, h, c)
    for y in range(4)
    for z in range(4)
    for x in range(4)
    for h in range(2)
    for c in range(2)
]


def move(array, target):
    pairs = []
    for place in PLACES:
        to = target(*place)
        if to is not None:
            pairs.append((flat(*place), flat(*to)))
    return lax.ppermute(array, AXES, pairs)


def shift_y(k):
    return lambda y, z, x, h, c: ((y + k) % 4, z, x, h, c)


def shift_x(k):
    return lambda y, z, x, h, c: (y, z, (x + k) % 4, h, c)


def flip_h(y, z, x, h, c):
    return (y, z, x, 1 - h, c)


def flip_c(y, z, x, h, c):
    return (y, z, x, h, 1 - c)


def swap_zc(y, z, x, h, c):
    return (y, (z // 2) * 2 + c, x, h, z % 2)


def cross_zc(y, z, x, h, c):
    return (y, (z // 2) * 2 + c, x, 1 - h, z % 2)


def flip_z0(y, z, x, h, c):
    return (y, z ^ 1, x, h, c) if c != z % 2 else None


def after(arrays, *others):
    return lax.optimization_barrier(tuple(arrays) + others)[: len(arrays)]


def scatter_z(s):
    return lambda y, z, x, h, c: (y, (z // 2 ^ s // 2) * 2 + c, x, h, z % 2 ^ s % 2)


def flip_z1(y, z, x, h, c):
    return (y, z ^ 2, x, h, c)


def apply_kernel(place, *refs):
    p_refs = refs[:8]
    a_refs = refs[8:16]
    out = refs[16]
    panel, left, last, ends, numbers, offsets, sems = refs[17:]
    y, z, x, h, c = (place[i] for i in range(5))
    copies = []

    def start(src, dst):
        copy = pltpu.make_async_copy(src, dst, sems.at[len(copies)])
        copy.start()
        copies.append(copy)

    for f in range(2):
        for i in range(4):
            start(a_refs[4 * f + i].at[pl.ds(1280, 16)], ends.at[2 * i + f])
    for i, k in enumerate(STEPS):
        jx = lax.rem(y + 4 - k, 4)
        for s in range(4):
            j1, l0 = lax.rem(z // 2 + s % 2, 2), lax.rem(c + s // 2, 2)
            src = p_refs[4 * (s // 2) + i].at[pl.ds((s % 2) * 1280, 1280)]
            start(src, panel.at[l0, pl.ds(pl.multiple_of((jx * 2 + j1) * 1280, 1280), 1280)])
        start(a_refs[i].at[pl.ds(1296, 320)], last.at[i])
        for f in range(2):
            start(a_refs[4 * f + i].at[pl.ds(0, 1280)], left.at[2 * i + f])

    for copy in copies[:8]:
        copy.wait()
    for slot in range(8):
        numbers[pl.ds(slot, 1), :] = ends[slot][:1, :128].astype(jnp.float32).astype(jnp.int32)
    scalars = pltpu.make_async_copy(numbers, offsets, sems.at[len(copies)])
    scalars.start()
    for copy in copies[8:] + [scalars]:
        copy.wait()

    step = lax.rem(x + 4 - y, 4)
    step = jnp.where(step > 1, 5 - step, step)
    own = step * 2 + lax.rem(h + z // 2, 2)
    bases = []
    for slot in range(8):
        jx = lax.rem(x + 4 - STEPS[slot // 2], 4)
        bases.append((jx * 2 + lax.rem(h + slot % 2, 2)) * 1280)
    own_base = (y * 2 + z // 2) * 1280

    def block(base, slot, at):
        rows = pl.ds(pl.multiple_of(base + offsets[slot, at] * BR, BR), BR)
        return jnp.concatenate([panel[0, rows, :], panel[1, rows, :]], axis=1)

    @pl.loop(0, 20)
    def _(t):
        rows = pl.ds(pl.multiple_of(t * BR, BR), BR)
        fifth = block(own_base, own, t * 5 + 4)
        nothing = jnp.zeros_like(fifth)
        right = jnp.concatenate([jnp.where(t // 5 == q, fifth, nothing) for q in range(4)], axis=0)
        total = jnp.dot(
            last[step, pl.ds(pl.multiple_of(lax.rem(t, 5) * BR, BR), BR), :],
            right,
            preferred_element_type=jnp.float32,
        )
        for slot in range(8):
            blocks = [block(bases[slot], slot, t * 5 + s) for s in range(4)]
            right = jnp.concatenate(blocks, axis=0)
            total += jnp.dot(left[slot, rows, :], right, preferred_element_type=jnp.float32)
        out[rows, :] = total


def apply_panel(place, p_pieces, a_pieces):
    anywhere = pl.BlockSpec(memory_space=pl.ANY)
    return pl.pallas_call(
        apply_kernel,
        out_shape=jax.ShapeDtypeStruct((1280, 256), jnp.float32),
        grid_spec=pltpu.PrefetchScalarGridSpec(
            num_scalar_prefetch=1,
            grid=(),
            in_specs=[anywhere] * 16,
            out_specs=pl.BlockSpec(memory_space=pltpu.VMEM),
            scratch_shapes=[
                pltpu.VMEM((2, 8 * 1280, 128), jnp.bfloat16),
                pltpu.VMEM((8, 1280, 256), jnp.bfloat16),
                pltpu.VMEM((4, 320, 256), jnp.bfloat16),
                pltpu.VMEM((8, 16, 256), jnp.bfloat16),
                pltpu.VMEM((8, 128), jnp.int32),
                pltpu.SMEM((8, 128), jnp.int32),
                pltpu.SemaphoreType.DMA((37,)),
            ],
        ),
        compiler_params=pltpu.CompilerParams(vmem_limit_bytes=56 * 2**20),
        cost_estimate=pl.CostEstimate(
            flops=2 * 1280 * 2048 * 256, bytes_accessed=12 * 2**20, transcendentals=0
        ),
        name="apply_panel",
    )(place, *p_pieces, *a_pieces)


def project_kernel(place, *refs):
    t_refs = refs[:8]
    prol = refs[8]
    outs = refs[9:13]
    left, sems = refs[13:]
    y, x, h = place[0], place[2], place[3]
    copies = []
    for i, k in enumerate(STEPS):
        m = lax.rem(x + 8 - k - y, 4)
        for f in range(2):
            src, dst = t_refs[4 * f + i], left.at[m, lax.rem(h + f, 2)]
            copy = pltpu.make_async_copy(src, dst, sems.at[2 * i + f])
            copy.start()
            copies.append(copy)
    for copy in copies:
        copy.wait()
    for m in range(4):
        for k1 in range(2):
            total = jnp.zeros((128, 256), jnp.float32)
            for i in range(5):
                total += jnp.dot(
                    left[m, k1, pl.ds(i * 128, 128), :],
                    prol[pl.ds(i * 256, 256), :],
                    preferred_element_type=jnp.float32,
                )
            outs[m][pl.ds(k1 * 128, 128), :] = total


def project(place, t_pieces, prol):
    anywhere = pl.BlockSpec(memory_space=pl.ANY)
    inside = pl.BlockSpec(memory_space=pltpu.VMEM)
    out = jax.ShapeDtypeStruct((256, 256), jnp.float32)
    return pl.pallas_call(
        project_kernel,
        out_shape=(out,) * 4,
        grid_spec=pltpu.PrefetchScalarGridSpec(
            num_scalar_prefetch=1,
            grid=(),
            in_specs=[anywhere] * 8 + [inside],
            out_specs=(inside,) * 4,
            scratch_shapes=[
                pltpu.VMEM((4, 2, 640, 256), jnp.bfloat16),
                pltpu.SemaphoreType.DMA((8,)),
            ],
        ),
        compiler_params=pltpu.CompilerParams(vmem_limit_bytes=32 * 2**20),
        cost_estimate=pl.CostEstimate(
            flops=2 * 1280 * 1024 * 256, bytes_accessed=4 * 2**20, transcendentals=0
        ),
        name="project",
    )(place, *t_pieces, prol)


def per_device(a_vals, a_cols, a_count, p_vals, p_mask):
    row, col = lax.axis_index("row"), lax.axis_index("col")
    y, z = row // 4, row % 4
    x, h, c = col // 4, (col // 2) % 2, col % 2
    place = jnp.stack([y, z, x, h, c]).astype(jnp.int32)

    p_live = p_vals * p_mask[:, :, None].astype(jnp.bfloat16)
    p_flat = p_live.reshape(1280, 128)
    p_own = jnp.concatenate([p_flat, move(p_flat, flip_z1)])
    p_twin = move(p_own, flip_c)

    live = jnp.arange(5, dtype=jnp.int32)[None, :] < a_count
    masked = jnp.where(live[:, :, None], a_vals, jnp.zeros_like(a_vals))
    slots = masked.reshape(20, 5, BR, BR)
    four = slots[:, :4].transpose(0, 2, 1, 3).reshape(1280, 256)
    offsets = jnp.clip(a_cols - col * 20, 0, 19).astype(jnp.bfloat16).reshape(1, 100)
    four = jnp.concatenate([four, jnp.pad(offsets, ((0, 15), (0, 156)))])
    swapped = move(four, swap_zc)

    def across(y, z, x, h, c):
        return (y, z, x, 1 - h, c) if h == z // 2 and x == y and c == z % 2 else None

    five = slots[:, 4].reshape(4, 320, BR)
    five = jnp.concatenate([five[q] for q in range(4)], axis=1)
    five = five + move(five, across)

    p_own, p_twin, swapped, four, five = after((p_own, p_twin, swapped, four, five))
    near = jnp.concatenate([swapped, five])
    far = move(four, cross_zc)
    a_near = [near] + [move(near, shift_x(k)) for k in (1, 3, 2)]
    p_mine = [p_own, move(p_own, shift_y(1))]
    far, p_own = after((far, p_own), *p_mine, *a_near)
    a_far = [far] + [move(far, shift_x(k)) for k in (1, 3, 2)]
    p_mine += [move(p_own, shift_y(k)) for k in (3, 2)]
    p_other = [p_twin] + [move(piece, flip_c) for piece in p_mine[1:]]

    t_own = p_flat.reshape(5, 256, 128).transpose(0, 2, 1).reshape(640, 256)
    (t_own,) = after((t_own,), *a_far, *p_other)
    t_far = move(t_own, flip_h)
    t_near = [t_own] + [move(t_own, shift_x(k)) for k in (1, 3, 2)]
    product = apply_panel(place, p_mine + p_other, a_near + a_far)
    product, t_far = after((product, t_far), *t_near)
    t_far = [t_far] + [move(t_far, shift_x(k)) for k in (1, 3, 2)]
    prolonged = (product + move(product, flip_z0)).astype(jnp.bfloat16)
    (prolonged,) = after((prolonged,), *t_near, *t_far)
    prolonged = jnp.where(c == z % 2, prolonged, move(prolonged, flip_c))

    blocks = project(place, t_near + t_far, prolonged)
    summed = blocks[0]
    for m in (1, 2, 3):
        summed = summed + move(blocks[m], shift_y(m))
    parts = summed.reshape(2, 128, 2, 128)
    total = None
    for s in range(4):
        k1 = (z // 2 + s // 2) % 2
        l0 = (z + s) % 2
        part = lax.dynamic_slice(parts, (k1, 0, l0, 0), (1, 128, 1, 128)).reshape(128, 128)
        got = move(part, scatter_z(s))
        total = got if total is None else total + got
    return total


def solution(mesh):
    placed = (
        P("row", "col", None),
        P("row", "col"),
        P("row", "col"),
        P("row", None, "col"),
        P("row", "col"),
    )
    return jax.shard_map(
        per_device, mesh=mesh, in_specs=placed, out_specs=P("row", "col"), check_vma=False
    )
```

time: 253 us -> 185 us (0.73); the launches traced: 248 us -> 185 us
  starting transfers between devices: 125 us -> 72.5 us
  local copies, waits for them, and re-layouts: 18.2 us -> 8.51 us
  waiting for transfers between devices: 81.7 us -> 79 us
    ppermute x55 -> x33, starting transfers between devices: 125 us -> 72.5 us  [move(): return lax.ppermute(array, AXES, pairs)]
    slice x17 -> x1, local copies, waits for them, and re-layouts: 10.2 us -> 0.02 us  [per_device(): five = jnp.concatenate([five[q] for q in range(4)], axis=1)]
    ppermute x55 -> x33, waiting for transfers between devices: 81.7 us -> 79 us  [move(): return lax.ppermute(array, AXES, pairs)]
  transfers between devices with their start and end apart: 55 -> 33, of which waited for: 19 -> 16; matrix products, arithmetic and copies ran while one was open for 9% -> 7% of each run, Pallas kernels for 5% -> 7%
where the time goes in v2:
time: 185 us
  waiting for transfers between devices  79 us (43%)
  starting transfers between devices  72.5 us (39%)
  Pallas kernels  16.1 us (9%)
  local copies, waits for them, and re-layouts  8.51 us (5%)
  other arithmetic  8.43 us (5%)
    ppermute x33, waiting for transfers between devices, move(): return lax.ppermute(array, AXES, pairs)  79 us
    ppermute x33, starting transfers between devices, move(): return lax.ppermute(array, AXES, pairs)  72.5 us
    pallas_call x1, Pallas kernels, apply_panel(): pl.pallas_call(apply_kernel, out_shape=jax.ShapeDtypeStruct((1280, 256),...  13.2 us
  transfers between devices with their start and end apart: 33, of which 16 were waited for; matrix products, arithmetic and copies ran while one was open for 7% of the time, Pallas kernels for 7%

profile of v2, /device:TPU:1, one launch (start us, length us, event | category | flops | bytes accessed | tf_op | source)
XLA Modules:
  0.0 184.9 jit_solution(15646977362622417599)
XLA Ops:
  0.7 1.1 broadcast_multiply_fusion
  1.7 3.9 %collective-permute-start = (bf16[1280,128]{1,0:T(8,128)(2,1)S(1)}, bf16[1280,128]{1,0:T(8,128)(2,1)}, u32[]{:S(2)}, u32[]{:S(2)}) collective-permute-start(bf16[1280,128]{1,0:T(8,128)(2,1)S(1)} %bitcast.30), channel_id=1, source_target_pairs={{0,32},{1,33},{2,34},{3,35},{4,36},{5,37},{6,38},{7,39},{8,40},{9,... | collective-permute-start | bytes 983048 | tf_op jit(solution)/shard_map/ppermute | solution.py:33
  6.3 1.3 broadcast_select_fusion
  7.6 1.7 reshape.70
  10.3 2.3 %copy.10 = bf16[20,64,4,64]{3,2,1,0:T(4,128)(2,1)} copy(bf16[20,64,4,64]{3,1,0,2:T(8,128)(2,1)S(1)} %slice_bitcast_fusion) | data formatting | bytes 1310720 | tf_op jit(solution)/shard_map/transpose | solution.py:237
  12.5 2.3 %reshape.71 = bf16[1280,256]{1,0:T(8,128)(2,1)S(1)} reshape(bf16[20,64,4,64]{3,2,1,0:T(4,128)(2,1)} %copy.10) | data formatting | bytes 1310720 | tf_op jit(solution)/shard_map/reshape | solution.py:237
  14.9 4.4 %collective-permute-start.2 = (bf16[1296,256]{1,0:T(8,128)(2,1)S(1)}, bf16[1296,256]{1,0:T(8,128)(2,1)S(1)}, u32[]{:S(2)}, u32[]{:S(2)}) collective-permute-start(bf16[1296,256]{1,0:T(8,128)(2,1)S(1)} %fusion.1), channel_id=1, source_target_pairs={{0,0},{1,16},{2,2},{3,18},{4,4},{5,20},{6,6},{7,22},{8,8},{9,24},{... | collective-permute-start | bytes 1990664 | tf_op jit(solution)/shard_map/ppermute | solution.py:33
  19.5 1.0 pad_maximum_fusion.refs_0_
  20.5 2.0 %collective-permute-start.1 = (bf16[2560,128]{1,0:T(8,128)(2,1)S(1)}, bf16[2560,128]{1,0:T(8,128)(2,1)}, u32[]{:S(2)}, u32[]{:S(2)}) collective-permute-start(bf16[2560,128]{1,0:T(8,128)(2,1)S(1)} %pad_maximum_fusion.refs_0_), channel_id=1, source_target_pairs={{0,1},{1,0},{2,3},{3,2},{4,5},{5,4},{6,7},{7,6},{8,9},{9,8},{10,11... | collective-permute-start | bytes 1966088 | tf_op jit(solution)/shard_map/ppermute | solution.py:33
  23.6 4.2 %collective-permute-done.2 = bf16[1296,256]{1,0:T(8,128)(2,1)S(1)} collective-permute-done((bf16[1296,256]{1,0:T(8,128)(2,1)S(1)}, bf16[1296,256]{1,0:T(8,128)(2,1)S(1)}, u32[]{:S(2)}, u32[]{:S(2)}) %collective-permute-start.2) | collective-permute-done | bytes 663584 | tf_op jit(solution)/shard_map/ppermute | solution.py:33
  27.8 1.3 collective-permute-start.6
  29.1 1.5 collective-permute-start.7
  30.6 1.5 collective-permute-start.8
  32.1 5.8 %collective-permute-start.4 = (bf16[1296,256]{1,0:T(8,128)(2,1)S(1)}, bf16[1296,256]{1,0:T(8,128)(2,1)S(1)}, u32[]{:S(2)}, u32[]{:S(2)}) collective-permute-start(bf16[1296,256]{1,0:T(8,128)(2,1)S(1)} %fusion.1), channel_id=1, source_target_pairs={{0,2},{1,18},{2,0},{3,16},{4,6},{5,22},{6,4},{7,20},{8,10},{9,26},... | collective-permute-start | bytes 1990664 | tf_op jit(solution)/shard_map/ppermute | solution.py:33
  37.9 1.3 collective-permute-start.5
  39.2 9.7 %collective-permute-done.5.refs_1_ = bf16[2560,128]{1,0:T(8,128)(2,1)S(1)} collective-permute-done((bf16[2560,128]{1,0:T(8,128)(2,1)S(1)}, bf16[2560,128]{1,0:T(8,128)(2,1)S(1)}, u32[]{:S(2)}, u32[]{:S(2)}) %collective-permute-start.5) | collective-permute-done | bytes 655392 | tf_op jit(solution)/shard_map/ppermute | solution.py:33
  48.9 7.8 %collective-permute-start.12 = (bf16[2560,128]{1,0:T(8,128)(2,1)S(1)}, bf16[2560,128]{1,0:T(8,128)(2,1)S(1)}, u32[]{:S(2)}, u32[]{:S(2)}) collective-permute-start(bf16[2560,128]{1,0:T(8,128)(2,1)S(1)} %collective-permute-done.5.refs_1_), channel_id=1, source_target_pairs={{0,1},{1,0},{2,3},{3,2},{4,5},{5,4},{6,7},{7,6},{8,9},{9,8},{10,11... | collective-permute-start | bytes 1966088 | tf_op jit(solution)/shard_map/ppermute | solution.py:33
  56.7 5.3 %collective-permute-done.4.refs_12_ = bf16[1296,256]{1,0:T(8,128)(2,1)S(1)} collective-permute-done((bf16[1296,256]{1,0:T(8,128)(2,1)S(1)}, bf16[1296,256]{1,0:T(8,128)(2,1)S(1)}, u32[]{:S(2)}, u32[]{:S(2)}) %collective-permute-start.4) | collective-permute-done | bytes 663584 | tf_op jit(solution)/shard_map/ppermute | solution.py:33
  62.0 3.6 %collective-permute-done.8.refs_11_ = bf16[1616,256]{1,0:T(8,128)(2,1)S(1)} collective-permute-done((bf16[1616,256]{1,0:T(8,128)(2,1)S(1)}, bf16[1616,256]{1,0:T(8,128)(2,1)S(1)}, u32[]{:S(2)}, u32[]{:S(2)}) %collective-permute-start.8) | collective-permute-done | bytes 827424 | tf_op jit(solution)/shard_map/ppermute | solution.py:33
  65.6 3.0 %collective-permute-start.15 = (bf16[2560,128]{1,0:T(8,128)(2,1)S(1)}, bf16[2560,128]{1,0:T(8,128)(2,1)}, u32[]{:S(2)}, u32[]{:S(2)}) collective-permute-start(bf16[2560,128]{1,0:T(8,128)(2,1)S(1)} %pad_maximum_fusion.refs_0_), channel_id=1, source_target_pairs={{0,128},{1,129},{2,130},{3,131},{4,132},{5,133},{6,134},{7,135},{8... | collective-permute-start | bytes 1966088 | tf_op jit(solution)/shard_map/ppermute | solution.py:33
  68.6 1.5 collective-permute-start.10
  70.0 1.6 collective-permute-start.11
  71.6 8.1 %collective-permute-done.13.refs_2_ = bf16[2560,128]{1,0:T(8,128)(2,1)} collective-permute-done((bf16[2560,128]{1,0:T(8,128)(2,1)S(1)}, bf16[2560,128]{1,0:T(8,128)(2,1)}, u32[]{:S(2)}, u32[]{:S(2)}) %collective-permute-start.13) | collective-permute-done | bytes 655392 | tf_op jit(solution)/shard_map/ppermute | solution.py:33
  79.7 5.9 %collective-permute-start.14 = (bf16[2560,128]{1,0:T(8,128)(2,1)}, bf16[2560,128]{1,0:T(8,128)(2,1)}, u32[]{:S(2)}, u32[]{:S(2)}) collective-permute-start(bf16[2560,128]{1,0:T(8,128)(2,1)} %collective-permute-done.13.refs_2_), channel_id=1, source_target_pairs={{0,1},{1,0},{2,3},{3,2},{4,5},{5,4},{6,7},{7,6},{8,9},{9,8},{10,11... | collective-permute-start | bytes 1966088 | tf_op jit(solution)/shard_map/ppermute | solution.py:33
  85.8 16.9 %collective-permute-done.9.refs_13_ = bf16[1296,256]{1,0:T(8,128)(2,1)} collective-permute-done((bf16[1296,256]{1,0:T(8,128)(2,1)S(1)}, bf16[1296,256]{1,0:T(8,128)(2,1)}, u32[]{:S(2)}, u32[]{:S(2)}) %collective-permute-start.9) | collective-permute-done | bytes 663584 | tf_op jit(solution)/shard_map/ppermute | solution.py:33
  102.8 2.7 %collective-permute-start.18 = (bf16[640,256]{1,0:T(8,128)(2,1)S(1)}, bf16[640,256]{1,0:T(8,128)(2,1)S(1)}, u32[]{:S(2)}, u32[]{:S(2)}) collective-permute-start(bf16[640,256]{1,0:T(8,128)(2,1)S(1)} %bitcast.26), channel_id=1, source_target_pairs={{0,12},{1,13},{2,14},{3,15},{4,0},{5,1},{6,2},{7,3},{8,4},{9,5},{1... | collective-permute-start | bytes 983048 | tf_op jit(solution)/shard_map/ppermute | solution.py:33
  105.6 6.9 %collective-permute-start.20 = (bf16[640,256]{1,0:T(8,128)(2,1)S(1)}, bf16[640,256]{1,0:T(8,128)(2,1)S(1)}, u32[]{:S(2)}, u32[]{:S(2)}) collective-permute-start(bf16[640,256]{1,0:T(8,128)(2,1)S(1)} %bitcast.28), channel_id=1, source_target_pairs={{0,2},{1,3},{2,0},{3,1},{4,6},{5,7},{6,4},{7,5},{8,10},{9,11},{10,... | collective-permute-start | bytes 983048 | tf_op jit(solution)/shard_map/ppermute | solution.py:33
  113.2 13.2 %apply_panel.1 = f32[1280,256]{1,0:T(8,128)} custom-call(s32[5]{0:T(128)} %stack.23.place, bf16[2560,128]{1,0:T(8,128)(2,1)} %copy-done.2, bf16[2560,128]{1,0:T(8,128)(2,1)} %copy-done.7, bf16[2560,128]{1,0:T(8,128)(2,1)} %collective-permute-done.13.refs_2_, bf16[2560,128]{1,0:T(8,128)(2,1)} %collective-permute-done.15.refs_3_, ...), custom_call_target="tpu_custom_call" | custom-call | flops 1342177280 | bytes 12582912 | tf_op jit(solution)/shard_map/apply_panel/pallas_call | solution.py:144
  126.4 3.6 %collective-permute-start.24 = (f32[1280,256]{1,0:T(8,128)}, f32[1280,256]{1,0:T(8,128)S(1)}, u32[]{:S(2)}, u32[]{:S(2)}) collective-permute-start(f32[1280,256]{1,0:T(8,128)} %apply_panel.1), channel_id=1, source_target_pairs={{1,17},{3,19},{5,21},{7,23},{9,25},{11,27},{13,29},{15,31},{16,0},... | collective-permute-start | bytes 3932168 | tf_op jit(solution)/shard_map/ppermute | solution.py:33
  130.3 2.5 %collective-permute-start.22 = (bf16[640,256]{1,0:T(8,128)(2,1)S(1)}, bf16[640,256]{1,0:T(8,128)(2,1)S(1)}, u32[]{:S(2)}, u32[]{:S(2)}) collective-permute-start(bf16[640,256]{1,0:T(8,128)(2,1)S(1)} %collective-permute-done.20.refs_4_), channel_id=1, source_target_pairs={{0,12},{1,13},{2,14},{3,15},{4,0},{5,1},{6,2},{7,3},{8,4},{9,5},{1... | collective-permute-start | bytes 983048 | tf_op jit(solution)/shard_map/ppermute | solution.py:33
  132.8 1.3 collective-permute-start.23
  134.1 10.7 %collective-permute-done.24 = f32[1280,256]{1,0:T(8,128)S(1)} collective-permute-done((f32[1280,256]{1,0:T(8,128)}, f32[1280,256]{1,0:T(8,128)S(1)}, u32[]{:S(2)}, u32[]{:S(2)}) %collective-permute-start.24) | collective-permute-done | bytes 1310752 | tf_op jit(solution)/shard_map/ppermute | solution.py:33
  144.8 1.5 add_convert_fusion
  146.3 0.8 collective-permute-done.22.refs_6_
  147.6 1.8 collective-permute-start.25
  149.4 1.9 %collective-permute-done.25 = bf16[1280,256]{1,0:T(8,128)(2,1)} collective-permute-done((bf16[1280,256]{1,0:T(8,128)(2,1)S(1)}, bf16[1280,256]{1,0:T(8,128)(2,1)}, u32[]{:S(2)}, u32[]{:S(2)}) %collective-permute-start.25) | collective-permute-done | bytes 655392 | tf_op jit(solution)/shard_map/ppermute | solution.py:33
  151.3 1.2 broadcast_select_fusion.1.refs_8_
  152.4 2.9 %project.1 = (f32[256,256]{1,0:T(8,128)S(1)}, f32[256,256]{1,0:T(8,128)}, f32[256,256]{1,0:T(8,128)S(1)}, f32[256,256]{1,0:T(8,128)S(1)}) custom-call(s32[5]{0:T(128)S(1)} %copy-done, bf16[640,256]{1,0:T(8,128)(2,1)S(1)} %bitcast.29, bf16[640,256]{1,0:T(8,128)(2,1)S(1)} %collective-permute-done.17.refs_1_, ...), custom_call_target="tpu_custom_call" | custom-call | flops 671088640 | bytes 4194304 | tf_op jit(solution)/shard_map/project/pallas_call | solution.py:202
  155.4 0.8 collective-permute-start.26
  156.2 2.0 %collective-permute-start.27 = (f32[256,256]{1,0:T(8,128)S(1)}, f32[256,256]{1,0:T(8,128)S(1)}, u32[]{:S(2)}, u32[]{:S(2)}) collective-permute-start(f32[256,256]{1,0:T(8,128)S(1)} %get-tuple-element.33), channel_id=1, source_target_pairs={{0,128},{1,129},{2,130},{3,131},{4,132},{5,133},{6,134},{7,135},{8... | collective-permute-start | bytes 786440 | tf_op jit(solution)/shard_map/ppermute | solution.py:33
  158.2 1.6 collective-permute-start.28
  159.8 5.2 %collective-permute-done.26 = f32[256,256]{1,0:T(8,128)S(1)} collective-permute-done((f32[256,256]{1,0:T(8,128)}, f32[256,256]{1,0:T(8,128)S(1)}, u32[]{:S(2)}, u32[]{:S(2)}) %collective-permute-start.26) | collective-permute-done | bytes 262176 | tf_op jit(solution)/shard_map/ppermute | solution.py:33
  165.0 5.3 %collective-permute-done.27 = f32[256,256]{1,0:T(8,128)S(1)} collective-permute-done((f32[256,256]{1,0:T(8,128)S(1)}, f32[256,256]{1,0:T(8,128)S(1)}, u32[]{:S(2)}, u32[]{:S(2)}) %collective-permute-start.27) | collective-permute-done | bytes 262176 | tf_op jit(solution)/shard_map/ppermute | solution.py:33
  170.4 0.8 collective-permute-done.28
  171.6 1.9 %collective-permute-start.29 = (f32[128,128]{1,0:T(8,128)S(1)}, f32[128,128]{1,0:T(8,128)S(1)}, u32[]{:S(2)}, u32[]{:S(2)}) collective-permute-start(f32[128,128]{1,0:T(8,128)S(1)} %bitcast.44), channel_id=1, source_target_pairs={{0,0},{1,16},{2,2},{3,18},{4,4},{5,20},{6,6},{7,22},{8,8},{9,24},{... | collective-permute-start | bytes 196616 | tf_op jit(solution)/shard_map/ppermute | solution.py:33
  173.7 4.7 %collective-permute-start.31 = (f32[128,128]{1,0:T(8,128)S(1)}, f32[128,128]{1,0:T(8,128)S(1)}, u32[]{:S(2)}, u32[]{:S(2)}) collective-permute-start(f32[128,128]{1,0:T(8,128)S(1)} %bitcast.42), channel_id=1, source_target_pairs={{0,32},{1,48},{2,34},{3,50},{4,36},{5,52},{6,38},{7,54},{8,40},{9,... | collective-permute-start | bytes 196616 | tf_op jit(solution)/shard_map/ppermute | solution.py:33
  178.5 4.5 %collective-permute-done.31 = f32[128,128]{1,0:T(8,128)S(1)} collective-permute-done((f32[128,128]{1,0:T(8,128)S(1)}, f32[128,128]{1,0:T(8,128)S(1)}, u32[]{:S(2)}, u32[]{:S(2)}) %collective-permute-start.31) | collective-permute-done | bytes 65568 | tf_op jit(solution)/shard_map/ppermute | solution.py:33
  183.0 1.3 collective-permute-done.32
  (66 shorter events, 6.6 us)
Async XLA Ops:
  1.7 17.8 %collective-permute-start = (bf16[1280,128]{1,0:T(8,128)(2,1)S(1)}, bf16[1280,128]{1,0:T(8,128)(2,1)}, u32[]{:S(2)}, u32[]{:S(2)}) collective-permute-start(bf16[1280,128]{1,0:T(8,128)(2,1)S(1)} %bitcast.30), channel_id=1, source_target_pairs={{0,32},{1,33},{2,34},{3,35},{4,36},{5,37},{6,38},{7,39},{8,40},{9,... | collective-permute-start | bytes 983048 | tf_op jit(solution)/shard_map/ppermute | solution.py:33
  9.4 0.7 copy-start.9
  14.9 12.8 %collective-permute-start.2 = (bf16[1296,256]{1,0:T(8,128)(2,1)S(1)}, bf16[1296,256]{1,0:T(8,128)(2,1)S(1)}, u32[]{:S(2)}, u32[]{:S(2)}) collective-permute-start(bf16[1296,256]{1,0:T(8,128)(2,1)S(1)} %fusion.1), channel_id=1, source_target_pairs={{0,0},{1,16},{2,2},{3,18},{4,4},{5,20},{6,6},{7,22},{8,8},{9,24},{... | collective-permute-start | bytes 1990664 | tf_op jit(solution)/shard_map/ppermute | solution.py:33
  20.5 45.0 %copy-start.2 = (bf16[2560,128]{1,0:T(8,128)(2,1)}, bf16[2560,128]{1,0:T(8,128)(2,1)S(1)}, u32[]{:S(2)}) copy-start(bf16[2560,128]{1,0:T(8,128)(2,1)S(1)} %pad_maximum_fusion.refs_0_) | copy-start | bytes 1966084
  20.5 7.2 %collective-permute-start.1 = (bf16[2560,128]{1,0:T(8,128)(2,1)S(1)}, bf16[2560,128]{1,0:T(8,128)(2,1)}, u32[]{:S(2)}, u32[]{:S(2)}) collective-permute-start(bf16[2560,128]{1,0:T(8,128)(2,1)S(1)} %pad_maximum_fusion.refs_0_), channel_id=1, source_target_pairs={{0,1},{1,0},{2,3},{3,2},{4,5},{5,4},{6,7},{7,6},{8,9},{9,8},{10,11... | collective-permute-start | bytes 1966088 | tf_op jit(solution)/shard_map/ppermute | solution.py:33
  22.7 0.7 collective-permute-start.3
  27.8 85.4 %copy-start.1 = (bf16[1616,256]{1,0:T(8,128)(2,1)}, bf16[1616,256]{1,0:T(8,128)(2,1)S(1)}, u32[]{:S(2)}) copy-start(bf16[1616,256]{1,0:T(8,128)(2,1)S(1)} %constant_dynamic-update-slice_fusion.refs_8_) | copy-start | bytes 2482180
  27.8 34.1 %collective-permute-start.6 = (bf16[1616,256]{1,0:T(8,128)(2,1)S(1)}, bf16[1616,256]{1,0:T(8,128)(2,1)S(1)}, u32[]{:S(2)}, u32[]{:S(2)}) collective-permute-start(bf16[1616,256]{1,0:T(8,128)(2,1)S(1)} %constant_dynamic-update-slice_fusion.refs_8_), channel_id=1, source_target_pairs={{0,4},{1,5},{2,6},{3,7},{4,8},{5,9},{6,10},{7,11},{8,12},{9,13},{1... | collective-permute-start | bytes 2482184 | tf_op jit(solution)/shard_map/ppermute | solution.py:33
  29.1 32.8 %collective-permute-start.7 = (bf16[1616,256]{1,0:T(8,128)(2,1)S(1)}, bf16[1616,256]{1,0:T(8,128)(2,1)S(1)}, u32[]{:S(2)}, u32[]{:S(2)}) collective-permute-start(bf16[1616,256]{1,0:T(8,128)(2,1)S(1)} %constant_dynamic-update-slice_fusion.refs_8_), channel_id=1, source_target_pairs={{0,12},{1,13},{2,14},{3,15},{4,0},{5,1},{6,2},{7,3},{8,4},{9,5},{1... | collective-permute-start | bytes 2482184 | tf_op jit(solution)/shard_map/ppermute | solution.py:33
  30.6 35.0 %collective-permute-start.8 = (bf16[1616,256]{1,0:T(8,128)(2,1)S(1)}, bf16[1616,256]{1,0:T(8,128)(2,1)S(1)}, u32[]{:S(2)}, u32[]{:S(2)}) collective-permute-start(bf16[1616,256]{1,0:T(8,128)(2,1)S(1)} %constant_dynamic-update-slice_fusion.refs_8_), channel_id=1, source_target_pairs={{0,8},{1,9},{2,10},{3,11},{4,12},{5,13},{6,14},{7,15},{8,0},{9,1},... | collective-permute-start | bytes 2482184 | tf_op jit(solution)/shard_map/ppermute | solution.py:33
  32.1 29.8 %collective-permute-start.4 = (bf16[1296,256]{1,0:T(8,128)(2,1)S(1)}, bf16[1296,256]{1,0:T(8,128)(2,1)S(1)}, u32[]{:S(2)}, u32[]{:S(2)}) collective-permute-start(bf16[1296,256]{1,0:T(8,128)(2,1)S(1)} %fusion.1), channel_id=1, source_target_pairs={{0,2},{1,18},{2,0},{3,16},{4,6},{5,22},{6,4},{7,20},{8,10},{9,26},... | collective-permute-start | bytes 1990664 | tf_op jit(solution)/shard_map/ppermute | solution.py:33
  37.9 11.0 %collective-permute-start.5 = (bf16[2560,128]{1,0:T(8,128)(2,1)S(1)}, bf16[2560,128]{1,0:T(8,128)(2,1)S(1)}, u32[]{:S(2)}, u32[]{:S(2)}) collective-permute-start(bf16[2560,128]{1,0:T(8,128)(2,1)S(1)} %pad_maximum_fusion.refs_0_), channel_id=1, source_target_pairs={{0,64},{1,65},{2,66},{3,67},{4,68},{5,69},{6,70},{7,71},{8,72},{9,... | collective-permute-start | bytes 1966088 | tf_op jit(solution)/shard_map/ppermute | solution.py:33
  48.9 36.7 %copy-start.7 = (bf16[2560,128]{1,0:T(8,128)(2,1)}, bf16[2560,128]{1,0:T(8,128)(2,1)S(1)}, u32[]{:S(2)}) copy-start(bf16[2560,128]{1,0:T(8,128)(2,1)S(1)} %collective-permute-done.5.refs_1_) | copy-start | bytes 1966084
  48.9 22.7 %collective-permute-start.12 = (bf16[2560,128]{1,0:T(8,128)(2,1)S(1)}, bf16[2560,128]{1,0:T(8,128)(2,1)S(1)}, u32[]{:S(2)}, u32[]{:S(2)}) collective-permute-start(bf16[2560,128]{1,0:T(8,128)(2,1)S(1)} %collective-permute-done.5.refs_1_), channel_id=1, source_target_pairs={{0,1},{1,0},{2,3},{3,2},{4,5},{5,4},{6,7},{7,6},{8,9},{9,8},{10,11... | collective-permute-start | bytes 1966088 | tf_op jit(solution)/shard_map/ppermute | solution.py:33
  62.0 40.7 %copy-start.6 = (bf16[1296,256]{1,0:T(8,128)(2,1)}, bf16[1296,256]{1,0:T(8,128)(2,1)S(1)}, u32[]{:S(2)}) copy-start(bf16[1296,256]{1,0:T(8,128)(2,1)S(1)} %collective-permute-done.4.refs_12_) | copy-start | bytes 1990660
  62.0 23.6 %copy-start.3 = (bf16[1616,256]{1,0:T(8,128)(2,1)}, bf16[1616,256]{1,0:T(8,128)(2,1)S(1)}, u32[]{:S(2)}) copy-start(bf16[1616,256]{1,0:T(8,128)(2,1)S(1)} %collective-permute-done.6.refs_9_) | copy-start | bytes 2482180
  62.0 23.6 %copy-start.4 = (bf16[1616,256]{1,0:T(8,128)(2,1)}, bf16[1616,256]{1,0:T(8,128)(2,1)S(1)}, u32[]{:S(2)}) copy-start(bf16[1616,256]{1,0:T(8,128)(2,1)S(1)} %collective-permute-done.7.refs_10_) | copy-start | bytes 2482180
  65.6 20.0 %copy-start.5 = (bf16[1616,256]{1,0:T(8,128)(2,1)}, bf16[1616,256]{1,0:T(8,128)(2,1)S(1)}, u32[]{:S(2)}) copy-start(bf16[1616,256]{1,0:T(8,128)(2,1)S(1)} %collective-permute-done.8.refs_11_) | copy-start | bytes 2482180
  65.6 14.1 %collective-permute-start.13 = (bf16[2560,128]{1,0:T(8,128)(2,1)S(1)}, bf16[2560,128]{1,0:T(8,128)(2,1)}, u32[]{:S(2)}, u32[]{:S(2)}) collective-permute-start(bf16[2560,128]{1,0:T(8,128)(2,1)S(1)} %pad_maximum_fusion.refs_0_), channel_id=1, source_target_pairs={{0,192},{1,193},{2,194},{3,195},{4,196},{5,197},{6,198},{7,199},{8... | collective-permute-start | bytes 1966088 | tf_op jit(solution)/shard_map/ppermute | solution.py:33
  65.6 20.0 %collective-permute-start.15 = (bf16[2560,128]{1,0:T(8,128)(2,1)S(1)}, bf16[2560,128]{1,0:T(8,128)(2,1)}, u32[]{:S(2)}, u32[]{:S(2)}) collective-permute-start(bf16[2560,128]{1,0:T(8,128)(2,1)S(1)} %pad_maximum_fusion.refs_0_), channel_id=1, source_target_pairs={{0,128},{1,129},{2,130},{3,131},{4,132},{5,133},{6,134},{7,135},{8... | collective-permute-start | bytes 1966088 | tf_op jit(solution)/shard_map/ppermute | solution.py:33
  68.6 17.2 %collective-permute-start.10 = (bf16[1296,256]{1,0:T(8,128)(2,1)S(1)}, bf16[1296,256]{1,0:T(8,128)(2,1)}, u32[]{:S(2)}, u32[]{:S(2)}) collective-permute-start(bf16[1296,256]{1,0:T(8,128)(2,1)S(1)} %collective-permute-done.4.refs_12_), channel_id=1, source_target_pairs={{0,12},{1,13},{2,14},{3,15},{4,0},{5,1},{6,2},{7,3},{8,4},{9,5},{1... | collective-permute-start | bytes 1990664 | tf_op jit(solution)/shard_map/ppermute | solution.py:33
  70.0 15.8 %collective-permute-start.11 = (bf16[1296,256]{1,0:T(8,128)(2,1)S(1)}, bf16[1296,256]{1,0:T(8,128)(2,1)}, u32[]{:S(2)}, u32[]{:S(2)}) collective-permute-start(bf16[1296,256]{1,0:T(8,128)(2,1)S(1)} %collective-permute-done.4.refs_12_), channel_id=1, source_target_pairs={{0,8},{1,9},{2,10},{3,11},{4,12},{5,13},{6,14},{7,15},{8,0},{9,1},... | collective-permute-start | bytes 1990664 | tf_op jit(solution)/shard_map/ppermute | solution.py:33
  71.6 14.0 %copy-start.8 = (bf16[2560,128]{1,0:T(8,128)(2,1)}, bf16[2560,128]{1,0:T(8,128)(2,1)S(1)}, u32[]{:S(2)}) copy-start(bf16[2560,128]{1,0:T(8,128)(2,1)S(1)} %collective-permute-done.12.refs_5_) | copy-start | bytes 1966084
  71.6 31.1 %collective-permute-start.9 = (bf16[1296,256]{1,0:T(8,128)(2,1)S(1)}, bf16[1296,256]{1,0:T(8,128)(2,1)}, u32[]{:S(2)}, u32[]{:S(2)}) collective-permute-start(bf16[1296,256]{1,0:T(8,128)(2,1)S(1)} %collective-permute-done.4.refs_12_), channel_id=1, source_target_pairs={{0,4},{1,5},{2,6},{3,7},{4,8},{5,9},{6,10},{7,11},{8,12},{9,13},{1... | collective-permute-start | bytes 1990664 | tf_op jit(solution)/shard_map/ppermute | solution.py:33
  79.7 23.0 %collective-permute-start.14 = (bf16[2560,128]{1,0:T(8,128)(2,1)}, bf16[2560,128]{1,0:T(8,128)(2,1)}, u32[]{:S(2)}, u32[]{:S(2)}) collective-permute-start(bf16[2560,128]{1,0:T(8,128)(2,1)} %collective-permute-done.13.refs_2_), channel_id=1, source_target_pairs={{0,1},{1,0},{2,3},{3,2},{4,5},{5,4},{6,7},{7,6},{8,9},{9,8},{10,11... | collective-permute-start | bytes 1966088 | tf_op jit(solution)/shard_map/ppermute | solution.py:33
  85.6 17.1 %collective-permute-start.16 = (bf16[2560,128]{1,0:T(8,128)(2,1)}, bf16[2560,128]{1,0:T(8,128)(2,1)}, u32[]{:S(2)}, u32[]{:S(2)}) collective-permute-start(bf16[2560,128]{1,0:T(8,128)(2,1)} %collective-permute-done.15.refs_3_), channel_id=1, source_target_pairs={{0,1},{1,0},{2,3},{3,2},{4,5},{5,4},{6,7},{7,6},{8,9},{9,8},{10,11... | collective-permute-start | bytes 1966088 | tf_op jit(solution)/shard_map/ppermute | solution.py:33
  102.7 23.7 %collective-permute-start.17 = (bf16[640,256]{1,0:T(8,128)(2,1)S(1)}, bf16[640,256]{1,0:T(8,128)(2,1)S(1)}, u32[]{:S(2)}, u32[]{:S(2)}) collective-permute-start(bf16[640,256]{1,0:T(8,128)(2,1)S(1)} %bitcast.25), channel_id=1, source_target_pairs={{0,4},{1,5},{2,6},{3,7},{4,8},{5,9},{6,10},{7,11},{8,12},{9,13},{1... | collective-permute-start | bytes 983048 | tf_op jit(solution)/shard_map/ppermute | solution.py:33
  102.8 23.6 %collective-permute-start.18 = (bf16[640,256]{1,0:T(8,128)(2,1)S(1)}, bf16[640,256]{1,0:T(8,128)(2,1)S(1)}, u32[]{:S(2)}, u32[]{:S(2)}) collective-permute-start(bf16[640,256]{1,0:T(8,128)(2,1)S(1)} %bitcast.26), channel_id=1, source_target_pairs={{0,12},{1,13},{2,14},{3,15},{4,0},{5,1},{6,2},{7,3},{8,4},{9,5},{1... | collective-permute-start | bytes 983048 | tf_op jit(solution)/shard_map/ppermute | solution.py:33
  105.4 21.0 %collective-permute-start.19 = (bf16[640,256]{1,0:T(8,128)(2,1)S(1)}, bf16[640,256]{1,0:T(8,128)(2,1)S(1)}, u32[]{:S(2)}, u32[]{:S(2)}) collective-permute-start(bf16[640,256]{1,0:T(8,128)(2,1)S(1)} %bitcast.27), channel_id=1, source_target_pairs={{0,8},{1,9},{2,10},{3,11},{4,12},{5,13},{6,14},{7,15},{8,0},{9,1},... | collective-permute-start | bytes 983048 | tf_op jit(solution)/shard_map/ppermute | solution.py:33
  105.6 20.9 %collective-permute-start.20 = (bf16[640,256]{1,0:T(8,128)(2,1)S(1)}, bf16[640,256]{1,0:T(8,128)(2,1)S(1)}, u32[]{:S(2)}, u32[]{:S(2)}) collective-permute-start(bf16[640,256]{1,0:T(8,128)(2,1)S(1)} %bitcast.28), channel_id=1, source_target_pairs={{0,2},{1,3},{2,0},{3,1},{4,6},{5,7},{6,4},{7,5},{8,10},{9,11},{10,... | collective-permute-start | bytes 983048 | tf_op jit(solution)/shard_map/ppermute | solution.py:33
  126.4 18.4 %collective-permute-start.24 = (f32[1280,256]{1,0:T(8,128)}, f32[1280,256]{1,0:T(8,128)S(1)}, u32[]{:S(2)}, u32[]{:S(2)}) collective-permute-start(f32[1280,256]{1,0:T(8,128)} %apply_panel.1), channel_id=1, source_target_pairs={{1,17},{3,19},{5,21},{7,23},{9,25},{11,27},{13,29},{15,31},{16,0},... | collective-permute-start | bytes 3932168 | tf_op jit(solution)/shard_map/ppermute | solution.py:33
  130.0 16.3 %collective-permute-start.21 = (bf16[640,256]{1,0:T(8,128)(2,1)S(1)}, bf16[640,256]{1,0:T(8,128)(2,1)S(1)}, u32[]{:S(2)}, u32[]{:S(2)}) collective-permute-start(bf16[640,256]{1,0:T(8,128)(2,1)S(1)} %collective-permute-done.20.refs_4_), channel_id=1, source_target_pairs={{0,4},{1,5},{2,6},{3,7},{4,8},{5,9},{6,10},{7,11},{8,12},{9,13},{1... | collective-permute-start | bytes 983048 | tf_op jit(solution)/shard_map/ppermute | solution.py:33
  130.3 16.9 %collective-permute-start.22 = (bf16[640,256]{1,0:T(8,128)(2,1)S(1)}, bf16[640,256]{1,0:T(8,128)(2,1)S(1)}, u32[]{:S(2)}, u32[]{:S(2)}) collective-permute-start(bf16[640,256]{1,0:T(8,128)(2,1)S(1)} %collective-permute-done.20.refs_4_), channel_id=1, source_target_pairs={{0,12},{1,13},{2,14},{3,15},{4,0},{5,1},{6,2},{7,3},{8,4},{9,5},{1... | collective-permute-start | bytes 983048 | tf_op jit(solution)/shard_map/ppermute | solution.py:33
  132.8 14.8 %collective-permute-start.23 = (bf16[640,256]{1,0:T(8,128)(2,1)S(1)}, bf16[640,256]{1,0:T(8,128)(2,1)S(1)}, u32[]{:S(2)}, u32[]{:S(2)}) collective-permute-start(bf16[640,256]{1,0:T(8,128)(2,1)S(1)} %collective-permute-done.20.refs_4_), channel_id=1, source_target_pairs={{0,8},{1,9},{2,10},{3,11},{4,12},{5,13},{6,14},{7,15},{8,0},{9,1},... | collective-permute-start | bytes 983048 | tf_op jit(solution)/shard_map/ppermute | solution.py:33
  146.3 6.1 %copy-start = (s32[5]{0:T(128)S(1)}, s32[5]{0:T(128)}, u32[]{:S(2)}) copy-start(s32[5]{0:T(128)} %stack.23.place) | copy-start | bytes 64
  147.6 3.6 %collective-permute-start.25 = (bf16[1280,256]{1,0:T(8,128)(2,1)S(1)}, bf16[1280,256]{1,0:T(8,128)(2,1)}, u32[]{:S(2)}, u32[]{:S(2)}) collective-permute-start(bf16[1280,256]{1,0:T(8,128)(2,1)S(1)} %add_convert_fusion), channel_id=1, source_target_pairs={{0,1},{1,0},{2,3},{3,2},{4,5},{5,4},{6,7},{7,6},{8,9},{9,8},{10,11... | collective-permute-start | bytes 1966088 | tf_op jit(solution)/shard_map/ppermute | solution.py:33
  155.4 9.7 %collective-permute-start.26 = (f32[256,256]{1,0:T(8,128)}, f32[256,256]{1,0:T(8,128)S(1)}, u32[]{:S(2)}, u32[]{:S(2)}) collective-permute-start(f32[256,256]{1,0:T(8,128)} %get-tuple-element.32), channel_id=1, source_target_pairs={{0,64},{1,65},{2,66},{3,67},{4,68},{5,69},{6,70},{7,71},{8,72},{9,... | collective-permute-start | bytes 786440 | tf_op jit(solution)/shard_map/ppermute | solution.py:33
  156.2 14.2 %collective-permute-start.27 = (f32[256,256]{1,0:T(8,128)S(1)}, f32[256,256]{1,0:T(8,128)S(1)}, u32[]{:S(2)}, u32[]{:S(2)}) collective-permute-start(f32[256,256]{1,0:T(8,128)S(1)} %get-tuple-element.33), channel_id=1, source_target_pairs={{0,128},{1,129},{2,130},{3,131},{4,132},{5,133},{6,134},{7,135},{8... | collective-permute-start | bytes 786440 | tf_op jit(solution)/shard_map/ppermute | solution.py:33
  158.2 13.0 %collective-permute-start.28 = (f32[256,256]{1,0:T(8,128)S(1)}, f32[256,256]{1,0:T(8,128)S(1)}, u32[]{:S(2)}, u32[]{:S(2)}) collective-permute-start(f32[256,256]{1,0:T(8,128)S(1)} %get-tuple-element.34), channel_id=1, source_target_pairs={{0,192},{1,193},{2,194},{3,195},{4,196},{5,197},{6,198},{7,199},{8... | collective-permute-start | bytes 786440 | tf_op jit(solution)/shard_map/ppermute | solution.py:33
  171.6 6.8 %collective-permute-start.29 = (f32[128,128]{1,0:T(8,128)S(1)}, f32[128,128]{1,0:T(8,128)S(1)}, u32[]{:S(2)}, u32[]{:S(2)}) collective-permute-start(f32[128,128]{1,0:T(8,128)S(1)} %bitcast.44), channel_id=1, source_target_pairs={{0,0},{1,16},{2,2},{3,18},{4,4},{5,20},{6,6},{7,22},{8,8},{9,24},{... | collective-permute-start | bytes 196616 | tf_op jit(solution)/shard_map/ppermute | solution.py:33
  173.6 4.9 %collective-permute-start.30 = (f32[128,128]{1,0:T(8,128)S(1)}, f32[128,128]{1,0:T(8,128)S(1)}, u32[]{:S(2)}, u32[]{:S(2)}) collective-permute-start(f32[128,128]{1,0:T(8,128)S(1)} %bitcast.43), channel_id=1, source_target_pairs={{0,1},{1,17},{2,3},{3,19},{4,5},{5,21},{6,7},{7,23},{8,9},{9,25},{... | collective-permute-start | bytes 196616 | tf_op jit(solution)/shard_map/ppermute | solution.py:33
  173.7 9.3 %collective-permute-start.31 = (f32[128,128]{1,0:T(8,128)S(1)}, f32[128,128]{1,0:T(8,128)S(1)}, u32[]{:S(2)}, u32[]{:S(2)}) collective-permute-start(f32[128,128]{1,0:T(8,128)S(1)} %bitcast.42), channel_id=1, source_target_pairs={{0,32},{1,48},{2,34},{3,50},{4,36},{5,52},{6,38},{7,54},{8,40},{9,... | collective-permute-start | bytes 196616 | tf_op jit(solution)/shard_map/ppermute | solution.py:33
  178.4 5.9 %collective-permute-start.32 = (f32[128,128]{1,0:T(8,128)S(1)}, f32[128,128]{1,0:T(8,128)S(1)}, u32[]{:S(2)}, u32[]{:S(2)}) collective-permute-start(f32[128,128]{1,0:T(8,128)S(1)} %bitcast.41), channel_id=1, source_target_pairs={{0,33},{1,49},{2,35},{3,51},{4,37},{5,53},{6,39},{7,55},{8,41},{9,... | collective-permute-start | bytes 196616 | tf_op jit(solution)/shard_map/ppermute | solution.py:33

commit v3 on v2

--- a/solution.py
+++ b/solution.py
@@ -73,11 +73,52 @@
     return (y, z ^ 2, x, h, c)
 
 
+def pack_kernel(count, diagonal, blocks, cols, four, five):
+    nothing = jnp.zeros((BR, BR), jnp.bfloat16)
+
+    def live(t, s):
+        return jnp.where(s < count[t], blocks[t, s], nothing)
+
+    for t in range(20):
+        rows = pl.ds(t * BR, BR)
+        four[rows, :] = jnp.concatenate([live(t, s) for s in range(4)], axis=1)
+    for t in range(5):
+        quarters = [live(q * 5 + t, 4) for q in range(4)]
+        five[pl.ds(t * BR, BR), :] = jnp.concatenate(quarters, axis=1)
+    ends = jnp.clip(cols[...], 0, 19).astype(jnp.float32)
+    ends = jnp.concatenate([ends, jnp.zeros((20, 123), jnp.float32)], axis=1)
+    ends = jnp.concatenate([ends, jnp.zeros((12, 128), jnp.float32)], axis=0)
+    four[pl.ds(1280, 32), :128] = ends.astype(jnp.bfloat16)
+    four[pl.ds(1280, 32), 128:] = jnp.zeros((32, 128), jnp.bfloat16)
+    own = diagonal[0] == 1
+    five[pl.ds(320, 32), :128] = jnp.where(own, ends, 0.0).astype(jnp.bfloat16)
+    five[pl.ds(320, 32), 128:] = jnp.zeros((32, 128), jnp.bfloat16)
+
+
+def pack(count, diagonal, blocks, cols):
+    inside = pl.BlockSpec(memory_space=pltpu.VMEM)
+    return pl.pallas_call(
+        pack_kernel,
+        out_shape=(
+            jax.ShapeDtypeStruct((1312, 256), jnp.bfloat16),
+            jax.ShapeDtypeStruct((352, 256), jnp.bfloat16),
+        ),
+        grid_spec=pltpu.PrefetchScalarGridSpec(
+            num_scalar_prefetch=2,
+            grid=(),
+            in_specs=[inside, inside],
+            out_specs=(inside, inside),
+        ),
+        cost_estimate=pl.CostEstimate(flops=0, bytes_accessed=3 * 2**20, transcendentals=0),
+        name="pack",
+    )(count, diagonal, blocks, cols)
+
+
 def apply_kernel(place, *refs):
     p_refs = refs[:8]
     a_refs = refs[8:16]
     out = refs[16]
-    panel, left, last, ends, numbers, offsets, sems = refs[17:]
+    panel, left, ends, numbers, offsets, sems = refs[17:]
     y, z, x, h, c = (place[i] for i in range(5))
     copies = []
 
@@ -88,52 +129,40 @@
 
     for f in range(2):
         for i in range(4):
-            start(a_refs[4 * f + i].at[pl.ds(1280, 16)], ends.at[2 * i + f])
+            start(a_refs[4 * f + i].at[pl.ds(1280, 32)], ends.at[2 * i + f])
     for i, k in enumerate(STEPS):
         jx = lax.rem(y + 4 - k, 4)
         for s in range(4):
             j1, l0 = lax.rem(z // 2 + s % 2, 2), lax.rem(c + s // 2, 2)
             src = p_refs[4 * (s // 2) + i].at[pl.ds((s % 2) * 1280, 1280)]
             start(src, panel.at[l0, pl.ds(pl.multiple_of((jx * 2 + j1) * 1280, 1280), 1280)])
-        start(a_refs[i].at[pl.ds(1296, 320)], last.at[i])
         for f in range(2):
             start(a_refs[4 * f + i].at[pl.ds(0, 1280)], left.at[2 * i + f])
 
     for copy in copies[:8]:
         copy.wait()
     for slot in range(8):
-        numbers[pl.ds(slot, 1), :] = ends[slot][:1, :128].astype(jnp.float32).astype(jnp.int32)
+        numbers[slot] = ends[slot][:24, :128].astype(jnp.float32).astype(jnp.int32)
     scalars = pltpu.make_async_copy(numbers, offsets, sems.at[len(copies)])
     scalars.start()
     for copy in copies[8:] + [scalars]:
         copy.wait()
 
-    step = lax.rem(x + 4 - y, 4)
-    step = jnp.where(step > 1, 5 - step, step)
-    own = step * 2 + lax.rem(h + z // 2, 2)
     bases = []
     for slot in range(8):
         jx = lax.rem(x + 4 - STEPS[slot // 2], 4)
         bases.append((jx * 2 + lax.rem(h + slot % 2, 2)) * 1280)
-    own_base = (y * 2 + z // 2) * 1280
 
     def block(base, slot, at):
-        rows = pl.ds(pl.multiple_of(base + offsets[slot, at] * BR, BR), BR)
+        rows = pl.ds(pl.multiple_of(base + offsets[slot, at[0], at[1]] * BR, BR), BR)
         return jnp.concatenate([panel[0, rows, :], panel[1, rows, :]], axis=1)
 
     @pl.loop(0, 20)
     def _(t):
         rows = pl.ds(pl.multiple_of(t * BR, BR), BR)
-        fifth = block(own_base, own, t * 5 + 4)
-        nothing = jnp.zeros_like(fifth)
-        right = jnp.concatenate([jnp.where(t // 5 == q, fifth, nothing) for q in range(4)], axis=0)
-        total = jnp.dot(
-            last[step, pl.ds(pl.multiple_of(lax.rem(t, 5) * BR, BR), BR), :],
-            right,
-            preferred_element_type=jnp.float32,
-        )
+        total = jnp.zeros((BR, 256), jnp.float32)
         for slot in range(8):
-            blocks = [block(bases[slot], slot, t * 5 + s) for s in range(4)]
+            blocks = [block(bases[slot], slot, (t, s)) for s in range(4)]
             right = jnp.concatenate(blocks, axis=0)
             total += jnp.dot(left[slot, rows, :], right, preferred_element_type=jnp.float32)
         out[rows, :] = total
@@ -141,6 +170,7 @@
 
 def apply_panel(place, p_pieces, a_pieces):
     anywhere = pl.BlockSpec(memory_space=pl.ANY)
+    inside = pl.BlockSpec(memory_space=pltpu.VMEM)
     return pl.pallas_call(
         apply_kernel,
         out_shape=jax.ShapeDtypeStruct((1280, 256), jnp.float32),
@@ -148,15 +178,14 @@
             num_scalar_prefetch=1,
             grid=(),
             in_specs=[anywhere] * 16,
-            out_specs=pl.BlockSpec(memory_space=pltpu.VMEM),
+            out_specs=inside,
             scratch_shapes=[
                 pltpu.VMEM((2, 8 * 1280, 128), jnp.bfloat16),
                 pltpu.VMEM((8, 1280, 256), jnp.bfloat16),
-                pltpu.VMEM((4, 320, 256), jnp.bfloat16),
-                pltpu.VMEM((8, 16, 256), jnp.bfloat16),
-                pltpu.VMEM((8, 128), jnp.int32),
-                pltpu.SMEM((8, 128), jnp.int32),
-                pltpu.SemaphoreType.DMA((37,)),
+                pltpu.VMEM((8, 32, 256), jnp.bfloat16),
+                pltpu.VMEM((8, 24, 128), jnp.int32),
+                pltpu.SMEM((8, 24, 128), jnp.int32),
+                pltpu.SemaphoreType.DMA((33,)),
             ],
         ),
         compiler_params=pltpu.CompilerParams(vmem_limit_bytes=56 * 2**20),
@@ -165,6 +194,57 @@
         ),
         name="apply_panel",
     )(place, *p_pieces, *a_pieces)
+
+
+def last_kernel(place, mine, other, five, out, panel, numbers, offsets, sems):
+    c = place[4]
+    copies = []
+    for n, src in enumerate((mine, other)):
+        dst = panel.at[lax.rem(c + n, 2)]
+        copies.append(pltpu.make_async_copy(src.at[pl.ds(0, 1280)], dst, sems.at[n]))
+        copies[n].start()
+    numbers[...] = five[pl.ds(320, 32), :128][:24].astype(jnp.float32).astype(jnp.int32)
+    scalars = pltpu.make_async_copy(numbers, offsets, sems.at[2])
+    scalars.start()
+    for copy in copies + [scalars]:
+        copy.wait()
+
+    @pl.loop(0, 20)
+    def _(t):
+        rows = pl.ds(pl.multiple_of(offsets[t, 4] * BR, BR), BR)
+        block = jnp.concatenate([panel[0, rows, :], panel[1, rows, :]], axis=1)
+        nothing = jnp.zeros_like(block)
+        right = jnp.concatenate([jnp.where(t // 5 == q, block, nothing) for q in range(4)], axis=0)
+        out[pl.ds(pl.multiple_of(t * BR, BR), BR), :] = jnp.dot(
+            five[pl.ds(pl.multiple_of(lax.rem(t, 5) * BR, BR), BR), :],
+            right,
+            preferred_element_type=jnp.float32,
+        )
+
+
+def apply_last(place, mine, other, five):
+    anywhere = pl.BlockSpec(memory_space=pl.ANY)
+    inside = pl.BlockSpec(memory_space=pltpu.VMEM)
+    return pl.pallas_call(
+        last_kernel,
+        out_shape=jax.ShapeDtypeStruct((1280, 256), jnp.float32),
+        grid_spec=pltpu.PrefetchScalarGridSpec(
+            num_scalar_prefetch=1,
+            grid=(),
+            in_specs=[anywhere, anywhere, inside],
+            out_specs=inside,
+            scratch_shapes=[
+                pltpu.VMEM((2, 1280, 128), jnp.bfloat16),
+                pltpu.VMEM((24, 128), jnp.int32),
+                pltpu.SMEM((24, 128), jnp.int32),
+                pltpu.SemaphoreType.DMA((3,)),
+            ],
+        ),
+        cost_estimate=pl.CostEstimate(
+            flops=2 * 1280 * 256 * 256, bytes_accessed=2 * 2**20, transcendentals=0
+        ),
+        name="apply_last",
+    )(place, mine, other, five)
 
 
 def project_kernel(place, *refs):
@@ -231,23 +311,21 @@
     p_own = jnp.concatenate([p_flat, move(p_flat, flip_z1)])
     p_twin = move(p_own, flip_c)
 
-    live = jnp.arange(5, dtype=jnp.int32)[None, :] < a_count
-    masked = jnp.where(live[:, :, None], a_vals, jnp.zeros_like(a_vals))
-    slots = masked.reshape(20, 5, BR, BR)
-    four = slots[:, :4].transpose(0, 2, 1, 3).reshape(1280, 256)
-    offsets = jnp.clip(a_cols - col * 20, 0, 19).astype(jnp.bfloat16).reshape(1, 100)
-    four = jnp.concatenate([four, jnp.pad(offsets, ((0, 15), (0, 156)))])
+    diagonal = (row == col).astype(jnp.int32).reshape(1)
+    four, five = pack(a_count.reshape(20), diagonal, a_vals.reshape(20, 5, BR, BR), a_cols - col * 20)
     swapped = move(four, swap_zc)
 
     def across(y, z, x, h, c):
         return (y, z, x, 1 - h, c) if h == z // 2 and x == y and c == z % 2 else None
 
-    five = slots[:, 4].reshape(4, 320, BR)
-    five = jnp.concatenate([five[q] for q in range(4)], axis=1)
-    five = five + move(five, across)
-
-    p_own, p_twin, swapped, four, five = after((p_own, p_twin, swapped, four, five))
-    near = jnp.concatenate([swapped, five])
+    def next_x(y, z, x, h, c):
+        return (y, z, (x + 1) % 4, h, c) if x == y and c == z % 2 else None
+
+    def over_x(y, z, x, h, c):
+        return (y, z, (x + 2) % 4, h, c) if (x - y) % 4 < 2 and c == z % 2 else None
+
+
+    p_own, near, four = after((p_own, swapped, four))
     far = move(four, cross_zc)
     a_near = [near] + [move(near, shift_x(k)) for k in (1, 3, 2)]
     p_mine = [p_own, move(p_own, shift_y(1))]
@@ -257,13 +335,17 @@
     p_other = [p_twin] + [move(piece, flip_c) for piece in p_mine[1:]]
 
     t_own = p_flat.reshape(5, 256, 128).transpose(0, 2, 1).reshape(640, 256)
-    (t_own,) = after((t_own,), *a_far, *p_other)
+    t_own, five = after((t_own, five), *a_far, *p_other)
     t_far = move(t_own, flip_h)
     t_near = [t_own] + [move(t_own, shift_x(k)) for k in (1, 3, 2)]
+    five = five + move(five, across)
     product = apply_panel(place, p_mine + p_other, a_near + a_far)
-    product, t_far = after((product, t_far), *t_near)
+    product, t_far, five = after((product, t_far, five), *t_near)
     t_far = [t_far] + [move(t_far, shift_x(k)) for k in (1, 3, 2)]
-    prolonged = (product + move(product, flip_z0)).astype(jnp.bfloat16)
+    five = five + move(five, next_x)
+    five = five + move(five, over_x)
+    extra = apply_last(place, p_mine[0], p_other[0], five)
+    prolonged = (product + extra + move(product, flip_z0)).astype(jnp.bfloat16)
     (prolonged,) = after((prolonged,), *t_near, *t_far)
     prolonged = jnp.where(c == z % 2, prolonged, move(prolonged, flip_c))
 

time: 185 us -> 179 us (0.968)
  Pallas kernels: 16.1 us -> 25.3 us
  waiting for transfers between devices: 79 us -> 70.7 us
  starting transfers between devices: 72.5 us -> 68.4 us
  local copies, waits for them, and re-layouts: 8.51 us -> 6.17 us
    pallas_call x0 -> x2, Pallas kernels: none -> 10.2 us  [the longest x1 6.94 us: apply_last(): pl.pallas_call(last_kernel, out_shape=jax.ShapeDtypeStruct((1280, 256), j...]
    ppermute x33 -> x35, waiting for transfers between devices: 79 us -> 70.7 us  [move(): return lax.ppermute(array, AXES, pairs)]
    ppermute x33 -> x35, starting transfers between devices: 72.5 us -> 68.4 us  [move(): return lax.ppermute(array, AXES, pairs)]
    transpose x2 -> x0, local copies, waits for them, and re-layouts: 2.35 us -> none  [per_device(): four = slots[:, :4].transpose(0, 2, 1, 3).reshape(1280, 256)]
    reshape x3 -> x2, local copies, waits for them, and re-layouts: 4.14 us -> 4.23 us  [per_device(): a_vals.reshape(20, 5, BR, BR)]
  transfers between devices with their start and end apart: 33 -> 35, of which waited for: 16 -> 13; matrix products, arithmetic and copies ran while one was open for 7% -> 5% of each run, Pallas kernels for 7% -> 13%
where the time goes in v3:
time: 179 us; the launch traced here: 178 us
  waiting for transfers between devices  70.7 us (39%)
  starting transfers between devices  68.4 us (38%)
  Pallas kernels  25.3 us (14%)
  other arithmetic  7.35 us (4%)
  local copies, waits for them, and re-layouts  6.17 us (3%)
    ppermute x35, waiting for transfers between devices, move(): return lax.ppermute(array, AXES, pairs)  70.7 us
    ppermute x35, starting transfers between devices, move(): return lax.ppermute(array, AXES, pairs)  68.4 us
    pallas_call x1, Pallas kernels, apply_panel(): pl.pallas_call(apply_kernel, out_shape=jax.ShapeDtypeStruct((1280, 256),...  12.2 us
    pallas_call x1, Pallas kernels, apply_last(): pl.pallas_call(last_kernel, out_shape=jax.ShapeDtypeStruct((1280, 256), j...  6.94 us
    reshape x2, local copies, waits for them, and re-layouts, per_device(): a_vals.reshape(20, 5, BR, BR)  4.23 us
  transfers between devices with their start and end apart: 35, of which 13 were waited for; matrix products, arithmetic and copies ran while one was open for 5% of the time, Pallas kernels for 13%

profile of v3, /device:TPU:1, one launch (start us, length us, event | category | flops | bytes accessed | tf_op | source)
XLA Modules:
  0.0 178.4 jit_solution(7071225862594383126)
XLA Ops:
  0.0 0.7 convert_bitcast_fusion
  0.7 1.1 broadcast_multiply_fusion
  1.7 3.9 %collective-permute-start = (bf16[1280,128]{1,0:T(8,128)(2,1)S(1)}, bf16[1280,128]{1,0:T(8,128)(2,1)S(1)}, u32[]{:S(2)}, u32[]{:S(2)}) collective-permute-start(bf16[1280,128]{1,0:T(8,128)(2,1)S(1)} %bitcast.25), channel_id=1, source_target_pairs={{0,32},{1,33},{2,34},{3,35},{4,36},{5,37},{6,38},{7,39},{8,40},{9,... | collective-permute-start | bytes 983048 | tf_op jit(solution)/shard_map/ppermute | solution.py:33
  5.6 0.8 copy.13
  7.0 2.9 %reshape.44 = bf16[20,5,64,64]{3,2,0,1:T(8,128)(2,1)S(1)} reshape(bf16[20,5,4096]{2,0,1:T(8,128)(2,1)} %param.5) | data formatting | bytes 1638400 | tf_op jit(solution)/shard_map/reshape | solution.py:315
  9.9 1.3 copy.15.blocks
  11.2 3.3 %pack.1 = (bf16[1312,256]{1,0:T(8,128)(2,1)}, bf16[352,256]{1,0:T(8,128)(2,1)}) custom-call(s32[20]{0:T(128)} %bitcast.32, s32[1]{0:T(128)} %bitcast.10.diagonal, bf16[20,5,64,64]{3,2,1,0:T(8,128)(2,1)} %copy.15.blocks, s32[20,5]{1,0:T(8,128)} %broadcast_subtract_fusion.cols), custom_call_target="tpu_custom_call" | custom-call | bytes 3145728 | tf_op jit(solution)/shard_map/pack/pallas_call | solution.py:100
  14.5 4.5 %collective-permute-start.1 = (bf16[1312,256]{1,0:T(8,128)(2,1)}, bf16[1312,256]{1,0:T(8,128)(2,1)S(1)}, u32[]{:S(2)}, u32[]{:S(2)}) collective-permute-start(bf16[1312,256]{1,0:T(8,128)(2,1)} %get-tuple-element.24), channel_id=1, source_target_pairs={{0,0},{1,16},{2,2},{3,18},{4,4},{5,20},{6,6},{7,22},{8,8},{9,24},{... | collective-permute-start | bytes 2015240 | tf_op jit(solution)/shard_map/ppermute | solution.py:33
  19.5 8.7 %collective-permute-done.1.refs_8_ = bf16[1312,256]{1,0:T(8,128)(2,1)S(1)} collective-permute-done((bf16[1312,256]{1,0:T(8,128)(2,1)}, bf16[1312,256]{1,0:T(8,128)(2,1)S(1)}, u32[]{:S(2)}, u32[]{:S(2)}) %collective-permute-start.1) | collective-permute-done | bytes 671776 | tf_op jit(solution)/shard_map/ppermute | solution.py:33
  28.1 1.2 collective-permute-start.4
  29.3 1.5 collective-permute-start.5
  30.8 1.5 collective-permute-start.6
  32.3 11.9 %collective-permute-start.2 = (bf16[1312,256]{1,0:T(8,128)(2,1)S(1)}, bf16[1312,256]{1,0:T(8,128)(2,1)}, u32[]{:S(2)}, u32[]{:S(2)}) collective-permute-start(bf16[1312,256]{1,0:T(8,128)(2,1)S(1)} %copy-done.10), channel_id=1, source_target_pairs={{0,2},{1,18},{2,0},{3,16},{4,6},{5,22},{6,4},{7,20},{8,10},{9,26},... | collective-permute-start | bytes 2015240 | tf_op jit(solution)/shard_map/ppermute | solution.py:33
  44.2 1.3 collective-permute-start.3
  45.5 9.4 %collective-permute-done.3.refs_1_ = bf16[2560,128]{1,0:T(8,128)(2,1)S(1)} collective-permute-done((bf16[2560,128]{1,0:T(8,128)(2,1)S(1)}, bf16[2560,128]{1,0:T(8,128)(2,1)S(1)}, u32[]{:S(2)}, u32[]{:S(2)}) %collective-permute-start.3) | collective-permute-done | bytes 655392 | tf_op jit(solution)/shard_map/ppermute | solution.py:33
  55.5 7.6 %collective-permute-done.2.refs_12_ = bf16[1312,256]{1,0:T(8,128)(2,1)} collective-permute-done((bf16[1312,256]{1,0:T(8,128)(2,1)S(1)}, bf16[1312,256]{1,0:T(8,128)(2,1)}, u32[]{:S(2)}, u32[]{:S(2)}) %collective-permute-start.2) | collective-permute-done | bytes 671776 | tf_op jit(solution)/shard_map/ppermute | solution.py:33
  63.0 2.7 %collective-permute-start.12 = (bf16[2560,128]{1,0:T(8,128)(2,1)S(1)}, bf16[2560,128]{1,0:T(8,128)(2,1)}, u32[]{:S(2)}, u32[]{:S(2)}) collective-permute-start(bf16[2560,128]{1,0:T(8,128)(2,1)S(1)} %pad_maximum_fusion.refs_0_.mine), channel_id=1, source_target_pairs={{0,192},{1,193},{2,194},{3,195},{4,196},{5,197},{6,198},{7,199},{8... | collective-permute-start | bytes 1966088 | tf_op jit(solution)/shard_map/ppermute | solution.py:33
  66.5 2.3 %collective-permute-start.8 = (bf16[1312,256]{1,0:T(8,128)(2,1)}, bf16[1312,256]{1,0:T(8,128)(2,1)}, u32[]{:S(2)}, u32[]{:S(2)}) collective-permute-start(bf16[1312,256]{1,0:T(8,128)(2,1)} %collective-permute-done.2.refs_12_), channel_id=1, source_target_pairs={{0,12},{1,13},{2,14},{3,15},{4,0},{5,1},{6,2},{7,3},{8,4},{9,5},{1... | collective-permute-start | bytes 2015240 | tf_op jit(solution)/shard_map/ppermute | solution.py:33
  69.1 17.6 %collective-permute-done.12.refs_2_ = bf16[2560,128]{1,0:T(8,128)(2,1)} collective-permute-done((bf16[2560,128]{1,0:T(8,128)(2,1)S(1)}, bf16[2560,128]{1,0:T(8,128)(2,1)}, u32[]{:S(2)}, u32[]{:S(2)}) %collective-permute-start.12) | collective-permute-done | bytes 655392 | tf_op jit(solution)/shard_map/ppermute | solution.py:33
  87.4 3.9 %collective-permute-done.7.refs_13_ = bf16[1312,256]{1,0:T(8,128)(2,1)} collective-permute-done((bf16[1312,256]{1,0:T(8,128)(2,1)}, bf16[1312,256]{1,0:T(8,128)(2,1)}, u32[]{:S(2)}, u32[]{:S(2)}) %collective-permute-start.7) | collective-permute-done | bytes 671776 | tf_op jit(solution)/shard_map/ppermute | solution.py:33
  91.3 0.8 collective-permute-start.16
  92.1 2.6 %collective-permute-start.17 = (bf16[640,256]{1,0:T(8,128)(2,1)S(1)}, bf16[640,256]{1,0:T(8,128)(2,1)S(1)}, u32[]{:S(2)}, u32[]{:S(2)}) collective-permute-start(bf16[640,256]{1,0:T(8,128)(2,1)S(1)} %bitcast.21), channel_id=1, source_target_pairs={{0,12},{1,13},{2,14},{3,15},{4,0},{5,1},{6,2},{7,3},{8,4},{9,5},{1... | collective-permute-start | bytes 983048 | tf_op jit(solution)/shard_map/ppermute | solution.py:33
  94.7 1.1 collective-permute-start.18
  95.8 6.0 %collective-permute-start.19 = (bf16[640,256]{1,0:T(8,128)(2,1)S(1)}, bf16[640,256]{1,0:T(8,128)(2,1)S(1)}, u32[]{:S(2)}, u32[]{:S(2)}) collective-permute-start(bf16[640,256]{1,0:T(8,128)(2,1)S(1)} %bitcast.23), channel_id=1, source_target_pairs={{0,2},{1,3},{2,0},{3,1},{4,6},{5,7},{6,4},{7,5},{8,10},{9,11},{10,... | collective-permute-start | bytes 983048 | tf_op jit(solution)/shard_map/ppermute | solution.py:33
  101.8 0.7 collective-permute-start.20
  103.1 12.2 %apply_panel.1 = f32[1280,256]{1,0:T(8,128)} custom-call(s32[5]{0:T(128)} %stack.23.place, bf16[2560,128]{1,0:T(8,128)(2,1)} %copy-done.1, bf16[2560,128]{1,0:T(8,128)(2,1)} %copy-done.7, bf16[2560,128]{1,0:T(8,128)(2,1)} %collective-permute-done.12.refs_2_, bf16[2560,128]{1,0:T(8,128)(2,1)} %collective-permute-done.14.refs_3_, bf16[2560,128]{1,0:T(8,128)(2,1)} %copy-done.2, ...), custom_call_target="tpu_custom_call" | custom-call | flops 1342177280 | bytes 12582912 | tf_op jit(solution)/shard_map/apply_panel/pallas_call | solution.py:174
  115.5 1.6 collective-permute-done.19.refs_4_
  117.1 2.3 %collective-permute-start.26 = (f32[1280,256]{1,0:T(8,128)}, f32[1280,256]{1,0:T(8,128)}, u32[]{:S(2)}, u32[]{:S(2)}) collective-permute-start(f32[1280,256]{1,0:T(8,128)} %apply_panel.1), channel_id=1, source_target_pairs={{1,17},{3,19},{5,21},{7,23},{9,25},{11,27},{13,29},{15,31},{16,0},... | collective-permute-start | bytes 3932168 | tf_op jit(solution)/shard_map/ppermute | solution.py:33
  119.5 0.7 collective-permute-start.24
  120.2 0.7 collective-permute-start.25
  121.0 2.7 %collective-permute-start.22 = (bf16[640,256]{1,0:T(8,128)(2,1)S(1)}, bf16[640,256]{1,0:T(8,128)(2,1)S(1)}, u32[]{:S(2)}, u32[]{:S(2)}) collective-permute-start(bf16[640,256]{1,0:T(8,128)(2,1)S(1)} %collective-permute-done.19.refs_4_), channel_id=1, source_target_pairs={{0,12},{1,13},{2,14},{3,15},{4,0},{5,1},{6,2},{7,3},{8,4},{9,5},{1... | collective-permute-start | bytes 983048 | tf_op jit(solution)/shard_map/ppermute | solution.py:33
  123.6 0.7 add.107.five
  124.3 6.9 %apply_last.1 = f32[1280,256]{1,0:T(8,128)} custom-call(s32[5]{0:T(128)} %stack.23.place, bf16[2560,128]{1,0:T(8,128)(2,1)} %copy-done.1, bf16[2560,128]{1,0:T(8,128)(2,1)} %copy-done.2, bf16[352,256]{1,0:T(8,128)(2,1)} %add.107.five), custom_call_target="tpu_custom_call" | custom-call | flops 167772160 | bytes 2097152 | tf_op jit(solution)/shard_map/apply_last/pallas_call | solution.py:228
  131.3 2.0 %collective-permute-done.26 = f32[1280,256]{1,0:T(8,128)} collective-permute-done((f32[1280,256]{1,0:T(8,128)}, f32[1280,256]{1,0:T(8,128)}, u32[]{:S(2)}, u32[]{:S(2)}) %collective-permute-start.26) | collective-permute-done | bytes 1310752 | tf_op jit(solution)/shard_map/ppermute | solution.py:33
  133.2 2.3 %add_convert_fusion = bf16[1280,256]{1,0:T(8,128)(2,1)S(1)} fusion(f32[1280,256]{1,0:T(8,128)} %collective-permute-done.26, f32[1280,256]{1,0:T(8,128)} %apply_panel.1, f32[1280,256]{1,0:T(8,128)} %apply_last.1), kind=kLoop, calls=%fused_computation | loop fusion | flops 983040 | bytes 4587520 | tf_op jit(solution)/shard_map/convert_element_type | solution.py:348
  135.6 5.7 %collective-permute-start.27 = (bf16[1280,256]{1,0:T(8,128)(2,1)S(1)}, bf16[1280,256]{1,0:T(8,128)(2,1)}, u32[]{:S(2)}, u32[]{:S(2)}) collective-permute-start(bf16[1280,256]{1,0:T(8,128)(2,1)S(1)} %add_convert_fusion), channel_id=1, source_target_pairs={{0,1},{1,0},{2,3},{3,2},{4,5},{5,4},{6,7},{7,6},{8,9},{9,8},{10,11... | collective-permute-start | bytes 1966088 | tf_op jit(solution)/shard_map/ppermute | solution.py:33
  141.3 1.9 %collective-permute-done.27 = bf16[1280,256]{1,0:T(8,128)(2,1)} collective-permute-done((bf16[1280,256]{1,0:T(8,128)(2,1)S(1)}, bf16[1280,256]{1,0:T(8,128)(2,1)}, u32[]{:S(2)}, u32[]{:S(2)}) %collective-permute-start.27) | collective-permute-done | bytes 655392 | tf_op jit(solution)/shard_map/ppermute | solution.py:33
  143.2 1.2 broadcast_select_fusion.refs_8_
  144.3 2.9 %project.1 = (f32[256,256]{1,0:T(8,128)S(1)}, f32[256,256]{1,0:T(8,128)}, f32[256,256]{1,0:T(8,128)S(1)}, f32[256,256]{1,0:T(8,128)S(1)}) custom-call(s32[5]{0:T(128)S(1)} %copy-done, bf16[640,256]{1,0:T(8,128)(2,1)S(1)} %bitcast.24, bf16[640,256]{1,0:T(8,128)(2,1)S(1)} %collective-permute-done.16.refs_1_, ...), custom_call_target="tpu_custom_call" | custom-call | flops 671088640 | bytes 4194304 | tf_op jit(solution)/shard_map/project/pallas_call | solution.py:282
  147.2 3.3 %collective-permute-start.28 = (f32[256,256]{1,0:T(8,128)}, f32[256,256]{1,0:T(8,128)S(1)}, u32[]{:S(2)}, u32[]{:S(2)}) collective-permute-start(f32[256,256]{1,0:T(8,128)} %get-tuple-element.36), channel_id=1, source_target_pairs={{0,64},{1,65},{2,66},{3,67},{4,68},{5,69},{6,70},{7,71},{8,72},{9,... | collective-permute-start | bytes 786440 | tf_op jit(solution)/shard_map/ppermute | solution.py:33
  150.6 3.0 %collective-permute-start.29 = (f32[256,256]{1,0:T(8,128)S(1)}, f32[256,256]{1,0:T(8,128)S(1)}, u32[]{:S(2)}, u32[]{:S(2)}) collective-permute-start(f32[256,256]{1,0:T(8,128)S(1)} %get-tuple-element.37), channel_id=1, source_target_pairs={{0,128},{1,129},{2,130},{3,131},{4,132},{5,133},{6,134},{7,135},{8... | collective-permute-start | bytes 786440 | tf_op jit(solution)/shard_map/ppermute | solution.py:33
  153.5 5.0 %collective-permute-done.28 = f32[256,256]{1,0:T(8,128)S(1)} collective-permute-done((f32[256,256]{1,0:T(8,128)}, f32[256,256]{1,0:T(8,128)S(1)}, u32[]{:S(2)}, u32[]{:S(2)}) %collective-permute-start.28) | collective-permute-done | bytes 262176 | tf_op jit(solution)/shard_map/ppermute | solution.py:33
  158.6 7.1 %collective-permute-done.29 = f32[256,256]{1,0:T(8,128)S(1)} collective-permute-done((f32[256,256]{1,0:T(8,128)S(1)}, f32[256,256]{1,0:T(8,128)S(1)}, u32[]{:S(2)}, u32[]{:S(2)}) %collective-permute-start.29) | collective-permute-done | bytes 262176 | tf_op jit(solution)/shard_map/ppermute | solution.py:33
  166.2 1.9 %collective-permute-start.31 = (f32[128,128]{1,0:T(8,128)S(1)}, f32[128,128]{1,0:T(8,128)S(1)}, u32[]{:S(2)}, u32[]{:S(2)}) collective-permute-start(f32[128,128]{1,0:T(8,128)S(1)} %bitcast.31), channel_id=1, source_target_pairs={{0,0},{1,16},{2,2},{3,18},{4,4},{5,20},{6,6},{7,22},{8,8},{9,24},{... | collective-permute-start | bytes 196616 | tf_op jit(solution)/shard_map/ppermute | solution.py:33
  168.3 3.8 %collective-permute-start.34 = (f32[128,128]{1,0:T(8,128)S(1)}, f32[128,128]{1,0:T(8,128)S(1)}, u32[]{:S(2)}, u32[]{:S(2)}) collective-permute-start(f32[128,128]{1,0:T(8,128)S(1)} %bitcast.28), channel_id=1, source_target_pairs={{0,33},{1,49},{2,35},{3,51},{4,37},{5,53},{6,39},{7,55},{8,41},{9,... | collective-permute-start | bytes 196616 | tf_op jit(solution)/shard_map/ppermute | solution.py:33
  172.1 2.5 %collective-permute-done.33 = f32[128,128]{1,0:T(8,128)S(1)} collective-permute-done((f32[128,128]{1,0:T(8,128)S(1)}, f32[128,128]{1,0:T(8,128)S(1)}, u32[]{:S(2)}, u32[]{:S(2)}) %collective-permute-start.33) | collective-permute-done | bytes 65568 | tf_op jit(solution)/shard_map/ppermute | solution.py:33
  174.6 3.2 %collective-permute-done.34 = f32[128,128]{1,0:T(8,128)S(1)} collective-permute-done((f32[128,128]{1,0:T(8,128)S(1)}, f32[128,128]{1,0:T(8,128)S(1)}, u32[]{:S(2)}, u32[]{:S(2)}) %collective-permute-start.34) | collective-permute-done | bytes 65568 | tf_op jit(solution)/shard_map/ppermute | solution.py:33
  177.7 0.6 add_add_fusion.1
  (66 shorter events, 4.7 us)
Async XLA Ops:
  1.7 17.7 %collective-permute-start = (bf16[1280,128]{1,0:T(8,128)(2,1)S(1)}, bf16[1280,128]{1,0:T(8,128)(2,1)S(1)}, u32[]{:S(2)}, u32[]{:S(2)}) collective-permute-start(bf16[1280,128]{1,0:T(8,128)(2,1)S(1)} %bitcast.25), channel_id=1, source_target_pairs={{0,32},{1,33},{2,34},{3,35},{4,36},{5,37},{6,38},{7,39},{8,40},{9,... | collective-permute-start | bytes 983048 | tf_op jit(solution)/shard_map/ppermute | solution.py:33
  14.5 17.8 %copy-start.10 = (bf16[1312,256]{1,0:T(8,128)(2,1)S(1)}, bf16[1312,256]{1,0:T(8,128)(2,1)}, u32[]{:S(2)}) copy-start(bf16[1312,256]{1,0:T(8,128)(2,1)} %get-tuple-element.24) | copy-start | bytes 2015236
  14.5 87.3 %copy-start.9 = (bf16[352,256]{1,0:T(8,128)(2,1)S(1)}, bf16[352,256]{1,0:T(8,128)(2,1)}, u32[]{:S(2)}) copy-start(bf16[352,256]{1,0:T(8,128)(2,1)} %get-tuple-element.30) | copy-start | bytes 540676
  14.5 13.6 %collective-permute-start.1 = (bf16[1312,256]{1,0:T(8,128)(2,1)}, bf16[1312,256]{1,0:T(8,128)(2,1)S(1)}, u32[]{:S(2)}, u32[]{:S(2)}) collective-permute-start(bf16[1312,256]{1,0:T(8,128)(2,1)} %get-tuple-element.24), channel_id=1, source_target_pairs={{0,0},{1,16},{2,2},{3,18},{4,4},{5,20},{6,6},{7,22},{8,8},{9,24},{... | collective-permute-start | bytes 2015240 | tf_op jit(solution)/shard_map/ppermute | solution.py:33
  19.5 83.7 %copy-start.1 = (bf16[2560,128]{1,0:T(8,128)(2,1)}, bf16[2560,128]{1,0:T(8,128)(2,1)S(1)}, u32[]{:S(2)}) copy-start(bf16[2560,128]{1,0:T(8,128)(2,1)S(1)} %pad_maximum_fusion.refs_0_.mine) | copy-start | bytes 1966084
  28.1 63.1 %copy-start.3 = (bf16[1312,256]{1,0:T(8,128)(2,1)}, bf16[1312,256]{1,0:T(8,128)(2,1)S(1)}, u32[]{:S(2)}) copy-start(bf16[1312,256]{1,0:T(8,128)(2,1)S(1)} %collective-permute-done.1.refs_8_) | copy-start | bytes 2015236
  28.1 26.8 %collective-permute-start.4 = (bf16[1312,256]{1,0:T(8,128)(2,1)S(1)}, bf16[1312,256]{1,0:T(8,128)(2,1)S(1)}, u32[]{:S(2)}, u32[]{:S(2)}) collective-permute-start(bf16[1312,256]{1,0:T(8,128)(2,1)S(1)} %collective-permute-done.1.refs_8_), channel_id=1, source_target_pairs={{0,4},{1,5},{2,6},{3,7},{4,8},{5,9},{6,10},{7,11},{8,12},{9,13},{1... | collective-permute-start | bytes 2015240 | tf_op jit(solution)/shard_map/ppermute | solution.py:33
  29.3 26.1 %collective-permute-start.5 = (bf16[1312,256]{1,0:T(8,128)(2,1)S(1)}, bf16[1312,256]{1,0:T(8,128)(2,1)S(1)}, u32[]{:S(2)}, u32[]{:S(2)}) collective-permute-start(bf16[1312,256]{1,0:T(8,128)(2,1)S(1)} %collective-permute-done.1.refs_8_), channel_id=1, source_target_pairs={{0,12},{1,13},{2,14},{3,15},{4,0},{5,1},{6,2},{7,3},{8,4},{9,5},{1... | collective-permute-start | bytes 2015240 | tf_op jit(solution)/shard_map/ppermute | solution.py:33
  30.8 24.7 %collective-permute-start.6 = (bf16[1312,256]{1,0:T(8,128)(2,1)S(1)}, bf16[1312,256]{1,0:T(8,128)(2,1)S(1)}, u32[]{:S(2)}, u32[]{:S(2)}) collective-permute-start(bf16[1312,256]{1,0:T(8,128)(2,1)S(1)} %collective-permute-done.1.refs_8_), channel_id=1, source_target_pairs={{0,8},{1,9},{2,10},{3,11},{4,12},{5,13},{6,14},{7,15},{8,0},{9,1},... | collective-permute-start | bytes 2015240 | tf_op jit(solution)/shard_map/ppermute | solution.py:33
  32.3 30.7 %collective-permute-start.2 = (bf16[1312,256]{1,0:T(8,128)(2,1)S(1)}, bf16[1312,256]{1,0:T(8,128)(2,1)}, u32[]{:S(2)}, u32[]{:S(2)}) collective-permute-start(bf16[1312,256]{1,0:T(8,128)(2,1)S(1)} %copy-done.10), channel_id=1, source_target_pairs={{0,2},{1,18},{2,0},{3,16},{4,6},{5,22},{6,4},{7,20},{8,10},{9,26},... | collective-permute-start | bytes 2015240 | tf_op jit(solution)/shard_map/ppermute | solution.py:33
  44.2 10.7 %collective-permute-start.3 = (bf16[2560,128]{1,0:T(8,128)(2,1)S(1)}, bf16[2560,128]{1,0:T(8,128)(2,1)S(1)}, u32[]{:S(2)}, u32[]{:S(2)}) collective-permute-start(bf16[2560,128]{1,0:T(8,128)(2,1)S(1)} %pad_maximum_fusion.refs_0_.mine), channel_id=1, source_target_pairs={{0,64},{1,65},{2,66},{3,67},{4,68},{5,69},{6,70},{7,71},{8,72},{9,... | collective-permute-start | bytes 1966088 | tf_op jit(solution)/shard_map/ppermute | solution.py:33
  54.9 32.2 %copy-start.7 = (bf16[2560,128]{1,0:T(8,128)(2,1)}, bf16[2560,128]{1,0:T(8,128)(2,1)S(1)}, u32[]{:S(2)}) copy-start(bf16[2560,128]{1,0:T(8,128)(2,1)S(1)} %collective-permute-done.3.refs_1_) | copy-start | bytes 1966084
  54.9 11.5 %collective-permute-start.10 = (bf16[2560,128]{1,0:T(8,128)(2,1)S(1)}, bf16[2560,128]{1,0:T(8,128)(2,1)S(1)}, u32[]{:S(2)}, u32[]{:S(2)}) collective-permute-start(bf16[2560,128]{1,0:T(8,128)(2,1)S(1)} %pad_maximum_fusion.refs_0_.mine), channel_id=1, source_target_pairs={{0,1},{1,0},{2,3},{3,2},{4,5},{5,4},{6,7},{7,6},{8,9},{9,8},{10,11... | collective-permute-start | bytes 1966088 | tf_op jit(solution)/shard_map/ppermute | solution.py:33
  54.9 32.2 %copy-start.4 = (bf16[1312,256]{1,0:T(8,128)(2,1)}, bf16[1312,256]{1,0:T(8,128)(2,1)S(1)}, u32[]{:S(2)}) copy-start(bf16[1312,256]{1,0:T(8,128)(2,1)S(1)} %collective-permute-done.4.refs_9_) | copy-start | bytes 2015236
  55.0 13.8 %collective-permute-start.11 = (bf16[2560,128]{1,0:T(8,128)(2,1)S(1)}, bf16[2560,128]{1,0:T(8,128)(2,1)S(1)}, u32[]{:S(2)}, u32[]{:S(2)}) collective-permute-start(bf16[2560,128]{1,0:T(8,128)(2,1)S(1)} %collective-permute-done.3.refs_1_), channel_id=1, source_target_pairs={{0,1},{1,0},{2,3},{3,2},{4,5},{5,4},{6,7},{7,6},{8,9},{9,8},{10,11... | collective-permute-start | bytes 1966088 | tf_op jit(solution)/shard_map/ppermute | solution.py:33
  55.5 31.7 %copy-start.5 = (bf16[1312,256]{1,0:T(8,128)(2,1)}, bf16[1312,256]{1,0:T(8,128)(2,1)S(1)}, u32[]{:S(2)}) copy-start(bf16[1312,256]{1,0:T(8,128)(2,1)S(1)} %collective-permute-done.5.refs_10_) | copy-start | bytes 2015236
  55.5 31.7 %copy-start.6 = (bf16[1312,256]{1,0:T(8,128)(2,1)}, bf16[1312,256]{1,0:T(8,128)(2,1)S(1)}, u32[]{:S(2)}) copy-start(bf16[1312,256]{1,0:T(8,128)(2,1)S(1)} %collective-permute-done.6.refs_11_) | copy-start | bytes 2015236
  63.0 23.6 %collective-permute-start.12 = (bf16[2560,128]{1,0:T(8,128)(2,1)S(1)}, bf16[2560,128]{1,0:T(8,128)(2,1)}, u32[]{:S(2)}, u32[]{:S(2)}) collective-permute-start(bf16[2560,128]{1,0:T(8,128)(2,1)S(1)} %pad_maximum_fusion.refs_0_.mine), channel_id=1, source_target_pairs={{0,192},{1,193},{2,194},{3,195},{4,196},{5,197},{6,198},{7,199},{8... | collective-permute-start | bytes 1966088 | tf_op jit(solution)/shard_map/ppermute | solution.py:33
  65.8 20.9 %collective-permute-start.14 = (bf16[2560,128]{1,0:T(8,128)(2,1)S(1)}, bf16[2560,128]{1,0:T(8,128)(2,1)}, u32[]{:S(2)}, u32[]{:S(2)}) collective-permute-start(bf16[2560,128]{1,0:T(8,128)(2,1)S(1)} %pad_maximum_fusion.refs_0_.mine), channel_id=1, source_target_pairs={{0,128},{1,129},{2,130},{3,131},{4,132},{5,133},{6,134},{7,135},{8... | collective-permute-start | bytes 1966088 | tf_op jit(solution)/shard_map/ppermute | solution.py:33
  66.1 25.1 %collective-permute-start.7 = (bf16[1312,256]{1,0:T(8,128)(2,1)}, bf16[1312,256]{1,0:T(8,128)(2,1)}, u32[]{:S(2)}, u32[]{:S(2)}) collective-permute-start(bf16[1312,256]{1,0:T(8,128)(2,1)} %collective-permute-done.2.refs_12_), channel_id=1, source_target_pairs={{0,4},{1,5},{2,6},{3,7},{4,8},{5,9},{6,10},{7,11},{8,12},{9,13},{1... | collective-permute-start | bytes 2015240 | tf_op jit(solution)/shard_map/ppermute | solution.py:33
  66.5 36.7 %copy-start.2 = (bf16[2560,128]{1,0:T(8,128)(2,1)}, bf16[2560,128]{1,0:T(8,128)(2,1)S(1)}, u32[]{:S(2)}) copy-start(bf16[2560,128]{1,0:T(8,128)(2,1)S(1)} %collective-permute-done.10.refs_4_.other) | copy-start | bytes 1966084
  66.5 24.8 %collective-permute-start.8 = (bf16[1312,256]{1,0:T(8,128)(2,1)}, bf16[1312,256]{1,0:T(8,128)(2,1)}, u32[]{:S(2)}, u32[]{:S(2)}) collective-permute-start(bf16[1312,256]{1,0:T(8,128)(2,1)} %collective-permute-done.2.refs_12_), channel_id=1, source_target_pairs={{0,12},{1,13},{2,14},{3,15},{4,0},{5,1},{6,2},{7,3},{8,4},{9,5},{1... | collective-permute-start | bytes 2015240 | tf_op jit(solution)/shard_map/ppermute | solution.py:33
  68.8 18.4 %copy-start.8 = (bf16[2560,128]{1,0:T(8,128)(2,1)}, bf16[2560,128]{1,0:T(8,128)(2,1)S(1)}, u32[]{:S(2)}) copy-start(bf16[2560,128]{1,0:T(8,128)(2,1)S(1)} %collective-permute-done.11.refs_5_) | copy-start | bytes 1966084
  68.8 22.4 %collective-permute-start.9 = (bf16[1312,256]{1,0:T(8,128)(2,1)}, bf16[1312,256]{1,0:T(8,128)(2,1)}, u32[]{:S(2)}, u32[]{:S(2)}) collective-permute-start(bf16[1312,256]{1,0:T(8,128)(2,1)} %collective-permute-done.2.refs_12_), channel_id=1, source_target_pairs={{0,8},{1,9},{2,10},{3,11},{4,12},{5,13},{6,14},{7,15},{8,0},{9,1},... | collective-permute-start | bytes 2015240 | tf_op jit(solution)/shard_map/ppermute | solution.py:33
  86.6 4.6 %collective-permute-start.13 = (bf16[2560,128]{1,0:T(8,128)(2,1)}, bf16[2560,128]{1,0:T(8,128)(2,1)}, u32[]{:S(2)}, u32[]{:S(2)}) collective-permute-start(bf16[2560,128]{1,0:T(8,128)(2,1)} %collective-permute-done.12.refs_2_), channel_id=1, source_target_pairs={{0,1},{1,0},{2,3},{3,2},{4,5},{5,4},{6,7},{7,6},{8,9},{9,8},{10,11... | collective-permute-start | bytes 1966088 | tf_op jit(solution)/shard_map/ppermute | solution.py:33
  86.7 4.6 %collective-permute-start.15 = (bf16[2560,128]{1,0:T(8,128)(2,1)}, bf16[2560,128]{1,0:T(8,128)(2,1)}, u32[]{:S(2)}, u32[]{:S(2)}) collective-permute-start(bf16[2560,128]{1,0:T(8,128)(2,1)} %collective-permute-done.14.refs_3_), channel_id=1, source_target_pairs={{0,1},{1,0},{2,3},{3,2},{4,5},{5,4},{6,7},{7,6},{8,9},{9,8},{10,11... | collective-permute-start | bytes 1966088 | tf_op jit(solution)/shard_map/ppermute | solution.py:33
  91.3 24.2 %collective-permute-start.16 = (bf16[640,256]{1,0:T(8,128)(2,1)S(1)}, bf16[640,256]{1,0:T(8,128)(2,1)S(1)}, u32[]{:S(2)}, u32[]{:S(2)}) collective-permute-start(bf16[640,256]{1,0:T(8,128)(2,1)S(1)} %bitcast.20), channel_id=1, source_target_pairs={{0,4},{1,5},{2,6},{3,7},{4,8},{5,9},{6,10},{7,11},{8,12},{9,13},{1... | collective-permute-start | bytes 983048 | tf_op jit(solution)/shard_map/ppermute | solution.py:33
  92.1 23.3 %collective-permute-start.17 = (bf16[640,256]{1,0:T(8,128)(2,1)S(1)}, bf16[640,256]{1,0:T(8,128)(2,1)S(1)}, u32[]{:S(2)}, u32[]{:S(2)}) collective-permute-start(bf16[640,256]{1,0:T(8,128)(2,1)S(1)} %bitcast.21), channel_id=1, source_target_pairs={{0,12},{1,13},{2,14},{3,15},{4,0},{5,1},{6,2},{7,3},{8,4},{9,5},{1... | collective-permute-start | bytes 983048 | tf_op jit(solution)/shard_map/ppermute | solution.py:33
  94.7 20.8 %collective-permute-start.18 = (bf16[640,256]{1,0:T(8,128)(2,1)S(1)}, bf16[640,256]{1,0:T(8,128)(2,1)S(1)}, u32[]{:S(2)}, u32[]{:S(2)}) collective-permute-start(bf16[640,256]{1,0:T(8,128)(2,1)S(1)} %bitcast.22), channel_id=1, source_target_pairs={{0,8},{1,9},{2,10},{3,11},{4,12},{5,13},{6,14},{7,15},{8,0},{9,1},... | collective-permute-start | bytes 983048 | tf_op jit(solution)/shard_map/ppermute | solution.py:33
  95.8 21.3 %collective-permute-start.19 = (bf16[640,256]{1,0:T(8,128)(2,1)S(1)}, bf16[640,256]{1,0:T(8,128)(2,1)S(1)}, u32[]{:S(2)}, u32[]{:S(2)}) collective-permute-start(bf16[640,256]{1,0:T(8,128)(2,1)S(1)} %bitcast.23), channel_id=1, source_target_pairs={{0,2},{1,3},{2,0},{3,1},{4,6},{5,7},{6,4},{7,5},{8,10},{9,11},{10,... | collective-permute-start | bytes 983048 | tf_op jit(solution)/shard_map/ppermute | solution.py:33
  101.8 13.5 %collective-permute-start.20 = (bf16[352,256]{1,0:T(8,128)(2,1)S(1)}, bf16[352,256]{1,0:T(8,128)(2,1)S(1)}, u32[]{:S(2)}, u32[]{:S(2)}) collective-permute-start(bf16[352,256]{1,0:T(8,128)(2,1)S(1)} %copy-done.9), channel_id=1, source_target_pairs={{0,2},{17,19},{34,32},{51,49},{68,70},{85,87},{102,100},{119,117},... | collective-permute-start | bytes 540680 | tf_op jit(solution)/shard_map/ppermute | solution.py:33
  117.1 16.1 %collective-permute-start.26 = (f32[1280,256]{1,0:T(8,128)}, f32[1280,256]{1,0:T(8,128)}, u32[]{:S(2)}, u32[]{:S(2)}) collective-permute-start(f32[1280,256]{1,0:T(8,128)} %apply_panel.1), channel_id=1, source_target_pairs={{1,17},{3,19},{5,21},{7,23},{9,25},{11,27},{13,29},{15,31},{16,0},... | collective-permute-start | bytes 3932168 | tf_op jit(solution)/shard_map/ppermute | solution.py:33
  119.5 0.7 collective-permute-start.24
  120.2 3.4 %collective-permute-start.25 = (bf16[352,256]{1,0:T(8,128)(2,1)S(1)}, bf16[352,256]{1,0:T(8,128)(2,1)S(1)}, u32[]{:S(2)}, u32[]{:S(2)}) collective-permute-start(bf16[352,256]{1,0:T(8,128)(2,1)S(1)} %add.106), channel_id=1, source_target_pairs={{0,8},{2,10},{4,12},{6,14},{17,25},{19,27},{21,29},{23,31},{32,40}... | collective-permute-start | bytes 540680 | tf_op jit(solution)/shard_map/ppermute | solution.py:33
  120.9 14.7 %collective-permute-start.21 = (bf16[640,256]{1,0:T(8,128)(2,1)S(1)}, bf16[640,256]{1,0:T(8,128)(2,1)S(1)}, u32[]{:S(2)}, u32[]{:S(2)}) collective-permute-start(bf16[640,256]{1,0:T(8,128)(2,1)S(1)} %collective-permute-done.19.refs_4_), channel_id=1, source_target_pairs={{0,4},{1,5},{2,6},{3,7},{4,8},{5,9},{6,10},{7,11},{8,12},{9,13},{1... | collective-permute-start | bytes 983048 | tf_op jit(solution)/shard_map/ppermute | solution.py:33
  121.0 14.6 %collective-permute-start.22 = (bf16[640,256]{1,0:T(8,128)(2,1)S(1)}, bf16[640,256]{1,0:T(8,128)(2,1)S(1)}, u32[]{:S(2)}, u32[]{:S(2)}) collective-permute-start(bf16[640,256]{1,0:T(8,128)(2,1)S(1)} %collective-permute-done.19.refs_4_), channel_id=1, source_target_pairs={{0,12},{1,13},{2,14},{3,15},{4,0},{5,1},{6,2},{7,3},{8,4},{9,5},{1... | collective-permute-start | bytes 983048 | tf_op jit(solution)/shard_map/ppermute | solution.py:33
  123.6 12.0 %collective-permute-start.23 = (bf16[640,256]{1,0:T(8,128)(2,1)S(1)}, bf16[640,256]{1,0:T(8,128)(2,1)S(1)}, u32[]{:S(2)}, u32[]{:S(2)}) collective-permute-start(bf16[640,256]{1,0:T(8,128)(2,1)S(1)} %collective-permute-done.19.refs_4_), channel_id=1, source_target_pairs={{0,8},{1,9},{2,10},{3,11},{4,12},{5,13},{6,14},{7,15},{8,0},{9,1},... | collective-permute-start | bytes 983048 | tf_op jit(solution)/shard_map/ppermute | solution.py:33
  135.6 8.8 %copy-start = (s32[5]{0:T(128)S(1)}, s32[5]{0:T(128)}, u32[]{:S(2)}) copy-start(s32[5]{0:T(128)} %stack.23.place) | copy-start | bytes 64
  135.6 7.6 %collective-permute-start.27 = (bf16[1280,256]{1,0:T(8,128)(2,1)S(1)}, bf16[1280,256]{1,0:T(8,128)(2,1)}, u32[]{:S(2)}, u32[]{:S(2)}) collective-permute-start(bf16[1280,256]{1,0:T(8,128)(2,1)S(1)} %add_convert_fusion), channel_id=1, source_target_pairs={{0,1},{1,0},{2,3},{3,2},{4,5},{5,4},{6,7},{7,6},{8,9},{9,8},{10,11... | collective-permute-start | bytes 1966088 | tf_op jit(solution)/shard_map/ppermute | solution.py:33
  147.2 11.4 %collective-permute-start.28 = (f32[256,256]{1,0:T(8,128)}, f32[256,256]{1,0:T(8,128)S(1)}, u32[]{:S(2)}, u32[]{:S(2)}) collective-permute-start(f32[256,256]{1,0:T(8,128)} %get-tuple-element.36), channel_id=1, source_target_pairs={{0,64},{1,65},{2,66},{3,67},{4,68},{5,69},{6,70},{7,71},{8,72},{9,... | collective-permute-start | bytes 786440 | tf_op jit(solution)/shard_map/ppermute | solution.py:33
  150.6 15.1 %collective-permute-start.29 = (f32[256,256]{1,0:T(8,128)S(1)}, f32[256,256]{1,0:T(8,128)S(1)}, u32[]{:S(2)}, u32[]{:S(2)}) collective-permute-start(f32[256,256]{1,0:T(8,128)S(1)} %get-tuple-element.37), channel_id=1, source_target_pairs={{0,128},{1,129},{2,130},{3,131},{4,132},{5,133},{6,134},{7,135},{8... | collective-permute-start | bytes 786440 | tf_op jit(solution)/shard_map/ppermute | solution.py:33
  153.5 12.2 %collective-permute-start.30 = (f32[256,256]{1,0:T(8,128)S(1)}, f32[256,256]{1,0:T(8,128)S(1)}, u32[]{:S(2)}, u32[]{:S(2)}) collective-permute-start(f32[256,256]{1,0:T(8,128)S(1)} %get-tuple-element.38), channel_id=1, source_target_pairs={{0,192},{1,193},{2,194},{3,195},{4,196},{5,197},{6,198},{7,199},{8... | collective-permute-start | bytes 786440 | tf_op jit(solution)/shard_map/ppermute | solution.py:33
  166.2 5.9 %collective-permute-start.31 = (f32[128,128]{1,0:T(8,128)S(1)}, f32[128,128]{1,0:T(8,128)S(1)}, u32[]{:S(2)}, u32[]{:S(2)}) collective-permute-start(f32[128,128]{1,0:T(8,128)S(1)} %bitcast.31), channel_id=1, source_target_pairs={{0,0},{1,16},{2,2},{3,18},{4,4},{5,20},{6,6},{7,22},{8,8},{9,24},{... | collective-permute-start | bytes 196616 | tf_op jit(solution)/shard_map/ppermute | solution.py:33
  168.1 4.0 %collective-permute-start.32 = (f32[128,128]{1,0:T(8,128)S(1)}, f32[128,128]{1,0:T(8,128)S(1)}, u32[]{:S(2)}, u32[]{:S(2)}) collective-permute-start(f32[128,128]{1,0:T(8,128)S(1)} %bitcast.30), channel_id=1, source_target_pairs={{0,1},{1,17},{2,3},{3,19},{4,5},{5,21},{6,7},{7,23},{8,9},{9,25},{... | collective-permute-start | bytes 196616 | tf_op jit(solution)/shard_map/ppermute | solution.py:33
  168.2 6.4 %collective-permute-start.33 = (f32[128,128]{1,0:T(8,128)S(1)}, f32[128,128]{1,0:T(8,128)S(1)}, u32[]{:S(2)}, u32[]{:S(2)}) collective-permute-start(f32[128,128]{1,0:T(8,128)S(1)} %bitcast.29), channel_id=1, source_target_pairs={{0,32},{1,48},{2,34},{3,50},{4,36},{5,52},{6,38},{7,54},{8,40},{9,... | collective-permute-start | bytes 196616 | tf_op jit(solution)/shard_map/ppermute | solution.py:33
  168.3 9.5 %collective-permute-start.34 = (f32[128,128]{1,0:T(8,128)S(1)}, f32[128,128]{1,0:T(8,128)S(1)}, u32[]{:S(2)}, u32[]{:S(2)}) collective-permute-start(f32[128,128]{1,0:T(8,128)S(1)} %bitcast.28), channel_id=1, source_target_pairs={{0,33},{1,49},{2,35},{3,51},{4,37},{5,53},{6,39},{7,55},{8,41},{9,... | collective-permute-start | bytes 196616 | tf_op jit(solution)/shard_map/ppermute | solution.py:33

commit v4 on v3

--- a/solution.py
+++ b/solution.py
@@ -196,7 +196,7 @@
     )(place, *p_pieces, *a_pieces)
 
 
-def last_kernel(place, mine, other, five, out, panel, numbers, offsets, sems):
+def last_kernel(place, mine, other, five, before, out, panel, numbers, offsets, sems):
     c = place[4]
     copies = []
     for n, src in enumerate((mine, other)):
@@ -209,20 +209,18 @@
     for copy in copies + [scalars]:
         copy.wait()
 
-    @pl.loop(0, 20)
-    def _(t):
+    for t in range(20):
         rows = pl.ds(pl.multiple_of(offsets[t, 4] * BR, BR), BR)
         block = jnp.concatenate([panel[0, rows, :], panel[1, rows, :]], axis=1)
-        nothing = jnp.zeros_like(block)
-        right = jnp.concatenate([jnp.where(t // 5 == q, block, nothing) for q in range(4)], axis=0)
-        out[pl.ds(pl.multiple_of(t * BR, BR), BR), :] = jnp.dot(
-            five[pl.ds(pl.multiple_of(lax.rem(t, 5) * BR, BR), BR), :],
-            right,
+        extra = jnp.dot(
+            five[pl.ds(t % 5 * BR, BR), pl.ds(t // 5 * BR, BR)],
+            block,
             preferred_element_type=jnp.float32,
         )
-
-
-def apply_last(place, mine, other, five):
+        out[pl.ds(t * BR, BR), :] = before[pl.ds(t * BR, BR), :] + extra
+
+
+def apply_last(place, mine, other, five, before):
     anywhere = pl.BlockSpec(memory_space=pl.ANY)
     inside = pl.BlockSpec(memory_space=pltpu.VMEM)
     return pl.pallas_call(
@@ -231,7 +229,7 @@
         grid_spec=pltpu.PrefetchScalarGridSpec(
             num_scalar_prefetch=1,
             grid=(),
-            in_specs=[anywhere, anywhere, inside],
+            in_specs=[anywhere, anywhere, inside, inside],
             out_specs=inside,
             scratch_shapes=[
                 pltpu.VMEM((2, 1280, 128), jnp.bfloat16),
@@ -244,15 +242,15 @@
             flops=2 * 1280 * 256 * 256, bytes_accessed=2 * 2**20, transcendentals=0
         ),
         name="apply_last",
-    )(place, mine, other, five)
+    )(place, mine, other, five, before)
 
 
 def project_kernel(place, *refs):
     t_refs = refs[:8]
-    prol = refs[8]
-    outs = refs[9:13]
-    left, sems = refs[13:]
-    y, x, h = place[0], place[2], place[3]
+    mine, twin = refs[8:10]
+    outs = refs[10:14]
+    left, prol, sems = refs[14:]
+    y, z, x, h, c = (place[i] for i in range(5))
     copies = []
     for i, k in enumerate(STEPS):
         m = lax.rem(x + 8 - k - y, 4)
@@ -261,6 +259,7 @@
             copy = pltpu.make_async_copy(src, dst, sems.at[2 * i + f])
             copy.start()
             copies.append(copy)
+    prol[...] = jnp.where(c == lax.rem(z, 2), mine[...], twin[...])
     for copy in copies:
         copy.wait()
     for m in range(4):
@@ -275,7 +274,7 @@
             outs[m][pl.ds(k1 * 128, 128), :] = total
 
 
-def project(place, t_pieces, prol):
+def project(place, t_pieces, mine, twin):
     anywhere = pl.BlockSpec(memory_space=pl.ANY)
     inside = pl.BlockSpec(memory_space=pltpu.VMEM)
     out = jax.ShapeDtypeStruct((256, 256), jnp.float32)
@@ -285,10 +284,11 @@
         grid_spec=pltpu.PrefetchScalarGridSpec(
             num_scalar_prefetch=1,
             grid=(),
-            in_specs=[anywhere] * 8 + [inside],
+            in_specs=[anywhere] * 8 + [inside] * 2,
             out_specs=(inside,) * 4,
             scratch_shapes=[
                 pltpu.VMEM((4, 2, 640, 256), jnp.bfloat16),
+                pltpu.VMEM((1280, 256), jnp.bfloat16),
                 pltpu.SemaphoreType.DMA((8,)),
             ],
         ),
@@ -297,7 +297,7 @@
             flops=2 * 1280 * 1024 * 256, bytes_accessed=4 * 2**20, transcendentals=0
         ),
         name="project",
-    )(place, *t_pieces, prol)
+    )(place, *t_pieces, mine, twin)
 
 
 def per_device(a_vals, a_cols, a_count, p_vals, p_mask):
@@ -344,12 +344,12 @@
     t_far = [t_far] + [move(t_far, shift_x(k)) for k in (1, 3, 2)]
     five = five + move(five, next_x)
     five = five + move(five, over_x)
-    extra = apply_last(place, p_mine[0], p_other[0], five)
-    prolonged = (product + extra + move(product, flip_z0)).astype(jnp.bfloat16)
+    total = apply_last(place, p_mine[0], p_other[0], five, product)
+    prolonged = (total + move(product, flip_z0)).astype(jnp.bfloat16)
     (prolonged,) = after((prolonged,), *t_near, *t_far)
-    prolonged = jnp.where(c == z % 2, prolonged, move(prolonged, flip_c))
-
-    blocks = project(place, t_near + t_far, prolonged)
+    twin = move(prolonged, flip_c)
+
+    blocks = project(place, t_near + t_far, prolonged, twin)
     summed = blocks[0]
     for m in (1, 2, 3):
         summed = summed + move(blocks[m], shift_y(m))

time: 179 us -> 176 us (0.983)
  Pallas kernels: 25.3 us -> 23.1 us
  waiting for transfers between devices: 70.7 us -> 72.6 us
    pallas_call x1, Pallas kernels: 6.94 us -> 4.6 us  [apply_last(): pl.pallas_call(last_kernel, out_shape=jax.ShapeDtypeStruct((1280, 256), j...]
    ppermute x35, waiting for transfers between devices: 70.7 us -> 72.6 us  [move(): return lax.ppermute(array, AXES, pairs)]
  transfers between devices with their start and end apart: 35 -> 35, of which waited for: 13 -> 13; matrix products, arithmetic and copies ran while one was open for 5% -> 5% of each run, Pallas kernels for 13% -> 11%
where the time goes in v4:
time: 176 us; the launch traced here: 175 us
  waiting for transfers between devices  72.6 us (41%)
  starting transfers between devices  67.4 us (38%)
  Pallas kernels  23.1 us (13%)
  local copies, waits for them, and re-layouts  6.21 us (4%)
  other arithmetic  5.72 us (3%)
    ppermute x35, waiting for transfers between devices, move(): return lax.ppermute(array, AXES, pairs)  72.6 us
    ppermute x35, starting transfers between devices, move(): return lax.ppermute(array, AXES, pairs)  67.4 us
    pallas_call x1, Pallas kernels, apply_panel(): pl.pallas_call(apply_kernel, out_shape=jax.ShapeDtypeStruct((1280, 256),...  12.2 us
    pallas_call x1, Pallas kernels, apply_last(): pl.pallas_call(last_kernel, out_shape=jax.ShapeDtypeStruct((1280, 256), j...  4.6 us
    reshape x2, local copies, waits for them, and re-layouts, per_device(): a_vals.reshape(20, 5, BR, BR)  4.23 us
  transfers between devices with their start and end apart: 35, of which 13 were waited for; matrix products, arithmetic and copies ran while one was open for 5% of the time, Pallas kernels for 11%

profile of v4, /device:TPU:1, one launch (start us, length us, event | category | flops | bytes accessed | tf_op | source)
XLA Modules:
  0.0 175.3 jit_solution(13092696067097889807)
XLA Ops:
  0.0 0.7 convert_bitcast_fusion
  0.7 1.1 broadcast_multiply_fusion
  1.7 3.9 %collective-permute-start = (bf16[1280,128]{1,0:T(8,128)(2,1)S(1)}, bf16[1280,128]{1,0:T(8,128)(2,1)S(1)}, u32[]{:S(2)}, u32[]{:S(2)}) collective-permute-start(bf16[1280,128]{1,0:T(8,128)(2,1)S(1)} %bitcast.25), channel_id=1, source_target_pairs={{0,32},{1,33},{2,34},{3,35},{4,36},{5,37},{6,38},{7,39},{8,40},{9,... | collective-permute-start | bytes 983048 | tf_op jit(solution)/shard_map/ppermute | solution.py:33
  5.6 0.8 copy.13
  6.4 0.6 broadcast_subtract_fusion.cols
  7.0 2.9 %reshape.44 = bf16[20,5,64,64]{3,2,0,1:T(8,128)(2,1)S(1)} reshape(bf16[20,5,4096]{2,0,1:T(8,128)(2,1)} %param.5) | data formatting | bytes 1638400 | tf_op jit(solution)/shard_map/reshape | solution.py:315
  9.9 1.3 copy.15.blocks
  11.2 3.3 %pack.1 = (bf16[1312,256]{1,0:T(8,128)(2,1)}, bf16[352,256]{1,0:T(8,128)(2,1)}) custom-call(s32[20]{0:T(128)} %bitcast.32, s32[1]{0:T(128)} %bitcast.10.diagonal, bf16[20,5,64,64]{3,2,1,0:T(8,128)(2,1)} %copy.15.blocks, s32[20,5]{1,0:T(8,128)} %broadcast_subtract_fusion.cols), custom_call_target="tpu_custom_call" | custom-call | bytes 3145728 | tf_op jit(solution)/shard_map/pack/pallas_call | solution.py:100
  14.5 4.5 %collective-permute-start.1 = (bf16[1312,256]{1,0:T(8,128)(2,1)}, bf16[1312,256]{1,0:T(8,128)(2,1)S(1)}, u32[]{:S(2)}, u32[]{:S(2)}) collective-permute-start(bf16[1312,256]{1,0:T(8,128)(2,1)} %get-tuple-element.24), channel_id=1, source_target_pairs={{0,0},{1,16},{2,2},{3,18},{4,4},{5,20},{6,6},{7,22},{8,8},{9,24},{... | collective-permute-start | bytes 2015240 | tf_op jit(solution)/shard_map/ppermute | solution.py:33
  19.5 8.7 %collective-permute-done.1.refs_8_ = bf16[1312,256]{1,0:T(8,128)(2,1)S(1)} collective-permute-done((bf16[1312,256]{1,0:T(8,128)(2,1)}, bf16[1312,256]{1,0:T(8,128)(2,1)S(1)}, u32[]{:S(2)}, u32[]{:S(2)}) %collective-permute-start.1) | collective-permute-done | bytes 671776 | tf_op jit(solution)/shard_map/ppermute | solution.py:33
  28.1 1.2 collective-permute-start.4
  29.3 1.5 collective-permute-start.5
  30.8 1.5 collective-permute-start.6
  32.3 11.9 %collective-permute-start.2 = (bf16[1312,256]{1,0:T(8,128)(2,1)S(1)}, bf16[1312,256]{1,0:T(8,128)(2,1)}, u32[]{:S(2)}, u32[]{:S(2)}) collective-permute-start(bf16[1312,256]{1,0:T(8,128)(2,1)S(1)} %copy-done.10), channel_id=1, source_target_pairs={{0,2},{1,18},{2,0},{3,16},{4,6},{5,22},{6,4},{7,20},{8,10},{9,26},... | collective-permute-start | bytes 2015240 | tf_op jit(solution)/shard_map/ppermute | solution.py:33
  44.2 1.3 collective-permute-start.3
  45.5 9.4 %collective-permute-done.3.refs_1_ = bf16[2560,128]{1,0:T(8,128)(2,1)S(1)} collective-permute-done((bf16[2560,128]{1,0:T(8,128)(2,1)S(1)}, bf16[2560,128]{1,0:T(8,128)(2,1)S(1)}, u32[]{:S(2)}, u32[]{:S(2)}) %collective-permute-start.3) | collective-permute-done | bytes 655392 | tf_op jit(solution)/shard_map/ppermute | solution.py:33
  55.5 7.6 %collective-permute-done.2.refs_12_ = bf16[1312,256]{1,0:T(8,128)(2,1)} collective-permute-done((bf16[1312,256]{1,0:T(8,128)(2,1)S(1)}, bf16[1312,256]{1,0:T(8,128)(2,1)}, u32[]{:S(2)}, u32[]{:S(2)}) %collective-permute-start.2) | collective-permute-done | bytes 671776 | tf_op jit(solution)/shard_map/ppermute | solution.py:33
  63.0 2.7 %collective-permute-start.12 = (bf16[2560,128]{1,0:T(8,128)(2,1)S(1)}, bf16[2560,128]{1,0:T(8,128)(2,1)}, u32[]{:S(2)}, u32[]{:S(2)}) collective-permute-start(bf16[2560,128]{1,0:T(8,128)(2,1)S(1)} %pad_maximum_fusion.refs_0_.mine), channel_id=1, source_target_pairs={{0,192},{1,193},{2,194},{3,195},{4,196},{5,197},{6,198},{7,199},{8... | collective-permute-start | bytes 1966088 | tf_op jit(solution)/shard_map/ppermute | solution.py:33
  66.5 2.3 %collective-permute-start.8 = (bf16[1312,256]{1,0:T(8,128)(2,1)}, bf16[1312,256]{1,0:T(8,128)(2,1)}, u32[]{:S(2)}, u32[]{:S(2)}) collective-permute-start(bf16[1312,256]{1,0:T(8,128)(2,1)} %collective-permute-done.2.refs_12_), channel_id=1, source_target_pairs={{0,12},{1,13},{2,14},{3,15},{4,0},{5,1},{6,2},{7,3},{8,4},{9,5},{1... | collective-permute-start | bytes 2015240 | tf_op jit(solution)/shard_map/ppermute | solution.py:33
  69.1 17.6 %collective-permute-done.12.refs_2_ = bf16[2560,128]{1,0:T(8,128)(2,1)} collective-permute-done((bf16[2560,128]{1,0:T(8,128)(2,1)S(1)}, bf16[2560,128]{1,0:T(8,128)(2,1)}, u32[]{:S(2)}, u32[]{:S(2)}) %collective-permute-start.12) | collective-permute-done | bytes 655392 | tf_op jit(solution)/shard_map/ppermute | solution.py:33
  87.4 3.8 %collective-permute-done.7.refs_13_ = bf16[1312,256]{1,0:T(8,128)(2,1)} collective-permute-done((bf16[1312,256]{1,0:T(8,128)(2,1)}, bf16[1312,256]{1,0:T(8,128)(2,1)}, u32[]{:S(2)}, u32[]{:S(2)}) %collective-permute-start.7) | collective-permute-done | bytes 671776 | tf_op jit(solution)/shard_map/ppermute | solution.py:33
  91.8 2.8 %collective-permute-start.17 = (bf16[640,256]{1,0:T(8,128)(2,1)S(1)}, bf16[640,256]{1,0:T(8,128)(2,1)S(1)}, u32[]{:S(2)}, u32[]{:S(2)}) collective-permute-start(bf16[640,256]{1,0:T(8,128)(2,1)S(1)} %bitcast.21), channel_id=1, source_target_pairs={{0,12},{1,13},{2,14},{3,15},{4,0},{5,1},{6,2},{7,3},{8,4},{9,5},{1... | collective-permute-start | bytes 983048 | tf_op jit(solution)/shard_map/ppermute | solution.py:33
  94.7 1.1 collective-permute-start.18
  95.8 6.0 %collective-permute-start.19 = (bf16[640,256]{1,0:T(8,128)(2,1)S(1)}, bf16[640,256]{1,0:T(8,128)(2,1)S(1)}, u32[]{:S(2)}, u32[]{:S(2)}) collective-permute-start(bf16[640,256]{1,0:T(8,128)(2,1)S(1)} %bitcast.23), channel_id=1, source_target_pairs={{0,2},{1,3},{2,0},{3,1},{4,6},{5,7},{6,4},{7,5},{8,10},{9,11},{10,... | collective-permute-start | bytes 983048 | tf_op jit(solution)/shard_map/ppermute | solution.py:33
  101.8 0.7 collective-permute-start.20
  102.6 0.6 stack.23.place
  103.2 12.2 %apply_panel.1.before = f32[1280,256]{1,0:T(8,128)} custom-call(s32[5]{0:T(128)} %stack.23.place, bf16[2560,128]{1,0:T(8,128)(2,1)} %copy-done.1, bf16[2560,128]{1,0:T(8,128)(2,1)} %copy-done.7, bf16[2560,128]{1,0:T(8,128)(2,1)} %collective-permute-done.12.refs_2_, bf16[2560,128]{1,0:T(8,128)(2,1)} %collective-permute-done.14.refs_3_, ...), custom_call_target="tpu_custom_call" | custom-call | flops 1342177280 | bytes 12582912 | tf_op jit(solution)/shard_map/apply_panel/pallas_call | solution.py:174
  115.5 1.6 collective-permute-done.19.refs_4_
  117.1 2.3 %collective-permute-start.26 = (f32[1280,256]{1,0:T(8,128)}, f32[1280,256]{1,0:T(8,128)}, u32[]{:S(2)}, u32[]{:S(2)}) collective-permute-start(f32[1280,256]{1,0:T(8,128)} %apply_panel.1.before), channel_id=1, source_target_pairs={{1,17},{3,19},{5,21},{7,23},{9,25},{11,27},{13,29},{15,31},{16,0},... | collective-permute-start | bytes 3932168 | tf_op jit(solution)/shard_map/ppermute | solution.py:33
  119.4 0.7 collective-permute-start.24
  120.2 0.7 collective-permute-start.25
  120.9 2.7 %collective-permute-start.22 = (bf16[640,256]{1,0:T(8,128)(2,1)S(1)}, bf16[640,256]{1,0:T(8,128)(2,1)S(1)}, u32[]{:S(2)}, u32[]{:S(2)}) collective-permute-start(bf16[640,256]{1,0:T(8,128)(2,1)S(1)} %collective-permute-done.19.refs_4_), channel_id=1, source_target_pairs={{0,12},{1,13},{2,14},{3,15},{4,0},{5,1},{6,2},{7,3},{8,4},{9,5},{1... | collective-permute-start | bytes 983048 | tf_op jit(solution)/shard_map/ppermute | solution.py:33
  123.6 0.7 add.102.five
  124.3 4.6 %apply_last.1 = f32[1280,256]{1,0:T(8,128)} custom-call(s32[5]{0:T(128)} %stack.23.place, bf16[2560,128]{1,0:T(8,128)(2,1)} %copy-done.1, bf16[2560,128]{1,0:T(8,128)(2,1)} %copy-done.2, bf16[352,256]{1,0:T(8,128)(2,1)} %add.102.five, f32[1280,256]{1,0:T(8,128)} %apply_panel.1.before), custom_call_target="tpu_custom_call" | custom-call | flops 167772160 | bytes 2097152 | tf_op jit(solution)/shard_map/apply_last/pallas_call | solution.py:226
  128.9 4.3 %collective-permute-done.26 = f32[1280,256]{1,0:T(8,128)} collective-permute-done((f32[1280,256]{1,0:T(8,128)}, f32[1280,256]{1,0:T(8,128)}, u32[]{:S(2)}, u32[]{:S(2)}) %collective-permute-start.26) | collective-permute-done | bytes 1310752 | tf_op jit(solution)/shard_map/ppermute | solution.py:33
  133.2 1.8 %add_convert_fusion.refs_8_ = bf16[1280,256]{1,0:T(8,128)(2,1)S(1)} fusion(f32[1280,256]{1,0:T(8,128)} %apply_last.1, f32[1280,256]{1,0:T(8,128)} %collective-permute-done.26), kind=kLoop, calls=%fused_computation | loop fusion | flops 655360 | bytes 3276800 | tf_op jit(solution)/shard_map/convert_element_type | solution.py:348
  135.1 5.5 %collective-permute-start.27 = (bf16[1280,256]{1,0:T(8,128)(2,1)S(1)}, bf16[1280,256]{1,0:T(8,128)(2,1)S(1)}, u32[]{:S(2)}, u32[]{:S(2)}) collective-permute-start(bf16[1280,256]{1,0:T(8,128)(2,1)S(1)} %add_convert_fusion.refs_8_), channel_id=1, source_target_pairs={{0,1},{1,0},{2,3},{3,2},{4,5},{5,4},{6,7},{7,6},{8,9},{9,8},{10,11... | collective-permute-start | bytes 1966088 | tf_op jit(solution)/shard_map/ppermute | solution.py:33
  140.6 1.7 collective-permute-done.27.refs_9_
  142.3 2.9 %project.1 = (f32[256,256]{1,0:T(8,128)S(1)}, f32[256,256]{1,0:T(8,128)}, f32[256,256]{1,0:T(8,128)S(1)}, f32[256,256]{1,0:T(8,128)S(1)}) custom-call(s32[5]{0:T(128)S(1)} %copy-done, bf16[640,256]{1,0:T(8,128)(2,1)S(1)} %bitcast.24, bf16[640,256]{1,0:T(8,128)(2,1)S(1)} %collective-permute-done.16.refs_1_, ...), custom_call_target="tpu_custom_call" | custom-call | flops 671088640 | bytes 4194304 | tf_op jit(solution)/shard_map/project/pallas_call | solution.py:281
  145.3 1.4 collective-permute-start.28
  146.7 4.0 %collective-permute-start.29 = (f32[256,256]{1,0:T(8,128)S(1)}, f32[256,256]{1,0:T(8,128)S(1)}, u32[]{:S(2)}, u32[]{:S(2)}) collective-permute-start(f32[256,256]{1,0:T(8,128)S(1)} %get-tuple-element.37), channel_id=1, source_target_pairs={{0,128},{1,129},{2,130},{3,131},{4,132},{5,133},{6,134},{7,135},{8... | collective-permute-start | bytes 786440 | tf_op jit(solution)/shard_map/ppermute | solution.py:33
  150.7 5.4 %collective-permute-done.28 = f32[256,256]{1,0:T(8,128)S(1)} collective-permute-done((f32[256,256]{1,0:T(8,128)}, f32[256,256]{1,0:T(8,128)S(1)}, u32[]{:S(2)}, u32[]{:S(2)}) %collective-permute-start.28) | collective-permute-done | bytes 262176 | tf_op jit(solution)/shard_map/ppermute | solution.py:33
  156.1 6.5 %collective-permute-done.29 = f32[256,256]{1,0:T(8,128)S(1)} collective-permute-done((f32[256,256]{1,0:T(8,128)S(1)}, f32[256,256]{1,0:T(8,128)S(1)}, u32[]{:S(2)}, u32[]{:S(2)}) %collective-permute-start.29) | collective-permute-done | bytes 262176 | tf_op jit(solution)/shard_map/ppermute | solution.py:33
  163.1 3.1 %collective-permute-start.31 = (f32[128,128]{1,0:T(8,128)S(1)}, f32[128,128]{1,0:T(8,128)S(1)}, u32[]{:S(2)}, u32[]{:S(2)}) collective-permute-start(f32[128,128]{1,0:T(8,128)S(1)} %bitcast.31), channel_id=1, source_target_pairs={{0,0},{1,16},{2,2},{3,18},{4,4},{5,20},{6,6},{7,22},{8,8},{9,24},{... | collective-permute-start | bytes 196616 | tf_op jit(solution)/shard_map/ppermute | solution.py:33
  166.3 2.7 %collective-permute-start.34 = (f32[128,128]{1,0:T(8,128)S(1)}, f32[128,128]{1,0:T(8,128)S(1)}, u32[]{:S(2)}, u32[]{:S(2)}) collective-permute-start(f32[128,128]{1,0:T(8,128)S(1)} %bitcast.28), channel_id=1, source_target_pairs={{0,33},{1,49},{2,35},{3,51},{4,37},{5,53},{6,39},{7,55},{8,41},{9,... | collective-permute-start | bytes 196616 | tf_op jit(solution)/shard_map/ppermute | solution.py:33
  169.0 3.1 %collective-permute-done.33 = f32[128,128]{1,0:T(8,128)S(1)} collective-permute-done((f32[128,128]{1,0:T(8,128)S(1)}, f32[128,128]{1,0:T(8,128)S(1)}, u32[]{:S(2)}, u32[]{:S(2)}) %collective-permute-start.33) | collective-permute-done | bytes 65568 | tf_op jit(solution)/shard_map/ppermute | solution.py:33
  172.2 2.5 %collective-permute-done.34 = f32[128,128]{1,0:T(8,128)S(1)} collective-permute-done((f32[128,128]{1,0:T(8,128)S(1)}, f32[128,128]{1,0:T(8,128)S(1)}, u32[]{:S(2)}, u32[]{:S(2)}) %collective-permute-start.34) | collective-permute-done | bytes 65568 | tf_op jit(solution)/shard_map/ppermute | solution.py:33
  174.7 0.6 add_add_fusion.1
  (65 shorter events, 4.1 us)
Async XLA Ops:
  1.7 17.7 %collective-permute-start = (bf16[1280,128]{1,0:T(8,128)(2,1)S(1)}, bf16[1280,128]{1,0:T(8,128)(2,1)S(1)}, u32[]{:S(2)}, u32[]{:S(2)}) collective-permute-start(bf16[1280,128]{1,0:T(8,128)(2,1)S(1)} %bitcast.25), channel_id=1, source_target_pairs={{0,32},{1,33},{2,34},{3,35},{4,36},{5,37},{6,38},{7,39},{8,40},{9,... | collective-permute-start | bytes 983048 | tf_op jit(solution)/shard_map/ppermute | solution.py:33
  14.5 17.8 %copy-start.10 = (bf16[1312,256]{1,0:T(8,128)(2,1)S(1)}, bf16[1312,256]{1,0:T(8,128)(2,1)}, u32[]{:S(2)}) copy-start(bf16[1312,256]{1,0:T(8,128)(2,1)} %get-tuple-element.24) | copy-start | bytes 2015236
  14.5 87.3 %copy-start.9 = (bf16[352,256]{1,0:T(8,128)(2,1)S(1)}, bf16[352,256]{1,0:T(8,128)(2,1)}, u32[]{:S(2)}) copy-start(bf16[352,256]{1,0:T(8,128)(2,1)} %get-tuple-element.30) | copy-start | bytes 540676
  14.5 13.6 %collective-permute-start.1 = (bf16[1312,256]{1,0:T(8,128)(2,1)}, bf16[1312,256]{1,0:T(8,128)(2,1)S(1)}, u32[]{:S(2)}, u32[]{:S(2)}) collective-permute-start(bf16[1312,256]{1,0:T(8,128)(2,1)} %get-tuple-element.24), channel_id=1, source_target_pairs={{0,0},{1,16},{2,2},{3,18},{4,4},{5,20},{6,6},{7,22},{8,8},{9,24},{... | collective-permute-start | bytes 2015240 | tf_op jit(solution)/shard_map/ppermute | solution.py:33
  19.5 83.7 %copy-start.1 = (bf16[2560,128]{1,0:T(8,128)(2,1)}, bf16[2560,128]{1,0:T(8,128)(2,1)S(1)}, u32[]{:S(2)}) copy-start(bf16[2560,128]{1,0:T(8,128)(2,1)S(1)} %pad_maximum_fusion.refs_0_.mine) | copy-start | bytes 1966084
  28.1 59.0 %copy-start.3 = (bf16[1312,256]{1,0:T(8,128)(2,1)}, bf16[1312,256]{1,0:T(8,128)(2,1)S(1)}, u32[]{:S(2)}) copy-start(bf16[1312,256]{1,0:T(8,128)(2,1)S(1)} %collective-permute-done.1.refs_8_) | copy-start | bytes 2015236
  28.1 26.8 %collective-permute-start.4 = (bf16[1312,256]{1,0:T(8,128)(2,1)S(1)}, bf16[1312,256]{1,0:T(8,128)(2,1)S(1)}, u32[]{:S(2)}, u32[]{:S(2)}) collective-permute-start(bf16[1312,256]{1,0:T(8,128)(2,1)S(1)} %collective-permute-done.1.refs_8_), channel_id=1, source_target_pairs={{0,4},{1,5},{2,6},{3,7},{4,8},{5,9},{6,10},{7,11},{8,12},{9,13},{1... | collective-permute-start | bytes 2015240 | tf_op jit(solution)/shard_map/ppermute | solution.py:33
  29.3 26.1 %collective-permute-start.5 = (bf16[1312,256]{1,0:T(8,128)(2,1)S(1)}, bf16[1312,256]{1,0:T(8,128)(2,1)S(1)}, u32[]{:S(2)}, u32[]{:S(2)}) collective-permute-start(bf16[1312,256]{1,0:T(8,128)(2,1)S(1)} %collective-permute-done.1.refs_8_), channel_id=1, source_target_pairs={{0,12},{1,13},{2,14},{3,15},{4,0},{5,1},{6,2},{7,3},{8,4},{9,5},{1... | collective-permute-start | bytes 2015240 | tf_op jit(solution)/shard_map/ppermute | solution.py:33
  30.8 24.7 %collective-permute-start.6 = (bf16[1312,256]{1,0:T(8,128)(2,1)S(1)}, bf16[1312,256]{1,0:T(8,128)(2,1)S(1)}, u32[]{:S(2)}, u32[]{:S(2)}) collective-permute-start(bf16[1312,256]{1,0:T(8,128)(2,1)S(1)} %collective-permute-done.1.refs_8_), channel_id=1, source_target_pairs={{0,8},{1,9},{2,10},{3,11},{4,12},{5,13},{6,14},{7,15},{8,0},{9,1},... | collective-permute-start | bytes 2015240 | tf_op jit(solution)/shard_map/ppermute | solution.py:33
  32.3 30.7 %collective-permute-start.2 = (bf16[1312,256]{1,0:T(8,128)(2,1)S(1)}, bf16[1312,256]{1,0:T(8,128)(2,1)}, u32[]{:S(2)}, u32[]{:S(2)}) collective-permute-start(bf16[1312,256]{1,0:T(8,128)(2,1)S(1)} %copy-done.10), channel_id=1, source_target_pairs={{0,2},{1,18},{2,0},{3,16},{4,6},{5,22},{6,4},{7,20},{8,10},{9,26},... | collective-permute-start | bytes 2015240 | tf_op jit(solution)/shard_map/ppermute | solution.py:33
  44.2 10.7 %collective-permute-start.3 = (bf16[2560,128]{1,0:T(8,128)(2,1)S(1)}, bf16[2560,128]{1,0:T(8,128)(2,1)S(1)}, u32[]{:S(2)}, u32[]{:S(2)}) collective-permute-start(bf16[2560,128]{1,0:T(8,128)(2,1)S(1)} %pad_maximum_fusion.refs_0_.mine), channel_id=1, source_target_pairs={{0,64},{1,65},{2,66},{3,67},{4,68},{5,69},{6,70},{7,71},{8,72},{9,... | collective-permute-start | bytes 1966088 | tf_op jit(solution)/shard_map/ppermute | solution.py:33
  54.9 32.2 %copy-start.7 = (bf16[2560,128]{1,0:T(8,128)(2,1)}, bf16[2560,128]{1,0:T(8,128)(2,1)S(1)}, u32[]{:S(2)}) copy-start(bf16[2560,128]{1,0:T(8,128)(2,1)S(1)} %collective-permute-done.3.refs_1_) | copy-start | bytes 1966084
  54.9 11.5 %collective-permute-start.10 = (bf16[2560,128]{1,0:T(8,128)(2,1)S(1)}, bf16[2560,128]{1,0:T(8,128)(2,1)S(1)}, u32[]{:S(2)}, u32[]{:S(2)}) collective-permute-start(bf16[2560,128]{1,0:T(8,128)(2,1)S(1)} %pad_maximum_fusion.refs_0_.mine), channel_id=1, source_target_pairs={{0,1},{1,0},{2,3},{3,2},{4,5},{5,4},{6,7},{7,6},{8,9},{9,8},{10,11... | collective-permute-start | bytes 1966088 | tf_op jit(solution)/shard_map/ppermute | solution.py:33
  54.9 32.2 %copy-start.4 = (bf16[1312,256]{1,0:T(8,128)(2,1)}, bf16[1312,256]{1,0:T(8,128)(2,1)S(1)}, u32[]{:S(2)}) copy-start(bf16[1312,256]{1,0:T(8,128)(2,1)S(1)} %collective-permute-done.4.refs_9_) | copy-start | bytes 2015236
  55.0 13.8 %collective-permute-start.11 = (bf16[2560,128]{1,0:T(8,128)(2,1)S(1)}, bf16[2560,128]{1,0:T(8,128)(2,1)S(1)}, u32[]{:S(2)}, u32[]{:S(2)}) collective-permute-start(bf16[2560,128]{1,0:T(8,128)(2,1)S(1)} %collective-permute-done.3.refs_1_), channel_id=1, source_target_pairs={{0,1},{1,0},{2,3},{3,2},{4,5},{5,4},{6,7},{7,6},{8,9},{9,8},{10,11... | collective-permute-start | bytes 1966088 | tf_op jit(solution)/shard_map/ppermute | solution.py:33
  55.5 31.7 %copy-start.5 = (bf16[1312,256]{1,0:T(8,128)(2,1)}, bf16[1312,256]{1,0:T(8,128)(2,1)S(1)}, u32[]{:S(2)}) copy-start(bf16[1312,256]{1,0:T(8,128)(2,1)S(1)} %collective-permute-done.5.refs_10_) | copy-start | bytes 2015236
  55.5 31.7 %copy-start.6 = (bf16[1312,256]{1,0:T(8,128)(2,1)}, bf16[1312,256]{1,0:T(8,128)(2,1)S(1)}, u32[]{:S(2)}) copy-start(bf16[1312,256]{1,0:T(8,128)(2,1)S(1)} %collective-permute-done.6.refs_11_) | copy-start | bytes 2015236
  63.0 23.6 %collective-permute-start.12 = (bf16[2560,128]{1,0:T(8,128)(2,1)S(1)}, bf16[2560,128]{1,0:T(8,128)(2,1)}, u32[]{:S(2)}, u32[]{:S(2)}) collective-permute-start(bf16[2560,128]{1,0:T(8,128)(2,1)S(1)} %pad_maximum_fusion.refs_0_.mine), channel_id=1, source_target_pairs={{0,192},{1,193},{2,194},{3,195},{4,196},{5,197},{6,198},{7,199},{8... | collective-permute-start | bytes 1966088 | tf_op jit(solution)/shard_map/ppermute | solution.py:33
  65.8 20.9 %collective-permute-start.14 = (bf16[2560,128]{1,0:T(8,128)(2,1)S(1)}, bf16[2560,128]{1,0:T(8,128)(2,1)}, u32[]{:S(2)}, u32[]{:S(2)}) collective-permute-start(bf16[2560,128]{1,0:T(8,128)(2,1)S(1)} %pad_maximum_fusion.refs_0_.mine), channel_id=1, source_target_pairs={{0,128},{1,129},{2,130},{3,131},{4,132},{5,133},{6,134},{7,135},{8... | collective-permute-start | bytes 1966088 | tf_op jit(solution)/shard_map/ppermute | solution.py:33
  66.1 25.1 %collective-permute-start.7 = (bf16[1312,256]{1,0:T(8,128)(2,1)}, bf16[1312,256]{1,0:T(8,128)(2,1)}, u32[]{:S(2)}, u32[]{:S(2)}) collective-permute-start(bf16[1312,256]{1,0:T(8,128)(2,1)} %collective-permute-done.2.refs_12_), channel_id=1, source_target_pairs={{0,4},{1,5},{2,6},{3,7},{4,8},{5,9},{6,10},{7,11},{8,12},{9,13},{1... | collective-permute-start | bytes 2015240 | tf_op jit(solution)/shard_map/ppermute | solution.py:33
  66.5 36.7 %copy-start.2 = (bf16[2560,128]{1,0:T(8,128)(2,1)}, bf16[2560,128]{1,0:T(8,128)(2,1)S(1)}, u32[]{:S(2)}) copy-start(bf16[2560,128]{1,0:T(8,128)(2,1)S(1)} %collective-permute-done.10.refs_4_.other) | copy-start | bytes 1966084
  66.5 24.8 %collective-permute-start.8 = (bf16[1312,256]{1,0:T(8,128)(2,1)}, bf16[1312,256]{1,0:T(8,128)(2,1)}, u32[]{:S(2)}, u32[]{:S(2)}) collective-permute-start(bf16[1312,256]{1,0:T(8,128)(2,1)} %collective-permute-done.2.refs_12_), channel_id=1, source_target_pairs={{0,12},{1,13},{2,14},{3,15},{4,0},{5,1},{6,2},{7,3},{8,4},{9,5},{1... | collective-permute-start | bytes 2015240 | tf_op jit(solution)/shard_map/ppermute | solution.py:33
  68.8 18.4 %copy-start.8 = (bf16[2560,128]{1,0:T(8,128)(2,1)}, bf16[2560,128]{1,0:T(8,128)(2,1)S(1)}, u32[]{:S(2)}) copy-start(bf16[2560,128]{1,0:T(8,128)(2,1)S(1)} %collective-permute-done.11.refs_5_) | copy-start | bytes 1966084
  68.8 22.4 %collective-permute-start.9 = (bf16[1312,256]{1,0:T(8,128)(2,1)}, bf16[1312,256]{1,0:T(8,128)(2,1)}, u32[]{:S(2)}, u32[]{:S(2)}) collective-permute-start(bf16[1312,256]{1,0:T(8,128)(2,1)} %collective-permute-done.2.refs_12_), channel_id=1, source_target_pairs={{0,8},{1,9},{2,10},{3,11},{4,12},{5,13},{6,14},{7,15},{8,0},{9,1},... | collective-permute-start | bytes 2015240 | tf_op jit(solution)/shard_map/ppermute | solution.py:33
  86.6 4.6 %collective-permute-start.13 = (bf16[2560,128]{1,0:T(8,128)(2,1)}, bf16[2560,128]{1,0:T(8,128)(2,1)}, u32[]{:S(2)}, u32[]{:S(2)}) collective-permute-start(bf16[2560,128]{1,0:T(8,128)(2,1)} %collective-permute-done.12.refs_2_), channel_id=1, source_target_pairs={{0,1},{1,0},{2,3},{3,2},{4,5},{5,4},{6,7},{7,6},{8,9},{9,8},{10,11... | collective-permute-start | bytes 1966088 | tf_op jit(solution)/shard_map/ppermute | solution.py:33
  86.7 4.6 %collective-permute-start.15 = (bf16[2560,128]{1,0:T(8,128)(2,1)}, bf16[2560,128]{1,0:T(8,128)(2,1)}, u32[]{:S(2)}, u32[]{:S(2)}) collective-permute-start(bf16[2560,128]{1,0:T(8,128)(2,1)} %collective-permute-done.14.refs_3_), channel_id=1, source_target_pairs={{0,1},{1,0},{2,3},{3,2},{4,5},{5,4},{6,7},{7,6},{8,9},{9,8},{10,11... | collective-permute-start | bytes 1966088 | tf_op jit(solution)/shard_map/ppermute | solution.py:33
  91.3 24.2 %collective-permute-start.16 = (bf16[640,256]{1,0:T(8,128)(2,1)S(1)}, bf16[640,256]{1,0:T(8,128)(2,1)S(1)}, u32[]{:S(2)}, u32[]{:S(2)}) collective-permute-start(bf16[640,256]{1,0:T(8,128)(2,1)S(1)} %bitcast.20), channel_id=1, source_target_pairs={{0,4},{1,5},{2,6},{3,7},{4,8},{5,9},{6,10},{7,11},{8,12},{9,13},{1... | collective-permute-start | bytes 983048 | tf_op jit(solution)/shard_map/ppermute | solution.py:33
  91.8 23.6 %collective-permute-start.17 = (bf16[640,256]{1,0:T(8,128)(2,1)S(1)}, bf16[640,256]{1,0:T(8,128)(2,1)S(1)}, u32[]{:S(2)}, u32[]{:S(2)}) collective-permute-start(bf16[640,256]{1,0:T(8,128)(2,1)S(1)} %bitcast.21), channel_id=1, source_target_pairs={{0,12},{1,13},{2,14},{3,15},{4,0},{5,1},{6,2},{7,3},{8,4},{9,5},{1... | collective-permute-start | bytes 983048 | tf_op jit(solution)/shard_map/ppermute | solution.py:33
  94.7 20.8 %collective-permute-start.18 = (bf16[640,256]{1,0:T(8,128)(2,1)S(1)}, bf16[640,256]{1,0:T(8,128)(2,1)S(1)}, u32[]{:S(2)}, u32[]{:S(2)}) collective-permute-start(bf16[640,256]{1,0:T(8,128)(2,1)S(1)} %bitcast.22), channel_id=1, source_target_pairs={{0,8},{1,9},{2,10},{3,11},{4,12},{5,13},{6,14},{7,15},{8,0},{9,1},... | collective-permute-start | bytes 983048 | tf_op jit(solution)/shard_map/ppermute | solution.py:33
  95.8 21.3 %collective-permute-start.19 = (bf16[640,256]{1,0:T(8,128)(2,1)S(1)}, bf16[640,256]{1,0:T(8,128)(2,1)S(1)}, u32[]{:S(2)}, u32[]{:S(2)}) collective-permute-start(bf16[640,256]{1,0:T(8,128)(2,1)S(1)} %bitcast.23), channel_id=1, source_target_pairs={{0,2},{1,3},{2,0},{3,1},{4,6},{5,7},{6,4},{7,5},{8,10},{9,11},{10,... | collective-permute-start | bytes 983048 | tf_op jit(solution)/shard_map/ppermute | solution.py:33
  101.8 13.6 %collective-permute-start.20 = (bf16[352,256]{1,0:T(8,128)(2,1)S(1)}, bf16[352,256]{1,0:T(8,128)(2,1)S(1)}, u32[]{:S(2)}, u32[]{:S(2)}) collective-permute-start(bf16[352,256]{1,0:T(8,128)(2,1)S(1)} %copy-done.9), channel_id=1, source_target_pairs={{0,2},{17,19},{34,32},{51,49},{68,70},{85,87},{102,100},{119,117},... | collective-permute-start | bytes 540680 | tf_op jit(solution)/shard_map/ppermute | solution.py:33
  117.1 16.1 %collective-permute-start.26 = (f32[1280,256]{1,0:T(8,128)}, f32[1280,256]{1,0:T(8,128)}, u32[]{:S(2)}, u32[]{:S(2)}) collective-permute-start(f32[1280,256]{1,0:T(8,128)} %apply_panel.1.before), channel_id=1, source_target_pairs={{1,17},{3,19},{5,21},{7,23},{9,25},{11,27},{13,29},{15,31},{16,0},... | collective-permute-start | bytes 3932168 | tf_op jit(solution)/shard_map/ppermute | solution.py:33
  119.4 0.7 collective-permute-start.24
  120.2 3.4 %collective-permute-start.25 = (bf16[352,256]{1,0:T(8,128)(2,1)S(1)}, bf16[352,256]{1,0:T(8,128)(2,1)S(1)}, u32[]{:S(2)}, u32[]{:S(2)}) collective-permute-start(bf16[352,256]{1,0:T(8,128)(2,1)S(1)} %add.101), channel_id=1, source_target_pairs={{0,8},{2,10},{4,12},{6,14},{17,25},{19,27},{21,29},{23,31},{32,40}... | collective-permute-start | bytes 540680 | tf_op jit(solution)/shard_map/ppermute | solution.py:33
  120.9 14.2 %collective-permute-start.21 = (bf16[640,256]{1,0:T(8,128)(2,1)S(1)}, bf16[640,256]{1,0:T(8,128)(2,1)S(1)}, u32[]{:S(2)}, u32[]{:S(2)}) collective-permute-start(bf16[640,256]{1,0:T(8,128)(2,1)S(1)} %collective-permute-done.19.refs_4_), channel_id=1, source_target_pairs={{0,4},{1,5},{2,6},{3,7},{4,8},{5,9},{6,10},{7,11},{8,12},{9,13},{1... | collective-permute-start | bytes 983048 | tf_op jit(solution)/shard_map/ppermute | solution.py:33
  120.9 14.1 %collective-permute-start.22 = (bf16[640,256]{1,0:T(8,128)(2,1)S(1)}, bf16[640,256]{1,0:T(8,128)(2,1)S(1)}, u32[]{:S(2)}, u32[]{:S(2)}) collective-permute-start(bf16[640,256]{1,0:T(8,128)(2,1)S(1)} %collective-permute-done.19.refs_4_), channel_id=1, source_target_pairs={{0,12},{1,13},{2,14},{3,15},{4,0},{5,1},{6,2},{7,3},{8,4},{9,5},{1... | collective-permute-start | bytes 983048 | tf_op jit(solution)/shard_map/ppermute | solution.py:33
  123.6 11.5 %collective-permute-start.23 = (bf16[640,256]{1,0:T(8,128)(2,1)S(1)}, bf16[640,256]{1,0:T(8,128)(2,1)S(1)}, u32[]{:S(2)}, u32[]{:S(2)}) collective-permute-start(bf16[640,256]{1,0:T(8,128)(2,1)S(1)} %collective-permute-done.19.refs_4_), channel_id=1, source_target_pairs={{0,8},{1,9},{2,10},{3,11},{4,12},{5,13},{6,14},{7,15},{8,0},{9,1},... | collective-permute-start | bytes 983048 | tf_op jit(solution)/shard_map/ppermute | solution.py:33
  128.9 13.4 %copy-start = (s32[5]{0:T(128)S(1)}, s32[5]{0:T(128)}, u32[]{:S(2)}) copy-start(s32[5]{0:T(128)} %stack.23.place) | copy-start | bytes 64
  135.1 7.2 %collective-permute-start.27 = (bf16[1280,256]{1,0:T(8,128)(2,1)S(1)}, bf16[1280,256]{1,0:T(8,128)(2,1)S(1)}, u32[]{:S(2)}, u32[]{:S(2)}) collective-permute-start(bf16[1280,256]{1,0:T(8,128)(2,1)S(1)} %add_convert_fusion.refs_8_), channel_id=1, source_target_pairs={{0,1},{1,0},{2,3},{3,2},{4,5},{5,4},{6,7},{7,6},{8,9},{9,8},{10,11... | collective-permute-start | bytes 1966088 | tf_op jit(solution)/shard_map/ppermute | solution.py:33
  145.3 10.8 %collective-permute-start.28 = (f32[256,256]{1,0:T(8,128)}, f32[256,256]{1,0:T(8,128)S(1)}, u32[]{:S(2)}, u32[]{:S(2)}) collective-permute-start(f32[256,256]{1,0:T(8,128)} %get-tuple-element.36), channel_id=1, source_target_pairs={{0,64},{1,65},{2,66},{3,67},{4,68},{5,69},{6,70},{7,71},{8,72},{9,... | collective-permute-start | bytes 786440 | tf_op jit(solution)/shard_map/ppermute | solution.py:33
  146.7 15.9 %collective-permute-start.29 = (f32[256,256]{1,0:T(8,128)S(1)}, f32[256,256]{1,0:T(8,128)S(1)}, u32[]{:S(2)}, u32[]{:S(2)}) collective-permute-start(f32[256,256]{1,0:T(8,128)S(1)} %get-tuple-element.37), channel_id=1, source_target_pairs={{0,128},{1,129},{2,130},{3,131},{4,132},{5,133},{6,134},{7,135},{8... | collective-permute-start | bytes 786440 | tf_op jit(solution)/shard_map/ppermute | solution.py:33
  150.7 11.9 %collective-permute-start.30 = (f32[256,256]{1,0:T(8,128)S(1)}, f32[256,256]{1,0:T(8,128)S(1)}, u32[]{:S(2)}, u32[]{:S(2)}) collective-permute-start(f32[256,256]{1,0:T(8,128)S(1)} %get-tuple-element.38), channel_id=1, source_target_pairs={{0,192},{1,193},{2,194},{3,195},{4,196},{5,197},{6,198},{7,199},{8... | collective-permute-start | bytes 786440 | tf_op jit(solution)/shard_map/ppermute | solution.py:33
  163.1 5.9 %collective-permute-start.31 = (f32[128,128]{1,0:T(8,128)S(1)}, f32[128,128]{1,0:T(8,128)S(1)}, u32[]{:S(2)}, u32[]{:S(2)}) collective-permute-start(f32[128,128]{1,0:T(8,128)S(1)} %bitcast.31), channel_id=1, source_target_pairs={{0,0},{1,16},{2,2},{3,18},{4,4},{5,20},{6,6},{7,22},{8,8},{9,24},{... | collective-permute-start | bytes 196616 | tf_op jit(solution)/shard_map/ppermute | solution.py:33
  166.1 2.9 %collective-permute-start.32 = (f32[128,128]{1,0:T(8,128)S(1)}, f32[128,128]{1,0:T(8,128)S(1)}, u32[]{:S(2)}, u32[]{:S(2)}) collective-permute-start(f32[128,128]{1,0:T(8,128)S(1)} %bitcast.30), channel_id=1, source_target_pairs={{0,1},{1,17},{2,3},{3,19},{4,5},{5,21},{6,7},{7,23},{8,9},{9,25},{... | collective-permute-start | bytes 196616 | tf_op jit(solution)/shard_map/ppermute | solution.py:33
  166.2 5.9 %collective-permute-start.33 = (f32[128,128]{1,0:T(8,128)S(1)}, f32[128,128]{1,0:T(8,128)S(1)}, u32[]{:S(2)}, u32[]{:S(2)}) collective-permute-start(f32[128,128]{1,0:T(8,128)S(1)} %bitcast.29), channel_id=1, source_target_pairs={{0,32},{1,48},{2,34},{3,50},{4,36},{5,52},{6,38},{7,54},{8,40},{9,... | collective-permute-start | bytes 196616 | tf_op jit(solution)/shard_map/ppermute | solution.py:33
  166.3 8.3 %collective-permute-start.34 = (f32[128,128]{1,0:T(8,128)S(1)}, f32[128,128]{1,0:T(8,128)S(1)}, u32[]{:S(2)}, u32[]{:S(2)}) collective-permute-start(f32[128,128]{1,0:T(8,128)S(1)} %bitcast.28), channel_id=1, source_target_pairs={{0,33},{1,49},{2,35},{3,51},{4,37},{5,53},{6,39},{7,55},{8,41},{9,... | collective-permute-start | bytes 196616 | tf_op jit(solution)/shard_map/ppermute | solution.py:33

commit v5 on v4

--- a/solution.py
+++ b/solution.py
@@ -142,7 +142,7 @@
     for copy in copies[:8]:
         copy.wait()
     for slot in range(8):
-        numbers[slot] = ends[slot][:24, :128].astype(jnp.float32).astype(jnp.int32)
+        numbers[slot] = ends[slot][:, :128].astype(jnp.float32)[:24].astype(jnp.int32)
     scalars = pltpu.make_async_copy(numbers, offsets, sems.at[len(copies)])
     scalars.start()
     for copy in copies[8:] + [scalars]:
@@ -203,7 +203,7 @@
         dst = panel.at[lax.rem(c + n, 2)]
         copies.append(pltpu.make_async_copy(src.at[pl.ds(0, 1280)], dst, sems.at[n]))
         copies[n].start()
-    numbers[...] = five[pl.ds(320, 32), :128][:24].astype(jnp.float32).astype(jnp.int32)
+    numbers[...] = five[pl.ds(320, 32), :128].astype(jnp.float32)[:24].astype(jnp.int32)
     scalars = pltpu.make_async_copy(numbers, offsets, sems.at[2])
     scalars.start()
     for copy in copies + [scalars]:

time: 176 us -> 176 us (level)
  no operation moved by 1% of the time
where the time goes in v5:
time: 176 us; the launch traced here: 175 us
  waiting for transfers between devices  72.6 us (41%)
  starting transfers between devices  67.4 us (38%)
  Pallas kernels  23.1 us (13%)
  local copies, waits for them, and re-layouts  6.21 us (4%)
  other arithmetic  5.72 us (3%)
    ppermute x35, waiting for transfers between devices, move(): return lax.ppermute(array, AXES, pairs)  72.6 us
    ppermute x35, starting transfers between devices, move(): return lax.ppermute(array, AXES, pairs)  67.4 us
    pallas_call x1, Pallas kernels, apply_panel(): pl.pallas_call(apply_kernel, out_shape=jax.ShapeDtypeStruct((1280, 256),...  12.2 us
    pallas_call x1, Pallas kernels, apply_last(): pl.pallas_call(last_kernel, out_shape=jax.ShapeDtypeStruct((1280, 256), j...  4.6 us
    reshape x2, local copies, waits for them, and re-layouts, per_device(): a_vals.reshape(20, 5, BR, BR)  4.23 us
  transfers between devices with their start and end apart: 35, of which 13 were waited for; matrix products, arithmetic and copies ran while one was open for 5% of the time, Pallas kernels for 11%

profile of v5, /device:TPU:1, one launch (start us, length us, event | category | flops | bytes accessed | tf_op | source)
XLA Modules:
  0.0 175.3 jit_solution(13092696067097889807)
XLA Ops:
  0.0 0.7 convert_bitcast_fusion
  0.7 1.1 broadcast_multiply_fusion
  1.7 3.9 %collective-permute-start = (bf16[1280,128]{1,0:T(8,128)(2,1)S(1)}, bf16[1280,128]{1,0:T(8,128)(2,1)S(1)}, u32[]{:S(2)}, u32[]{:S(2)}) collective-permute-start(bf16[1280,128]{1,0:T(8,128)(2,1)S(1)} %bitcast.25), channel_id=1, source_target_pairs={{0,32},{1,33},{2,34},{3,35},{4,36},{5,37},{6,38},{7,39},{8,40},{9,... | collective-permute-start | bytes 983048 | tf_op jit(solution)/shard_map/ppermute | solution.py:33
  5.6 0.8 copy.13
  6.4 0.6 broadcast_subtract_fusion.cols
  7.0 2.9 %reshape.44 = bf16[20,5,64,64]{3,2,0,1:T(8,128)(2,1)S(1)} reshape(bf16[20,5,4096]{2,0,1:T(8,128)(2,1)} %param.5) | data formatting | bytes 1638400 | tf_op jit(solution)/shard_map/reshape | solution.py:315
  9.9 1.3 copy.15.blocks
  11.2 3.3 %pack.1 = (bf16[1312,256]{1,0:T(8,128)(2,1)}, bf16[352,256]{1,0:T(8,128)(2,1)}) custom-call(s32[20]{0:T(128)} %bitcast.32, s32[1]{0:T(128)} %bitcast.10.diagonal, bf16[20,5,64,64]{3,2,1,0:T(8,128)(2,1)} %copy.15.blocks, s32[20,5]{1,0:T(8,128)} %broadcast_subtract_fusion.cols), custom_call_target="tpu_custom_call" | custom-call | bytes 3145728 | tf_op jit(solution)/shard_map/pack/pallas_call | solution.py:100
  14.5 4.5 %collective-permute-start.1 = (bf16[1312,256]{1,0:T(8,128)(2,1)}, bf16[1312,256]{1,0:T(8,128)(2,1)S(1)}, u32[]{:S(2)}, u32[]{:S(2)}) collective-permute-start(bf16[1312,256]{1,0:T(8,128)(2,1)} %get-tuple-element.24), channel_id=1, source_target_pairs={{0,0},{1,16},{2,2},{3,18},{4,4},{5,20},{6,6},{7,22},{8,8},{9,24},{... | collective-permute-start | bytes 2015240 | tf_op jit(solution)/shard_map/ppermute | solution.py:33
  19.5 8.7 %collective-permute-done.1.refs_8_ = bf16[1312,256]{1,0:T(8,128)(2,1)S(1)} collective-permute-done((bf16[1312,256]{1,0:T(8,128)(2,1)}, bf16[1312,256]{1,0:T(8,128)(2,1)S(1)}, u32[]{:S(2)}, u32[]{:S(2)}) %collective-permute-start.1) | collective-permute-done | bytes 671776 | tf_op jit(solution)/shard_map/ppermute | solution.py:33
  28.1 1.2 collective-permute-start.4
  29.3 1.5 collective-permute-start.5
  30.8 1.5 collective-permute-start.6
  32.3 11.9 %collective-permute-start.2 = (bf16[1312,256]{1,0:T(8,128)(2,1)S(1)}, bf16[1312,256]{1,0:T(8,128)(2,1)}, u32[]{:S(2)}, u32[]{:S(2)}) collective-permute-start(bf16[1312,256]{1,0:T(8,128)(2,1)S(1)} %copy-done.10), channel_id=1, source_target_pairs={{0,2},{1,18},{2,0},{3,16},{4,6},{5,22},{6,4},{7,20},{8,10},{9,26},... | collective-permute-start | bytes 2015240 | tf_op jit(solution)/shard_map/ppermute | solution.py:33
  44.2 1.3 collective-permute-start.3
  45.5 9.4 %collective-permute-done.3.refs_1_ = bf16[2560,128]{1,0:T(8,128)(2,1)S(1)} collective-permute-done((bf16[2560,128]{1,0:T(8,128)(2,1)S(1)}, bf16[2560,128]{1,0:T(8,128)(2,1)S(1)}, u32[]{:S(2)}, u32[]{:S(2)}) %collective-permute-start.3) | collective-permute-done | bytes 655392 | tf_op jit(solution)/shard_map/ppermute | solution.py:33
  55.5 7.6 %collective-permute-done.2.refs_12_ = bf16[1312,256]{1,0:T(8,128)(2,1)} collective-permute-done((bf16[1312,256]{1,0:T(8,128)(2,1)S(1)}, bf16[1312,256]{1,0:T(8,128)(2,1)}, u32[]{:S(2)}, u32[]{:S(2)}) %collective-permute-start.2) | collective-permute-done | bytes 671776 | tf_op jit(solution)/shard_map/ppermute | solution.py:33
  63.0 2.7 %collective-permute-start.12 = (bf16[2560,128]{1,0:T(8,128)(2,1)S(1)}, bf16[2560,128]{1,0:T(8,128)(2,1)}, u32[]{:S(2)}, u32[]{:S(2)}) collective-permute-start(bf16[2560,128]{1,0:T(8,128)(2,1)S(1)} %pad_maximum_fusion.refs_0_.mine), channel_id=1, source_target_pairs={{0,192},{1,193},{2,194},{3,195},{4,196},{5,197},{6,198},{7,199},{8... | collective-permute-start | bytes 1966088 | tf_op jit(solution)/shard_map/ppermute | solution.py:33
  66.5 2.3 %collective-permute-start.8 = (bf16[1312,256]{1,0:T(8,128)(2,1)}, bf16[1312,256]{1,0:T(8,128)(2,1)}, u32[]{:S(2)}, u32[]{:S(2)}) collective-permute-start(bf16[1312,256]{1,0:T(8,128)(2,1)} %collective-permute-done.2.refs_12_), channel_id=1, source_target_pairs={{0,12},{1,13},{2,14},{3,15},{4,0},{5,1},{6,2},{7,3},{8,4},{9,5},{1... | collective-permute-start | bytes 2015240 | tf_op jit(solution)/shard_map/ppermute | solution.py:33
  69.1 17.6 %collective-permute-done.12.refs_2_ = bf16[2560,128]{1,0:T(8,128)(2,1)} collective-permute-done((bf16[2560,128]{1,0:T(8,128)(2,1)S(1)}, bf16[2560,128]{1,0:T(8,128)(2,1)}, u32[]{:S(2)}, u32[]{:S(2)}) %collective-permute-start.12) | collective-permute-done | bytes 655392 | tf_op jit(solution)/shard_map/ppermute | solution.py:33
  87.4 3.8 %collective-permute-done.7.refs_13_ = bf16[1312,256]{1,0:T(8,128)(2,1)} collective-permute-done((bf16[1312,256]{1,0:T(8,128)(2,1)}, bf16[1312,256]{1,0:T(8,128)(2,1)}, u32[]{:S(2)}, u32[]{:S(2)}) %collective-permute-start.7) | collective-permute-done | bytes 671776 | tf_op jit(solution)/shard_map/ppermute | solution.py:33
  91.8 2.8 %collective-permute-start.17 = (bf16[640,256]{1,0:T(8,128)(2,1)S(1)}, bf16[640,256]{1,0:T(8,128)(2,1)S(1)}, u32[]{:S(2)}, u32[]{:S(2)}) collective-permute-start(bf16[640,256]{1,0:T(8,128)(2,1)S(1)} %bitcast.21), channel_id=1, source_target_pairs={{0,12},{1,13},{2,14},{3,15},{4,0},{5,1},{6,2},{7,3},{8,4},{9,5},{1... | collective-permute-start | bytes 983048 | tf_op jit(solution)/shard_map/ppermute | solution.py:33
  94.7 1.1 collective-permute-start.18
  95.8 6.0 %collective-permute-start.19 = (bf16[640,256]{1,0:T(8,128)(2,1)S(1)}, bf16[640,256]{1,0:T(8,128)(2,1)S(1)}, u32[]{:S(2)}, u32[]{:S(2)}) collective-permute-start(bf16[640,256]{1,0:T(8,128)(2,1)S(1)} %bitcast.23), channel_id=1, source_target_pairs={{0,2},{1,3},{2,0},{3,1},{4,6},{5,7},{6,4},{7,5},{8,10},{9,11},{10,... | collective-permute-start | bytes 983048 | tf_op jit(solution)/shard_map/ppermute | solution.py:33
  101.8 0.7 collective-permute-start.20
  102.6 0.6 stack.23.place
  103.2 12.2 %apply_panel.1.before = f32[1280,256]{1,0:T(8,128)} custom-call(s32[5]{0:T(128)} %stack.23.place, bf16[2560,128]{1,0:T(8,128)(2,1)} %copy-done.1, bf16[2560,128]{1,0:T(8,128)(2,1)} %copy-done.7, bf16[2560,128]{1,0:T(8,128)(2,1)} %collective-permute-done.12.refs_2_, bf16[2560,128]{1,0:T(8,128)(2,1)} %collective-permute-done.14.refs_3_, ...), custom_call_target="tpu_custom_call" | custom-call | flops 1342177280 | bytes 12582912 | tf_op jit(solution)/shard_map/apply_panel/pallas_call | solution.py:174
  115.5 1.6 collective-permute-done.19.refs_4_
  117.1 2.3 %collective-permute-start.26 = (f32[1280,256]{1,0:T(8,128)}, f32[1280,256]{1,0:T(8,128)}, u32[]{:S(2)}, u32[]{:S(2)}) collective-permute-start(f32[1280,256]{1,0:T(8,128)} %apply_panel.1.before), channel_id=1, source_target_pairs={{1,17},{3,19},{5,21},{7,23},{9,25},{11,27},{13,29},{15,31},{16,0},... | collective-permute-start | bytes 3932168 | tf_op jit(solution)/shard_map/ppermute | solution.py:33
  119.4 0.7 collective-permute-start.24
  120.2 0.7 collective-permute-start.25
  120.9 2.7 %collective-permute-start.22 = (bf16[640,256]{1,0:T(8,128)(2,1)S(1)}, bf16[640,256]{1,0:T(8,128)(2,1)S(1)}, u32[]{:S(2)}, u32[]{:S(2)}) collective-permute-start(bf16[640,256]{1,0:T(8,128)(2,1)S(1)} %collective-permute-done.19.refs_4_), channel_id=1, source_target_pairs={{0,12},{1,13},{2,14},{3,15},{4,0},{5,1},{6,2},{7,3},{8,4},{9,5},{1... | collective-permute-start | bytes 983048 | tf_op jit(solution)/shard_map/ppermute | solution.py:33
  123.6 0.7 add.102.five
  124.3 4.6 %apply_last.1 = f32[1280,256]{1,0:T(8,128)} custom-call(s32[5]{0:T(128)} %stack.23.place, bf16[2560,128]{1,0:T(8,128)(2,1)} %copy-done.1, bf16[2560,128]{1,0:T(8,128)(2,1)} %copy-done.2, bf16[352,256]{1,0:T(8,128)(2,1)} %add.102.five, f32[1280,256]{1,0:T(8,128)} %apply_panel.1.before), custom_call_target="tpu_custom_call" | custom-call | flops 167772160 | bytes 2097152 | tf_op jit(solution)/shard_map/apply_last/pallas_call | solution.py:226
  128.9 4.3 %collective-permute-done.26 = f32[1280,256]{1,0:T(8,128)} collective-permute-done((f32[1280,256]{1,0:T(8,128)}, f32[1280,256]{1,0:T(8,128)}, u32[]{:S(2)}, u32[]{:S(2)}) %collective-permute-start.26) | collective-permute-done | bytes 1310752 | tf_op jit(solution)/shard_map/ppermute | solution.py:33
  133.2 1.8 %add_convert_fusion.refs_8_ = bf16[1280,256]{1,0:T(8,128)(2,1)S(1)} fusion(f32[1280,256]{1,0:T(8,128)} %apply_last.1, f32[1280,256]{1,0:T(8,128)} %collective-permute-done.26), kind=kLoop, calls=%fused_computation | loop fusion | flops 655360 | bytes 3276800 | tf_op jit(solution)/shard_map/convert_element_type | solution.py:348
  135.1 5.5 %collective-permute-start.27 = (bf16[1280,256]{1,0:T(8,128)(2,1)S(1)}, bf16[1280,256]{1,0:T(8,128)(2,1)S(1)}, u32[]{:S(2)}, u32[]{:S(2)}) collective-permute-start(bf16[1280,256]{1,0:T(8,128)(2,1)S(1)} %add_convert_fusion.refs_8_), channel_id=1, source_target_pairs={{0,1},{1,0},{2,3},{3,2},{4,5},{5,4},{6,7},{7,6},{8,9},{9,8},{10,11... | collective-permute-start | bytes 1966088 | tf_op jit(solution)/shard_map/ppermute | solution.py:33
  140.6 1.7 collective-permute-done.27.refs_9_
  142.3 2.9 %project.1 = (f32[256,256]{1,0:T(8,128)S(1)}, f32[256,256]{1,0:T(8,128)}, f32[256,256]{1,0:T(8,128)S(1)}, f32[256,256]{1,0:T(8,128)S(1)}) custom-call(s32[5]{0:T(128)S(1)} %copy-done, bf16[640,256]{1,0:T(8,128)(2,1)S(1)} %bitcast.24, bf16[640,256]{1,0:T(8,128)(2,1)S(1)} %collective-permute-done.16.refs_1_, ...), custom_call_target="tpu_custom_call" | custom-call | flops 671088640 | bytes 4194304 | tf_op jit(solution)/shard_map/project/pallas_call | solution.py:281
  145.3 1.4 collective-permute-start.28
  146.7 4.0 %collective-permute-start.29 = (f32[256,256]{1,0:T(8,128)S(1)}, f32[256,256]{1,0:T(8,128)S(1)}, u32[]{:S(2)}, u32[]{:S(2)}) collective-permute-start(f32[256,256]{1,0:T(8,128)S(1)} %get-tuple-element.37), channel_id=1, source_target_pairs={{0,128},{1,129},{2,130},{3,131},{4,132},{5,133},{6,134},{7,135},{8... | collective-permute-start | bytes 786440 | tf_op jit(solution)/shard_map/ppermute | solution.py:33
  150.7 5.4 %collective-permute-done.28 = f32[256,256]{1,0:T(8,128)S(1)} collective-permute-done((f32[256,256]{1,0:T(8,128)}, f32[256,256]{1,0:T(8,128)S(1)}, u32[]{:S(2)}, u32[]{:S(2)}) %collective-permute-start.28) | collective-permute-done | bytes 262176 | tf_op jit(solution)/shard_map/ppermute | solution.py:33
  156.1 6.5 %collective-permute-done.29 = f32[256,256]{1,0:T(8,128)S(1)} collective-permute-done((f32[256,256]{1,0:T(8,128)S(1)}, f32[256,256]{1,0:T(8,128)S(1)}, u32[]{:S(2)}, u32[]{:S(2)}) %collective-permute-start.29) | collective-permute-done | bytes 262176 | tf_op jit(solution)/shard_map/ppermute | solution.py:33
  163.1 3.1 %collective-permute-start.31 = (f32[128,128]{1,0:T(8,128)S(1)}, f32[128,128]{1,0:T(8,128)S(1)}, u32[]{:S(2)}, u32[]{:S(2)}) collective-permute-start(f32[128,128]{1,0:T(8,128)S(1)} %bitcast.31), channel_id=1, source_target_pairs={{0,0},{1,16},{2,2},{3,18},{4,4},{5,20},{6,6},{7,22},{8,8},{9,24},{... | collective-permute-start | bytes 196616 | tf_op jit(solution)/shard_map/ppermute | solution.py:33
  166.3 2.7 %collective-permute-start.34 = (f32[128,128]{1,0:T(8,128)S(1)}, f32[128,128]{1,0:T(8,128)S(1)}, u32[]{:S(2)}, u32[]{:S(2)}) collective-permute-start(f32[128,128]{1,0:T(8,128)S(1)} %bitcast.28), channel_id=1, source_target_pairs={{0,33},{1,49},{2,35},{3,51},{4,37},{5,53},{6,39},{7,55},{8,41},{9,... | collective-permute-start | bytes 196616 | tf_op jit(solution)/shard_map/ppermute | solution.py:33
  169.0 3.1 %collective-permute-done.33 = f32[128,128]{1,0:T(8,128)S(1)} collective-permute-done((f32[128,128]{1,0:T(8,128)S(1)}, f32[128,128]{1,0:T(8,128)S(1)}, u32[]{:S(2)}, u32[]{:S(2)}) %collective-permute-start.33) | collective-permute-done | bytes 65568 | tf_op jit(solution)/shard_map/ppermute | solution.py:33
  172.2 2.5 %collective-permute-done.34 = f32[128,128]{1,0:T(8,128)S(1)} collective-permute-done((f32[128,128]{1,0:T(8,128)S(1)}, f32[128,128]{1,0:T(8,128)S(1)}, u32[]{:S(2)}, u32[]{:S(2)}) %collective-permute-start.34) | collective-permute-done | bytes 65568 | tf_op jit(solution)/shard_map/ppermute | solution.py:33
  174.7 0.6 add_add_fusion.1
  (65 shorter events, 4.1 us)
Async XLA Ops:
  1.7 17.7 %collective-permute-start = (bf16[1280,128]{1,0:T(8,128)(2,1)S(1)}, bf16[1280,128]{1,0:T(8,128)(2,1)S(1)}, u32[]{:S(2)}, u32[]{:S(2)}) collective-permute-start(bf16[1280,128]{1,0:T(8,128)(2,1)S(1)} %bitcast.25), channel_id=1, source_target_pairs={{0,32},{1,33},{2,34},{3,35},{4,36},{5,37},{6,38},{7,39},{8,40},{9,... | collective-permute-start | bytes 983048 | tf_op jit(solution)/shard_map/ppermute | solution.py:33
  14.5 17.8 %copy-start.10 = (bf16[1312,256]{1,0:T(8,128)(2,1)S(1)}, bf16[1312,256]{1,0:T(8,128)(2,1)}, u32[]{:S(2)}) copy-start(bf16[1312,256]{1,0:T(8,128)(2,1)} %get-tuple-element.24) | copy-start | bytes 2015236
  14.5 87.3 %copy-start.9 = (bf16[352,256]{1,0:T(8,128)(2,1)S(1)}, bf16[352,256]{1,0:T(8,128)(2,1)}, u32[]{:S(2)}) copy-start(bf16[352,256]{1,0:T(8,128)(2,1)} %get-tuple-element.30) | copy-start | bytes 540676
  14.5 13.6 %collective-permute-start.1 = (bf16[1312,256]{1,0:T(8,128)(2,1)}, bf16[1312,256]{1,0:T(8,128)(2,1)S(1)}, u32[]{:S(2)}, u32[]{:S(2)}) collective-permute-start(bf16[1312,256]{1,0:T(8,128)(2,1)} %get-tuple-element.24), channel_id=1, source_target_pairs={{0,0},{1,16},{2,2},{3,18},{4,4},{5,20},{6,6},{7,22},{8,8},{9,24},{... | collective-permute-start | bytes 2015240 | tf_op jit(solution)/shard_map/ppermute | solution.py:33
  19.5 83.7 %copy-start.1 = (bf16[2560,128]{1,0:T(8,128)(2,1)}, bf16[2560,128]{1,0:T(8,128)(2,1)S(1)}, u32[]{:S(2)}) copy-start(bf16[2560,128]{1,0:T(8,128)(2,1)S(1)} %pad_maximum_fusion.refs_0_.mine) | copy-start | bytes 1966084
  28.1 59.0 %copy-start.3 = (bf16[1312,256]{1,0:T(8,128)(2,1)}, bf16[1312,256]{1,0:T(8,128)(2,1)S(1)}, u32[]{:S(2)}) copy-start(bf16[1312,256]{1,0:T(8,128)(2,1)S(1)} %collective-permute-done.1.refs_8_) | copy-start | bytes 2015236
  28.1 26.8 %collective-permute-start.4 = (bf16[1312,256]{1,0:T(8,128)(2,1)S(1)}, bf16[1312,256]{1,0:T(8,128)(2,1)S(1)}, u32[]{:S(2)}, u32[]{:S(2)}) collective-permute-start(bf16[1312,256]{1,0:T(8,128)(2,1)S(1)} %collective-permute-done.1.refs_8_), channel_id=1, source_target_pairs={{0,4},{1,5},{2,6},{3,7},{4,8},{5,9},{6,10},{7,11},{8,12},{9,13},{1... | collective-permute-start | bytes 2015240 | tf_op jit(solution)/shard_map/ppermute | solution.py:33
  29.3 26.1 %collective-permute-start.5 = (bf16[1312,256]{1,0:T(8,128)(2,1)S(1)}, bf16[1312,256]{1,0:T(8,128)(2,1)S(1)}, u32[]{:S(2)}, u32[]{:S(2)}) collective-permute-start(bf16[1312,256]{1,0:T(8,128)(2,1)S(1)} %collective-permute-done.1.refs_8_), channel_id=1, source_target_pairs={{0,12},{1,13},{2,14},{3,15},{4,0},{5,1},{6,2},{7,3},{8,4},{9,5},{1... | collective-permute-start | bytes 2015240 | tf_op jit(solution)/shard_map/ppermute | solution.py:33
  30.8 24.7 %collective-permute-start.6 = (bf16[1312,256]{1,0:T(8,128)(2,1)S(1)}, bf16[1312,256]{1,0:T(8,128)(2,1)S(1)}, u32[]{:S(2)}, u32[]{:S(2)}) collective-permute-start(bf16[1312,256]{1,0:T(8,128)(2,1)S(1)} %collective-permute-done.1.refs_8_), channel_id=1, source_target_pairs={{0,8},{1,9},{2,10},{3,11},{4,12},{5,13},{6,14},{7,15},{8,0},{9,1},... | collective-permute-start | bytes 2015240 | tf_op jit(solution)/shard_map/ppermute | solution.py:33
  32.3 30.7 %collective-permute-start.2 = (bf16[1312,256]{1,0:T(8,128)(2,1)S(1)}, bf16[1312,256]{1,0:T(8,128)(2,1)}, u32[]{:S(2)}, u32[]{:S(2)}) collective-permute-start(bf16[1312,256]{1,0:T(8,128)(2,1)S(1)} %copy-done.10), channel_id=1, source_target_pairs={{0,2},{1,18},{2,0},{3,16},{4,6},{5,22},{6,4},{7,20},{8,10},{9,26},... | collective-permute-start | bytes 2015240 | tf_op jit(solution)/shard_map/ppermute | solution.py:33
  44.2 10.7 %collective-permute-start.3 = (bf16[2560,128]{1,0:T(8,128)(2,1)S(1)}, bf16[2560,128]{1,0:T(8,128)(2,1)S(1)}, u32[]{:S(2)}, u32[]{:S(2)}) collective-permute-start(bf16[2560,128]{1,0:T(8,128)(2,1)S(1)} %pad_maximum_fusion.refs_0_.mine), channel_id=1, source_target_pairs={{0,64},{1,65},{2,66},{3,67},{4,68},{5,69},{6,70},{7,71},{8,72},{9,... | collective-permute-start | bytes 1966088 | tf_op jit(solution)/shard_map/ppermute | solution.py:33
  54.9 32.2 %copy-start.7 = (bf16[2560,128]{1,0:T(8,128)(2,1)}, bf16[2560,128]{1,0:T(8,128)(2,1)S(1)}, u32[]{:S(2)}) copy-start(bf16[2560,128]{1,0:T(8,128)(2,1)S(1)} %collective-permute-done.3.refs_1_) | copy-start | bytes 1966084
  54.9 11.5 %collective-permute-start.10 = (bf16[2560,128]{1,0:T(8,128)(2,1)S(1)}, bf16[2560,128]{1,0:T(8,128)(2,1)S(1)}, u32[]{:S(2)}, u32[]{:S(2)}) collective-permute-start(bf16[2560,128]{1,0:T(8,128)(2,1)S(1)} %pad_maximum_fusion.refs_0_.mine), channel_id=1, source_target_pairs={{0,1},{1,0},{2,3},{3,2},{4,5},{5,4},{6,7},{7,6},{8,9},{9,8},{10,11... | collective-permute-start | bytes 1966088 | tf_op jit(solution)/shard_map/ppermute | solution.py:33
  54.9 32.2 %copy-start.4 = (bf16[1312,256]{1,0:T(8,128)(2,1)}, bf16[1312,256]{1,0:T(8,128)(2,1)S(1)}, u32[]{:S(2)}) copy-start(bf16[1312,256]{1,0:T(8,128)(2,1)S(1)} %collective-permute-done.4.refs_9_) | copy-start | bytes 2015236
  55.0 13.8 %collective-permute-start.11 = (bf16[2560,128]{1,0:T(8,128)(2,1)S(1)}, bf16[2560,128]{1,0:T(8,128)(2,1)S(1)}, u32[]{:S(2)}, u32[]{:S(2)}) collective-permute-start(bf16[2560,128]{1,0:T(8,128)(2,1)S(1)} %collective-permute-done.3.refs_1_), channel_id=1, source_target_pairs={{0,1},{1,0},{2,3},{3,2},{4,5},{5,4},{6,7},{7,6},{8,9},{9,8},{10,11... | collective-permute-start | bytes 1966088 | tf_op jit(solution)/shard_map/ppermute | solution.py:33
  55.5 31.7 %copy-start.5 = (bf16[1312,256]{1,0:T(8,128)(2,1)}, bf16[1312,256]{1,0:T(8,128)(2,1)S(1)}, u32[]{:S(2)}) copy-start(bf16[1312,256]{1,0:T(8,128)(2,1)S(1)} %collective-permute-done.5.refs_10_) | copy-start | bytes 2015236
  55.5 31.7 %copy-start.6 = (bf16[1312,256]{1,0:T(8,128)(2,1)}, bf16[1312,256]{1,0:T(8,128)(2,1)S(1)}, u32[]{:S(2)}) copy-start(bf16[1312,256]{1,0:T(8,128)(2,1)S(1)} %collective-permute-done.6.refs_11_) | copy-start | bytes 2015236
  63.0 23.6 %collective-permute-start.12 = (bf16[2560,128]{1,0:T(8,128)(2,1)S(1)}, bf16[2560,128]{1,0:T(8,128)(2,1)}, u32[]{:S(2)}, u32[]{:S(2)}) collective-permute-start(bf16[2560,128]{1,0:T(8,128)(2,1)S(1)} %pad_maximum_fusion.refs_0_.mine), channel_id=1, source_target_pairs={{0,192},{1,193},{2,194},{3,195},{4,196},{5,197},{6,198},{7,199},{8... | collective-permute-start | bytes 1966088 | tf_op jit(solution)/shard_map/ppermute | solution.py:33
  65.8 20.9 %collective-permute-start.14 = (bf16[2560,128]{1,0:T(8,128)(2,1)S(1)}, bf16[2560,128]{1,0:T(8,128)(2,1)}, u32[]{:S(2)}, u32[]{:S(2)}) collective-permute-start(bf16[2560,128]{1,0:T(8,128)(2,1)S(1)} %pad_maximum_fusion.refs_0_.mine), channel_id=1, source_target_pairs={{0,128},{1,129},{2,130},{3,131},{4,132},{5,133},{6,134},{7,135},{8... | collective-permute-start | bytes 1966088 | tf_op jit(solution)/shard_map/ppermute | solution.py:33
  66.1 25.1 %collective-permute-start.7 = (bf16[1312,256]{1,0:T(8,128)(2,1)}, bf16[1312,256]{1,0:T(8,128)(2,1)}, u32[]{:S(2)}, u32[]{:S(2)}) collective-permute-start(bf16[1312,256]{1,0:T(8,128)(2,1)} %collective-permute-done.2.refs_12_), channel_id=1, source_target_pairs={{0,4},{1,5},{2,6},{3,7},{4,8},{5,9},{6,10},{7,11},{8,12},{9,13},{1... | collective-permute-start | bytes 2015240 | tf_op jit(solution)/shard_map/ppermute | solution.py:33
  66.5 36.7 %copy-start.2 = (bf16[2560,128]{1,0:T(8,128)(2,1)}, bf16[2560,128]{1,0:T(8,128)(2,1)S(1)}, u32[]{:S(2)}) copy-start(bf16[2560,128]{1,0:T(8,128)(2,1)S(1)} %collective-permute-done.10.refs_4_.other) | copy-start | bytes 1966084
  66.5 24.8 %collective-permute-start.8 = (bf16[1312,256]{1,0:T(8,128)(2,1)}, bf16[1312,256]{1,0:T(8,128)(2,1)}, u32[]{:S(2)}, u32[]{:S(2)}) collective-permute-start(bf16[1312,256]{1,0:T(8,128)(2,1)} %collective-permute-done.2.refs_12_), channel_id=1, source_target_pairs={{0,12},{1,13},{2,14},{3,15},{4,0},{5,1},{6,2},{7,3},{8,4},{9,5},{1... | collective-permute-start | bytes 2015240 | tf_op jit(solution)/shard_map/ppermute | solution.py:33
  68.8 18.4 %copy-start.8 = (bf16[2560,128]{1,0:T(8,128)(2,1)}, bf16[2560,128]{1,0:T(8,128)(2,1)S(1)}, u32[]{:S(2)}) copy-start(bf16[2560,128]{1,0:T(8,128)(2,1)S(1)} %collective-permute-done.11.refs_5_) | copy-start | bytes 1966084
  68.8 22.4 %collective-permute-start.9 = (bf16[1312,256]{1,0:T(8,128)(2,1)}, bf16[1312,256]{1,0:T(8,128)(2,1)}, u32[]{:S(2)}, u32[]{:S(2)}) collective-permute-start(bf16[1312,256]{1,0:T(8,128)(2,1)} %collective-permute-done.2.refs_12_), channel_id=1, source_target_pairs={{0,8},{1,9},{2,10},{3,11},{4,12},{5,13},{6,14},{7,15},{8,0},{9,1},... | collective-permute-start | bytes 2015240 | tf_op jit(solution)/shard_map/ppermute | solution.py:33
  86.6 4.6 %collective-permute-start.13 = (bf16[2560,128]{1,0:T(8,128)(2,1)}, bf16[2560,128]{1,0:T(8,128)(2,1)}, u32[]{:S(2)}, u32[]{:S(2)}) collective-permute-start(bf16[2560,128]{1,0:T(8,128)(2,1)} %collective-permute-done.12.refs_2_), channel_id=1, source_target_pairs={{0,1},{1,0},{2,3},{3,2},{4,5},{5,4},{6,7},{7,6},{8,9},{9,8},{10,11... | collective-permute-start | bytes 1966088 | tf_op jit(solution)/shard_map/ppermute | solution.py:33
  86.7 4.6 %collective-permute-start.15 = (bf16[2560,128]{1,0:T(8,128)(2,1)}, bf16[2560,128]{1,0:T(8,128)(2,1)}, u32[]{:S(2)}, u32[]{:S(2)}) collective-permute-start(bf16[2560,128]{1,0:T(8,128)(2,1)} %collective-permute-done.14.refs_3_), channel_id=1, source_target_pairs={{0,1},{1,0},{2,3},{3,2},{4,5},{5,4},{6,7},{7,6},{8,9},{9,8},{10,11... | collective-permute-start | bytes 1966088 | tf_op jit(solution)/shard_map/ppermute | solution.py:33
  91.3 24.2 %collective-permute-start.16 = (bf16[640,256]{1,0:T(8,128)(2,1)S(1)}, bf16[640,256]{1,0:T(8,128)(2,1)S(1)}, u32[]{:S(2)}, u32[]{:S(2)}) collective-permute-start(bf16[640,256]{1,0:T(8,128)(2,1)S(1)} %bitcast.20), channel_id=1, source_target_pairs={{0,4},{1,5},{2,6},{3,7},{4,8},{5,9},{6,10},{7,11},{8,12},{9,13},{1... | collective-permute-start | bytes 983048 | tf_op jit(solution)/shard_map/ppermute | solution.py:33
  91.8 23.6 %collective-permute-start.17 = (bf16[640,256]{1,0:T(8,128)(2,1)S(1)}, bf16[640,256]{1,0:T(8,128)(2,1)S(1)}, u32[]{:S(2)}, u32[]{:S(2)}) collective-permute-start(bf16[640,256]{1,0:T(8,128)(2,1)S(1)} %bitcast.21), channel_id=1, source_target_pairs={{0,12},{1,13},{2,14},{3,15},{4,0},{5,1},{6,2},{7,3},{8,4},{9,5},{1... | collective-permute-start | bytes 983048 | tf_op jit(solution)/shard_map/ppermute | solution.py:33
  94.7 20.8 %collective-permute-start.18 = (bf16[640,256]{1,0:T(8,128)(2,1)S(1)}, bf16[640,256]{1,0:T(8,128)(2,1)S(1)}, u32[]{:S(2)}, u32[]{:S(2)}) collective-permute-start(bf16[640,256]{1,0:T(8,128)(2,1)S(1)} %bitcast.22), channel_id=1, source_target_pairs={{0,8},{1,9},{2,10},{3,11},{4,12},{5,13},{6,14},{7,15},{8,0},{9,1},... | collective-permute-start | bytes 983048 | tf_op jit(solution)/shard_map/ppermute | solution.py:33
  95.8 21.3 %collective-permute-start.19 = (bf16[640,256]{1,0:T(8,128)(2,1)S(1)}, bf16[640,256]{1,0:T(8,128)(2,1)S(1)}, u32[]{:S(2)}, u32[]{:S(2)}) collective-permute-start(bf16[640,256]{1,0:T(8,128)(2,1)S(1)} %bitcast.23), channel_id=1, source_target_pairs={{0,2},{1,3},{2,0},{3,1},{4,6},{5,7},{6,4},{7,5},{8,10},{9,11},{10,... | collective-permute-start | bytes 983048 | tf_op jit(solution)/shard_map/ppermute | solution.py:33
  101.8 13.6 %collective-permute-start.20 = (bf16[352,256]{1,0:T(8,128)(2,1)S(1)}, bf16[352,256]{1,0:T(8,128)(2,1)S(1)}, u32[]{:S(2)}, u32[]{:S(2)}) collective-permute-start(bf16[352,256]{1,0:T(8,128)(2,1)S(1)} %copy-done.9), channel_id=1, source_target_pairs={{0,2},{17,19},{34,32},{51,49},{68,70},{85,87},{102,100},{119,117},... | collective-permute-start | bytes 540680 | tf_op jit(solution)/shard_map/ppermute | solution.py:33
  117.1 16.1 %collective-permute-start.26 = (f32[1280,256]{1,0:T(8,128)}, f32[1280,256]{1,0:T(8,128)}, u32[]{:S(2)}, u32[]{:S(2)}) collective-permute-start(f32[1280,256]{1,0:T(8,128)} %apply_panel.1.before), channel_id=1, source_target_pairs={{1,17},{3,19},{5,21},{7,23},{9,25},{11,27},{13,29},{15,31},{16,0},... | collective-permute-start | bytes 3932168 | tf_op jit(solution)/shard_map/ppermute | solution.py:33
  119.4 0.7 collective-permute-start.24
  120.2 3.4 %collective-permute-start.25 = (bf16[352,256]{1,0:T(8,128)(2,1)S(1)}, bf16[352,256]{1,0:T(8,128)(2,1)S(1)}, u32[]{:S(2)}, u32[]{:S(2)}) collective-permute-start(bf16[352,256]{1,0:T(8,128)(2,1)S(1)} %add.101), channel_id=1, source_target_pairs={{0,8},{2,10},{4,12},{6,14},{17,25},{19,27},{21,29},{23,31},{32,40}... | collective-permute-start | bytes 540680 | tf_op jit(solution)/shard_map/ppermute | solution.py:33
  120.9 14.2 %collective-permute-start.21 = (bf16[640,256]{1,0:T(8,128)(2,1)S(1)}, bf16[640,256]{1,0:T(8,128)(2,1)S(1)}, u32[]{:S(2)}, u32[]{:S(2)}) collective-permute-start(bf16[640,256]{1,0:T(8,128)(2,1)S(1)} %collective-permute-done.19.refs_4_), channel_id=1, source_target_pairs={{0,4},{1,5},{2,6},{3,7},{4,8},{5,9},{6,10},{7,11},{8,12},{9,13},{1... | collective-permute-start | bytes 983048 | tf_op jit(solution)/shard_map/ppermute | solution.py:33
  120.9 14.1 %collective-permute-start.22 = (bf16[640,256]{1,0:T(8,128)(2,1)S(1)}, bf16[640,256]{1,0:T(8,128)(2,1)S(1)}, u32[]{:S(2)}, u32[]{:S(2)}) collective-permute-start(bf16[640,256]{1,0:T(8,128)(2,1)S(1)} %collective-permute-done.19.refs_4_), channel_id=1, source_target_pairs={{0,12},{1,13},{2,14},{3,15},{4,0},{5,1},{6,2},{7,3},{8,4},{9,5},{1... | collective-permute-start | bytes 983048 | tf_op jit(solution)/shard_map/ppermute | solution.py:33
  123.6 11.5 %collective-permute-start.23 = (bf16[640,256]{1,0:T(8,128)(2,1)S(1)}, bf16[640,256]{1,0:T(8,128)(2,1)S(1)}, u32[]{:S(2)}, u32[]{:S(2)}) collective-permute-start(bf16[640,256]{1,0:T(8,128)(2,1)S(1)} %collective-permute-done.19.refs_4_), channel_id=1, source_target_pairs={{0,8},{1,9},{2,10},{3,11},{4,12},{5,13},{6,14},{7,15},{8,0},{9,1},... | collective-permute-start | bytes 983048 | tf_op jit(solution)/shard_map/ppermute | solution.py:33
  128.9 13.4 %copy-start = (s32[5]{0:T(128)S(1)}, s32[5]{0:T(128)}, u32[]{:S(2)}) copy-start(s32[5]{0:T(128)} %stack.23.place) | copy-start | bytes 64
  135.1 7.2 %collective-permute-start.27 = (bf16[1280,256]{1,0:T(8,128)(2,1)S(1)}, bf16[1280,256]{1,0:T(8,128)(2,1)S(1)}, u32[]{:S(2)}, u32[]{:S(2)}) collective-permute-start(bf16[1280,256]{1,0:T(8,128)(2,1)S(1)} %add_convert_fusion.refs_8_), channel_id=1, source_target_pairs={{0,1},{1,0},{2,3},{3,2},{4,5},{5,4},{6,7},{7,6},{8,9},{9,8},{10,11... | collective-permute-start | bytes 1966088 | tf_op jit(solution)/shard_map/ppermute | solution.py:33
  145.3 10.8 %collective-permute-start.28 = (f32[256,256]{1,0:T(8,128)}, f32[256,256]{1,0:T(8,128)S(1)}, u32[]{:S(2)}, u32[]{:S(2)}) collective-permute-start(f32[256,256]{1,0:T(8,128)} %get-tuple-element.36), channel_id=1, source_target_pairs={{0,64},{1,65},{2,66},{3,67},{4,68},{5,69},{6,70},{7,71},{8,72},{9,... | collective-permute-start | bytes 786440 | tf_op jit(solution)/shard_map/ppermute | solution.py:33
  146.7 15.9 %collective-permute-start.29 = (f32[256,256]{1,0:T(8,128)S(1)}, f32[256,256]{1,0:T(8,128)S(1)}, u32[]{:S(2)}, u32[]{:S(2)}) collective-permute-start(f32[256,256]{1,0:T(8,128)S(1)} %get-tuple-element.37), channel_id=1, source_target_pairs={{0,128},{1,129},{2,130},{3,131},{4,132},{5,133},{6,134},{7,135},{8... | collective-permute-start | bytes 786440 | tf_op jit(solution)/shard_map/ppermute | solution.py:33
  150.7 11.9 %collective-permute-start.30 = (f32[256,256]{1,0:T(8,128)S(1)}, f32[256,256]{1,0:T(8,128)S(1)}, u32[]{:S(2)}, u32[]{:S(2)}) collective-permute-start(f32[256,256]{1,0:T(8,128)S(1)} %get-tuple-element.38), channel_id=1, source_target_pairs={{0,192},{1,193},{2,194},{3,195},{4,196},{5,197},{6,198},{7,199},{8... | collective-permute-start | bytes 786440 | tf_op jit(solution)/shard_map/ppermute | solution.py:33
  163.1 5.9 %collective-permute-start.31 = (f32[128,128]{1,0:T(8,128)S(1)}, f32[128,128]{1,0:T(8,128)S(1)}, u32[]{:S(2)}, u32[]{:S(2)}) collective-permute-start(f32[128,128]{1,0:T(8,128)S(1)} %bitcast.31), channel_id=1, source_target_pairs={{0,0},{1,16},{2,2},{3,18},{4,4},{5,20},{6,6},{7,22},{8,8},{9,24},{... | collective-permute-start | bytes 196616 | tf_op jit(solution)/shard_map/ppermute | solution.py:33
  166.1 2.9 %collective-permute-start.32 = (f32[128,128]{1,0:T(8,128)S(1)}, f32[128,128]{1,0:T(8,128)S(1)}, u32[]{:S(2)}, u32[]{:S(2)}) collective-permute-start(f32[128,128]{1,0:T(8,128)S(1)} %bitcast.30), channel_id=1, source_target_pairs={{0,1},{1,17},{2,3},{3,19},{4,5},{5,21},{6,7},{7,23},{8,9},{9,25},{... | collective-permute-start | bytes 196616 | tf_op jit(solution)/shard_map/ppermute | solution.py:33
  166.2 5.9 %collective-permute-start.33 = (f32[128,128]{1,0:T(8,128)S(1)}, f32[128,128]{1,0:T(8,128)S(1)}, u32[]{:S(2)}, u32[]{:S(2)}) collective-permute-start(f32[128,128]{1,0:T(8,128)S(1)} %bitcast.29), channel_id=1, source_target_pairs={{0,32},{1,48},{2,34},{3,50},{4,36},{5,52},{6,38},{7,54},{8,40},{9,... | collective-permute-start | bytes 196616 | tf_op jit(solution)/shard_map/ppermute | solution.py:33
  166.3 8.3 %collective-permute-start.34 = (f32[128,128]{1,0:T(8,128)S(1)}, f32[128,128]{1,0:T(8,128)S(1)}, u32[]{:S(2)}, u32[]{:S(2)}) collective-permute-start(f32[128,128]{1,0:T(8,128)S(1)} %bitcast.28), channel_id=1, source_target_pairs={{0,33},{1,49},{2,35},{3,51},{4,37},{5,53},{6,39},{7,55},{8,41},{9,... | collective-permute-start | bytes 196616 | tf_op jit(solution)/shard_map/ppermute | solution.py:33
